TPU v7x, 32 devices: a whole 2x2x4 slice. The times are simulated.
32 devices in a mesh: dp: 8 (over y, x, core), mp: 4 (over z).
Axes of the slice: x: 2, y: 2, z: 4, core: 2. Of those that a mesh axis runs over, the one named last changes fastest.
Arguments:
- frames: bfloat16 [16384, 768], P(('dp', 'mp')), may hold values from -6 to 6
- lengths: int32 [16], P('dp'), may hold values from 640 to 1024, as said below
- span_starts: int32 [16, 66], P('dp'), may hold values from 0 to 1014, as said below
- cotangent: bfloat16 [16384, 768], P(('dp', 'mp')), may hold values from -6 to 6
- query_weight: bfloat16 [768, 768], P('dp', 'mp'), may hold values from -0.3125 to 0.3125
- key_weight: bfloat16 [768, 768], P('dp', 'mp'), may hold values from -0.3125 to 0.3125
- value_weight: bfloat16 [768, 768], P('dp', 'mp'), may hold values from -0.21875 to 0.21875
- out_weight: bfloat16 [768, 768], P('mp', 'dp'), may hold values from -0.875 to 0.875
- up_weight: bfloat16 [768, 3072], P('dp', 'mp'), may hold values from -0.21875 to 0.21875
- down_weight: bfloat16 [3072, 768], P('mp', 'dp'), may hold values from -0.15625 to 0.15625
- query_bias: bfloat16 [12, 64], P('mp'), may hold values from -3 to 3
- value_bias: bfloat16 [12, 64], P('mp'), may hold values from -3 to 3
- up_bias: bfloat16 [24, 128], P('mp'), may hold values from -3 to 3
- out_bias: bfloat16 [768], replicated, may hold values from -3 to 3
- down_bias: bfloat16 [768], replicated, may hold values from -3 to 3
- first_gain: bfloat16 [768], replicated, may hold values from 0.25 to 1.75
- first_shift: bfloat16 [768], replicated, may hold values from -2 to 2
- second_gain: bfloat16 [768], replicated, may hold values from 0.25 to 1.75
- second_shift: bfloat16 [768], replicated, may hold values from -2 to 2
- mask_vector: bfloat16 [768], replicated, may hold values from -4 to 4
Outputs:
- out_frames: bfloat16 [16384, 768], P(('dp', 'mp'))
- grad_frames: bfloat16 [16384, 768], P(('dp', 'mp'))
- grad_query_weight: float32 [768, 768], P('dp', 'mp')
- grad_key_weight: float32 [768, 768], P('dp', 'mp')
- grad_value_weight: float32 [768, 768], P('dp', 'mp')
- grad_out_weight: float32 [768, 768], P('mp', 'dp')
- grad_up_weight: float32 [768, 3072], P('dp', 'mp')
- grad_down_weight: float32 [3072, 768], P('mp', 'dp')
- grad_query_bias: float32 [12, 64], P('mp', 'dp')
- grad_value_bias: float32 [12, 64], P('mp', 'dp')
- grad_up_bias: float32 [24, 128], P('mp', 'dp')
- grad_out_bias: float32 [768], P(('dp', 'mp'))
- grad_down_bias: float32 [768], P(('dp', 'mp'))
- grad_first_gain: float32 [768], P(('dp', 'mp'))
- grad_first_shift: float32 [768], P(('dp', 'mp'))
- grad_second_gain: float32 [768], P(('dp', 'mp'))
- grad_second_shift: float32 [768], P(('dp', 'mp'))
- grad_mask_vector: float32 [768], P(('dp', 'mp'))
Inputs may be any that keep to these rules, and one draw needn't show every extreme that they name: `lengths`: in each aligned block of 2 clips exactly one clip, drawn from the seed, has 1024 frames, and another has 640. `span_starts`: each start is at most the clip's length minus 10; spans may intersect.
All inputs are finite; a program needn't handle non-finite values.
Results may differ from a plain program's by a relative error of at most 0.022.
Values may be sent and summed in bfloat16 or wider, within the bound.
A program may use at most 128 MiB of HBM per device.

v0:
```python
import math

import jax
import jax.numpy as jnp
from jax import lax
from jax.sharding import PartitionSpec as P

HEAD_DIM = 64
SPAN = 10
LEN = 1024


EPSILON = 1e-05
NEGATIVE = -1e30


def layer_norm(hidden, gain_vec, shift_vec):
    row_mean = jnp.mean(hidden, axis=-1, keepdims=True)
    centered = hidden - row_mean
    variance = jnp.mean(centered * centered, axis=-1, keepdims=True)
    return centered * lax.rsqrt(variance + EPSILON) * gain_vec + shift_vec


def gelu_exact(hidden):
    return jax.nn.gelu(hidden, approximate=False)


def to_heads(block, clip_count):
    heads_here = block.shape[1] // HEAD_DIM
    shaped = block.reshape(clip_count, LEN, heads_here, HEAD_DIM).transpose(0, 2, 1, 3)
    return shaped.reshape(clip_count * heads_here, LEN, HEAD_DIM)


def from_heads(block, clip_count):
    heads_here = block.shape[0] // clip_count
    shaped = block.reshape(clip_count, heads_here, LEN, HEAD_DIM).transpose(0, 2, 1, 3)
    return shaped.reshape(clip_count * LEN, heads_here * HEAD_DIM)


def attend_block(pieces):
    queries, key_rows, values, key_valid = pieces
    score_scale = 1.0 / math.sqrt(HEAD_DIM)
    scores = (
        jnp.einsum("qd,kd->qk", queries, key_rows, preferred_element_type=jnp.float32) * score_scale
    )
    scores = jnp.where(key_valid[None, :], scores, NEGATIVE)
    row_max = jnp.max(scores, axis=1, keepdims=True)
    shifted = jnp.exp(scores - row_max)
    row_total = jnp.sum(shifted, axis=1, keepdims=True)
    attention = (shifted / row_total).astype(jnp.bfloat16)
    attended = jnp.dot(attention, values, preferred_element_type=jnp.float32)
    return (attended.astype(jnp.bfloat16), (row_max + jnp.log(row_total))[:, 0])


def attend_back(pieces):
    queries, key_rows, values, key_valid, log_total, grad_attended = pieces
    score_scale = 1.0 / math.sqrt(HEAD_DIM)
    scores = (
        jnp.einsum("qd,kd->qk", queries, key_rows, preferred_element_type=jnp.float32) * score_scale
    )
    scores = jnp.where(key_valid[None, :], scores, NEGATIVE)
    attention = jnp.exp(scores - log_total[:, None])
    grad_weights = jnp.einsum(
        "qd,kd->qk", grad_attended, values, preferred_element_type=jnp.float32
    )
    grad_values = jnp.einsum(
        "qk,qd->kd",
        attention.astype(jnp.bfloat16),
        grad_attended,
        preferred_element_type=jnp.float32,
    )
    inner_sum = jnp.sum(attention * grad_weights, axis=1, keepdims=True)
    grad_scores = jnp.where(key_valid[None, :], attention * (grad_weights - inner_sum), 0.0).astype(
        jnp.bfloat16
    )
    grad_queries = (
        jnp.einsum("qk,kd->qd", grad_scores, key_rows, preferred_element_type=jnp.float32)
        * score_scale
    )
    grad_keys = (
        jnp.einsum("qk,qd->kd", grad_scores, queries, preferred_element_type=jnp.float32)
        * score_scale
    )
    return (
        grad_queries.astype(jnp.bfloat16),
        grad_keys.astype(jnp.bfloat16),
        grad_values.astype(jnp.bfloat16),
    )


def shards(
    frames,
    lengths,
    span_starts,
    cotangent,
    query_weight,
    key_weight,
    value_weight,
    out_weight,
    up_weight,
    down_weight,
    query_bias,
    value_bias,
    up_bias,
    out_bias,
    down_bias,
    first_gain,
    first_shift,
    second_gain,
    second_shift,
    mask_vector,
):
    local_rows = frames.shape[0]
    clip_count = lengths.shape[0]
    group_rows = clip_count * LEN
    heads_here = query_bias.shape[0]
    row_offset = lax.axis_index("mp") * local_rows
    positions = jnp.arange(LEN, dtype=jnp.int32)
    valid_clip = positions[None, :] < lengths[:, None]
    covered = (positions[None, None, :] >= span_starts[:, :, None]) & (
        positions[None, None, :] < span_starts[:, :, None] + SPAN
    )
    masked_group = jnp.any(covered, axis=1).reshape(group_rows)
    masked_here = lax.dynamic_slice_in_dim(masked_group, row_offset, local_rows)[:, None]
    valid_here = lax.dynamic_slice_in_dim(valid_clip.reshape(group_rows), row_offset, local_rows)
    valid_here = valid_here.astype(jnp.float32)[:, None]
    key_valid = jnp.repeat(valid_clip, heads_here, axis=0)
    query_shift = query_bias.astype(jnp.float32).reshape(-1)
    value_shift = value_bias.astype(jnp.float32).reshape(-1)
    out_shift = out_bias.astype(jnp.float32)
    down_shift = down_bias.astype(jnp.float32)
    gain_one = first_gain.astype(jnp.float32)
    shift_one = first_shift.astype(jnp.float32)
    gain_two = second_gain.astype(jnp.float32)
    shift_two = second_shift.astype(jnp.float32)
    mask_fill = mask_vector.astype(jnp.float32)

    def run_forward(frame_rows, weight_set):
        full_weights = (
            lax.all_gather(weight_set[0], "dp", axis=0, tiled=True),
            lax.all_gather(weight_set[1], "dp", axis=0, tiled=True),
            lax.all_gather(weight_set[2], "dp", axis=0, tiled=True),
            lax.all_gather(weight_set[3], "dp", axis=1, tiled=True),
            lax.all_gather(weight_set[4], "dp", axis=0, tiled=True),
            lax.all_gather(weight_set[5], "dp", axis=1, tiled=True),
        )
        query_full, key_full, value_full, out_full, up_full, down_full = full_weights
        inputs = jnp.where(masked_here, mask_fill[None, :], frame_rows.astype(jnp.float32))
        inputs_all = lax.all_gather(inputs.astype(jnp.bfloat16), "mp", axis=0, tiled=True)
        joined = jnp.concatenate([query_full, key_full, value_full], axis=1)
        projected = jnp.dot(inputs_all, joined, preferred_element_type=jnp.float32)
        width = query_full.shape[1]
        queries = (projected[:, :width] + query_shift).astype(jnp.bfloat16)
        key_rows = projected[:, width : 2 * width].astype(jnp.bfloat16)
        values = (projected[:, 2 * width :] + value_shift).astype(jnp.bfloat16)
        head_out, log_total = lax.map(
            attend_block,
            (
                to_heads(queries, clip_count),
                to_heads(key_rows, clip_count),
                to_heads(values, clip_count),
                key_valid,
            ),
        )
        attended = from_heads(head_out, clip_count)
        piece = attended
        attn_branch = lax.psum_scatter(
            jnp.dot(piece, out_full, preferred_element_type=jnp.float32).astype(jnp.bfloat16),
            "mp",
            scatter_dimension=0,
            tiled=True,
        ).astype(jnp.float32)
        resid_one = inputs + attn_branch + out_shift
        normed_one = layer_norm(resid_one, gain_one, shift_one)
        normed_low = normed_one.astype(jnp.bfloat16)
        up_mats = (up_full, down_full, up_bias)
        ffn_inputs = lax.all_gather(normed_low, "mp", axis=0, tiled=True)
        pre_act = jnp.dot(ffn_inputs, up_full, preferred_element_type=jnp.float32)
        pre_act = pre_act + up_bias.astype(jnp.float32).reshape(-1)
        acted = gelu_exact(pre_act).astype(jnp.bfloat16)
        piece = acted
        ffn_branch = lax.psum_scatter(
            jnp.dot(piece, down_full, preferred_element_type=jnp.float32).astype(jnp.bfloat16),
            "mp",
            scatter_dimension=0,
            tiled=True,
        ).astype(jnp.float32)
        resid_two = normed_one + ffn_branch + down_shift
        output = layer_norm(resid_two, gain_two, shift_two) * valid_here
        saved = (
            out_full,
            joined,
            up_mats,
            inputs_all,
            queries,
            key_rows,
            values,
            log_total,
            attended,
            resid_one,
            ffn_inputs,
            pre_act,
            acted,
            resid_two,
        )
        return (output.astype(jnp.bfloat16), saved)

    weight_set = (query_weight, key_weight, value_weight, out_weight, up_weight, down_weight)
    out_frames, saved = run_forward(frames, weight_set)
    fresh_frames, fresh_weights = lax.optimization_barrier((frames, weight_set))
    saved = run_forward(fresh_frames, fresh_weights)[1]
    (
        out_full,
        joined,
        up_mats,
        inputs_all,
        queries,
        key_rows,
        values,
        log_total,
        attended,
        resid_one,
        ffn_inputs,
        pre_act,
        acted,
        resid_two,
    ) = saved
    grad_out = cotangent.astype(jnp.float32) * valid_here
    _, back_two = jax.vjp(layer_norm, resid_two, gain_two, shift_two)
    grad_two, grad_gain_two, grad_shift_two = back_two(grad_out)
    grad_branch_two = grad_two.astype(jnp.bfloat16)
    _, gelu_back = jax.vjp(gelu_exact, pre_act)
    grad_branch_all = lax.all_gather(grad_branch_two, "mp", axis=0, tiled=True)
    grad_acted = jnp.einsum(
        "gd,fd->gf", grad_branch_all, up_mats[1], preferred_element_type=jnp.float32
    )
    grad_pre = gelu_back(grad_acted)[0].astype(jnp.bfloat16)
    grad_up = jnp.einsum("gd,gf->df", ffn_inputs, grad_pre, preferred_element_type=jnp.float32)
    grad_down = jnp.einsum("gf,gd->fd", acted, grad_branch_all, preferred_element_type=jnp.float32)
    grad_up_shift = jnp.sum(grad_pre, axis=0, dtype=jnp.float32).reshape(up_bias.shape)
    piece = grad_pre
    grad_normed = grad_two + lax.psum_scatter(
        jnp.einsum("gf,df->gd", piece, up_mats[0], preferred_element_type=jnp.float32).astype(
            jnp.bfloat16
        ),
        "mp",
        scatter_dimension=0,
        tiled=True,
    ).astype(jnp.float32)
    _, back_one = jax.vjp(layer_norm, resid_one, gain_one, shift_one)
    grad_one, grad_gain_one, grad_shift_one = back_one(grad_normed)
    grad_branch_one = lax.all_gather(grad_one.astype(jnp.bfloat16), "mp", axis=0, tiled=True)
    grad_out_w = jnp.einsum(
        "gh,gd->hd", attended, grad_branch_one, preferred_element_type=jnp.float32
    )
    grad_attended = jnp.einsum(
        "gd,hd->gh", grad_branch_one, out_full, preferred_element_type=jnp.float32
    )
    grad_attended = grad_attended.astype(jnp.bfloat16)
    grad_query_h, grad_key_h, grad_value_h = lax.map(
        attend_back,
        (
            to_heads(queries, clip_count),
            to_heads(key_rows, clip_count),
            to_heads(values, clip_count),
            key_valid,
            log_total,
            to_heads(grad_attended, clip_count),
        ),
    )
    grad_proj = jnp.concatenate(
        [
            from_heads(grad_query_h, clip_count),
            from_heads(grad_key_h, clip_count),
            from_heads(grad_value_h, clip_count),
        ],
        axis=1,
    )
    width = out_full.shape[0]
    grad_joined = jnp.einsum("gd,gc->dc", inputs_all, grad_proj, preferred_element_type=jnp.float32)
    grad_query_w = grad_joined[:, :width]
    grad_key_w = grad_joined[:, width : 2 * width]
    grad_value_w = grad_joined[:, 2 * width :]
    grad_query_shift = jnp.sum(grad_proj[:, :width], axis=0, dtype=jnp.float32).reshape(
        query_bias.shape
    )
    grad_value_shift = jnp.sum(grad_proj[:, 2 * width :], axis=0, dtype=jnp.float32).reshape(
        value_bias.shape
    )
    piece = grad_proj
    grad_inputs = grad_one + lax.psum_scatter(
        jnp.einsum("gc,dc->gd", piece, joined, preferred_element_type=jnp.float32).astype(
            jnp.bfloat16
        ),
        "mp",
        scatter_dimension=0,
        tiled=True,
    ).astype(jnp.float32)
    grad_frames = jnp.where(masked_here, 0.0, grad_inputs).astype(jnp.bfloat16)
    grad_fill = jnp.sum(jnp.where(masked_here, grad_inputs, 0.0), axis=0)
    row_terms = jnp.stack(
        [
            jnp.sum(grad_one, axis=0),
            jnp.sum(grad_two, axis=0),
            grad_gain_one,
            grad_shift_one,
            grad_gain_two,
            grad_shift_two,
            grad_fill,
        ]
    )
    row_parts = lax.psum_scatter(row_terms, ("dp", "mp"), scatter_dimension=1, tiled=True)
    weight_parts = (
        lax.psum_scatter(grad_query_w, "dp", scatter_dimension=0, tiled=True),
        lax.psum_scatter(grad_key_w, "dp", scatter_dimension=0, tiled=True),
        lax.psum_scatter(grad_value_w, "dp", scatter_dimension=0, tiled=True),
        lax.psum_scatter(grad_out_w, "dp", scatter_dimension=1, tiled=True),
        lax.psum_scatter(grad_up, "dp", scatter_dimension=0, tiled=True),
        lax.psum_scatter(grad_down, "dp", scatter_dimension=1, tiled=True),
        lax.psum_scatter(grad_query_shift, "dp", scatter_dimension=1, tiled=True),
        lax.psum_scatter(grad_value_shift, "dp", scatter_dimension=1, tiled=True),
        lax.psum_scatter(grad_up_shift, "dp", scatter_dimension=1, tiled=True),
    )
    return (
        out_frames,
        grad_frames,
        weight_parts[0],
        weight_parts[1],
        weight_parts[2],
        weight_parts[3],
        weight_parts[4],
        weight_parts[5],
        weight_parts[6],
        weight_parts[7],
        weight_parts[8],
        row_parts[0],
        row_parts[1],
        row_parts[2],
        row_parts[3],
        row_parts[4],
        row_parts[5],
        row_parts[6],
    )


def solution(mesh):
    return jax.shard_map(
        shards,
        mesh=mesh,
        in_specs=(
            P(("dp", "mp"), None),
            P("dp"),
            P("dp", None),
            P(("dp", "mp"), None),
            P("dp", "mp"),
            P("dp", "mp"),
            P("dp", "mp"),
            P("mp", "dp"),
            P("dp", "mp"),
            P("mp", "dp"),
            P("mp", None),
            P("mp", None),
            P("mp", None),
            P(),
            P(),
            P(),
            P(),
            P(),
            P(),
            P(),
        ),
        out_specs=(
            P(("dp", "mp"), None),
            P(("dp", "mp"), None),
            P("dp", "mp"),
            P("dp", "mp"),
            P("dp", "mp"),
            P("mp", "dp"),
            P("dp", "mp"),
            P("mp", "dp"),
            P("mp", "dp"),
            P("mp", "dp"),
            P("mp", "dp"),
            P(("dp", "mp")),
            P(("dp", "mp")),
            P(("dp", "mp")),
            P(("dp", "mp")),
            P(("dp", "mp")),
            P(("dp", "mp")),
            P(("dp", "mp")),
        ),
        check_vma=False,
    )
```

profile of v0, /device:TPU:16, one launch (start us, length us, event | category | flops | bytes accessed | tf_op | source)
XLA Modules:
  0.0 1194.8 jit_solution(10546854757807781122)
XLA Ops:
  14.8 9.6 all_gather.55
  24.4 9.5 all_gather.56
  33.9 8.6 all_gather.57
  42.5 9.5 all_gather.63
  52.1 8.6 all_gather.64
  60.7 9.5 all_gather.65
  70.2 8.6 all_gather.66
  78.8 10.8 all_gather.58
  89.6 4.1 fusion.112
  96.9 44.3 %all-gather.11.cloned.1.call-done = bf16[2048,768]{1,0:T(8,128)(2,1)} async-done(((bf16[512,768]{1,0:T(8,128)(2,1)}), bf16[2048,768]{1,0:T(8,128)(2,1)}) %all-gather.11.cloned.1.call-update) | async-done | bytes 3145744 | tf_op jit(solution)/shard_map/all_gather | solution.py:149
  141.1 4.3 fusion.104
  163.0 58.8 %while.37 = (s32[]{:T(128)}, bf16[6,1024,64]{1,2,0:T(8,128)(2,1)}, f32[6,1024]{1,0:T(8,128)}, pred[6,1024]{1,0:T(8,128)(4,1)S(1)}, bf16[6,1024,64]{2,1,0:T(8,128...) while((s32[]{:T(128)}, bf16[6,1024,64]{1,2,0:T(8,128)(2,1)}, ...), condition=%wide.region_14.15_spmd, body=%wide.region_11.14_spmd.sunk | while | flops 281082880 | bytes 30330012 | solution.py:156
  168.6 4.1 fusion.216
  178.4 4.1 fusion.216
  188.2 4.1 fusion.216
  198.0 4.1 fusion.216
  207.8 4.1 fusion.216
  217.6 4.1 fusion.216
  234.9 3.4 copy.82
  243.3 27.7 %while.36 = (s32[]{:T(128)}, bf16[6,1024,64]{1,2,0:T(8,128)(2,1)}, pred[6,1024]{1,0:T(8,128)(4,1)S(1)}, bf16[6,1024,64]{2,1,0:T(8,128)(2,1)S(1)}, bf16[6,1024,64...) while((s32[]{:T(128)}, bf16[6,1024,64]{1,2,0:T(8,128)(2,1)}, ...), condition=%wide.region_4.5_spmd, body=%wide.region_1.4_spmd.sunk | while | flops 281081856 | bytes 13528145 | solution.py:156
  276.8 11.8 reduce-scatter.31.cloned.1.call-done
  290.3 60.7 %reduce-scatter.27.cloned.1.call-done = bf16[512,768]{1,0:T(8,128)(2,1)} async-done(((bf16[2048,768]{1,0:T(8,128)(2,1)}), bf16[512,768]{1,0:T(8,128)(2,1)}) %reduce-scatter.27.cloned.1.call-update) | async-done | bytes 786448 | tf_op jit(solution)/shard_map/reduce_scatter | solution.py:167
  356.0 61.4 %all-gather.21.cloned.1.call-done = bf16[2048,768]{1,0:T(8,128)(2,1)} async-done(((bf16[512,768]{1,0:T(8,128)(2,1)}), bf16[2048,768]{1,0:T(8,128)(2,1)}) %all-gather.21.cloned.1.call-update) | async-done | bytes 3145744 | tf_op jit(solution)/shard_map/all_gather | solution.py:177
  417.5 19.3 %multiply_convert_fusion = (bf16[2048,768]{1,0:T(8,128)(2,1)}, f32[2048,768]{1,0:T(8,128)}, f32[2048,768]{1,0:T(8,128)}) fusion(f32[768]{0:T(1024)S(1)} %bitcast_convert_fusion, bf16[2048,768]{1,0:T(8,128)(2,1)} %all-gather.21.cloned.1.call-done, bf16[768,768]{1,0:T(8,128)(2,1)} %all-gather.23.cloned.1.call-done), kind=kOutput, calls=%fused_computation.93 | convolution fusion | flops 2519728128 | bytes 20057088 | tf_op jit(solution)/shard_map/dot_general | solution.py:178
  436.7 6.4 all-gather.25.cloned.1.call-done
  443.1 6.6 convolution_convert_fusion.2
  450.6 59.5 %reduce-scatter.33.cloned.1.call-done = bf16[512,768]{1,0:T(8,128)(2,1)} async-done(((bf16[2048,768]{1,0:T(8,128)(2,1)}), bf16[512,768]{1,0:T(8,128)(2,1)}) %reduce-scatter.33.cloned.1.call-update) | async-done | bytes 786448 | tf_op jit(solution)/shard_map/reduce_scatter | solution.py:182
  517.4 61.7 %all-gather.27.cloned.1.call-done = bf16[2048,768]{1,0:T(8,128)(2,1)} async-done(((bf16[512,768]{1,0:T(8,128)(2,1)}), bf16[2048,768]{1,0:T(8,128)(2,1)}) %all-gather.27.cloned.1.call-update) | async-done | bytes 3145744 | tf_op jit(solution)/shard_map/all_gather | solution.py:233
  579.0 11.1 convert_reduce_fusion
  591.7 4.1 convolution_convert_fusion.1
  597.1 59.0 %reduce-scatter.35.cloned.1.call-done = bf16[512,768]{1,0:T(8,128)(2,1)} async-done(((bf16[2048,768]{1,0:T(8,128)(2,1)}), bf16[512,768]{1,0:T(8,128)(2,1)}) %reduce-scatter.35.cloned.1.call-update) | async-done | bytes 786448 | tf_op jit(solution)/shard_map/reduce_scatter | solution.py:242
  656.2 3.6 multiply_reduce_fusion.2
  667.7 59.2 %all-gather.29.cloned.1.call-done = bf16[2048,768]{1,0:T(8,128)(2,1)} async-done(((bf16[512,768]{1,0:T(8,128)(2,1)}), bf16[2048,768]{1,0:T(8,128)(2,1)}) %all-gather.29.cloned.1.call-update) | async-done | bytes 3145744 | tf_op jit(solution)/shard_map/all_gather | solution.py:252
  733.0 73.0 %while.38 = (s32[]{:T(128)}, bf16[6,1024,64]{1,2,0:T(8,128)(2,1)S(1)}, bf16[6,1024,64]{1,2,0:T(8,128)(2,1)S(1)}, bf16[6,1024,64]{1,2,0:T(8,128)(2,1)S(1)}, pred[...) while((s32[]{:T(128)}, ...), condition=%wide.region_28.29_spmd, body=%wide.region_26.28_spmd.sunk | while | flops 688192512 | bytes 33724532 | solution.py:260
  819.8 6.1 convolution_convert_fusion
  826.0 17.4 %all-gather.13.cloned.1.call-done = bf16[2048,768]{1,0:T(8,128)(2,1)} async-done(((bf16[512,768]{1,0:T(8,128)(2,1)}), bf16[2048,768]{1,0:T(8,128)(2,1)}) %all-gather.13.cloned.1.call-update) | async-done | bytes 3145744 | tf_op jit(solution)/shard_map/all_gather | solution.py:177
  843.4 20.9 %convolution_convert_fusion.3 = bf16[2048,768]{1,0:T(8,128)(2,1)} fusion(bf16[768,768]{0,1:T(8,128)(2,1)} %all-gather.17.cloned.1.call-done, bf16[2048,768]{1,0:T(8,128)(2,1)} %all-gather.13.cloned.1.call-done, bf16[768,768]{1,0:T(8,128)(2,1)} %all-gather.15.cloned.1.call-done, f32[768]{0:T(1024)S(1)} %copy-done.72), kind=kOutput, calls=%fused_computation.125 | convolution fusion | flops 4937220096 | bytes 8653824 | tf_op jit(solution)/shard_map/dot_general | solution.py:183
  864.6 7.0 fusion.157
  871.6 7.0 fusion.156
  878.7 4.6 fusion.158
  895.2 13.6 %all-reduce.3 = (f32[3,64]{1,0:T(4,128)S(1)}, f32[3,64]{1,0:T(4,128)S(1)}) all-reduce(f32[3,64]{1,0:T(4,128)S(1)} %convert_reduce_fusion.2, f32[3,64]{1,0:T(4,128)S(1)} %convert_reduce_fusion.1), channel_id=14, replica_groups=mesh['dp'=8,'mp'=4] {'dp'}, use_global_device_ids=true, to_apply=%region_37.38.clone | all-reduce | flops 384 | bytes 3072
  914.0 62.7 %reduce-scatter.29.cloned.1.call-done = bf16[512,768]{1,0:T(8,128)(2,1)} async-done(((bf16[2048,768]{1,0:T(8,128)(2,1)}), bf16[512,768]{1,0:T(8,128)(2,1)}) %reduce-scatter.29.cloned.1.call-update) | async-done | bytes 786448 | tf_op jit(solution)/shard_map/reduce_scatter | solution.py:182
  976.7 3.5 select_reduce_fusion
  980.3 39.3 %all-reduce.2 = f32[7,768]{1,0:T(8,128)S(1)} all-reduce(f32[7,768]{1,0:T(8,128)S(1)} %stack.19), channel_id=17, replica_groups=mesh['dp'=8,'mp'=4] {'dp','mp'}, use_global_device_ids=true, to_apply=%region_49.50.clone | all-reduce | flops 5376 | bytes 43008
  1023.3 46.5 %reduce-scatter.39.cloned.1.call-done = f32[96,768]{1,0:T(8,128)} async-done(((f32[768,768]{1,0:T(8,128)}), f32[96,768]{1,0:T(8,128)}) %reduce-scatter.39.cloned.1.call-update) | async-done | bytes 294928 | tf_op jit(solution)/shard_map/reduce_scatter | solution.py:318
  1069.7 38.9 %reduce-scatter.43.cloned.1.call-done = f32[96,192]{1,0:T(8,128)} async-done(((f32[768,192]{1,0:T(8,128)}), f32[96,192]{1,0:T(8,128)}) %reduce-scatter.43.cloned.1.call-update) | async-done | bytes 73744
  1108.6 39.1 %reduce-scatter.45.cloned.1.call-done = f32[96,192]{1,0:T(8,128)} async-done(((f32[768,192]{1,0:T(8,128)}), f32[96,192]{1,0:T(8,128)}) %reduce-scatter.45.cloned.1.call-update) | async-done | bytes 73744
  1147.7 39.1 %reduce-scatter.47.cloned.1.call-done = f32[96,192]{1,0:T(8,128)} async-done(((f32[768,192]{1,0:T(8,128)}), f32[96,192]{1,0:T(8,128)}) %reduce-scatter.47.cloned.1.call-update) | async-done | bytes 73744
  (454 shorter events, 250.7 us)
Async XLA Ops:
  8.1 81.5 %all-gather.19.cloned.1.call-start = ((), (), s32[]{:S(2)}) async-start(), calls=%async_computation.19 | async-start | bytes 3932160 | tf_op jit(solution)/shard_map/all_gather | solution.py:149
  13.4 127.7 %all-gather.11.cloned.1.call-start = ((), (), s32[]{:S(2)}) async-start(), calls=%async_computation.13 | async-start | bytes 3932160 | tf_op jit(solution)/shard_map/all_gather | solution.py:149
  14.2 274.4 %reduce-scatter.31.cloned.1.call-start = ((), (), s32[]{:S(2)}) async-start(), calls=%async_computation.20 | async-start | bytes 3932160 | tf_op jit(solution)/shard_map/reduce_scatter | solution.py:167
  14.6 27.9 %copy-start.45 = (pred[2,1024]{1,0:T(4,128)(4,1)}, pred[2,1024]{1,0:T(4,128)(4,1)S(1)}, u32[]{:S(2)}) copy-start(pred[2,1024]{1,0:T(4,128)(4,1)S(1)} %iota_compare_fusion.2) | copy-start | bytes 6148
  52.1 41.6 %copy-start.20 = (bf16[768,192]{1,0:T(8,128)(2,1)}, bf16[768,192]{1,0:T(8,128)(2,1)S(1)}, u32[]{:S(2)}) copy-start(bf16[768,192]{1,0:T(8,128)(2,1)S(1)} %all_gather.63) | copy-start | bytes 884740
  60.7 33.1 %copy-start.22 = (bf16[768,192]{1,0:T(8,128)(2,1)}, bf16[768,192]{1,0:T(8,128)(2,1)S(1)}, u32[]{:S(2)}) copy-start(bf16[768,192]{1,0:T(8,128)(2,1)S(1)} %all_gather.64) | copy-start | bytes 884740
  228.1 122.9 %reduce-scatter.27.cloned.1.call-start = ((), (), s32[]{:S(2)}) async-start(), calls=%async_computation.14 | async-start | bytes 3932160 | tf_op jit(solution)/shard_map/reduce_scatter | solution.py:167
  276.1 80.0 %all-gather.23.cloned.1.call-start = ((), (), s32[]{:S(2)}) async-start(), calls=%async_computation.22 | async-start | bytes 1327104 | tf_op jit(solution)/shard_map/all_gather | solution.py:144
  276.6 140.8 %all-gather.21.cloned.1.call-start = ((), (), s32[]{:S(2)}) async-start(), calls=%async_computation.21 | async-start | bytes 3932160 | tf_op jit(solution)/shard_map/all_gather | solution.py:177
  276.7 233.3 %copy-start.33 = (f32[768]{0:T(1024)}, f32[768]{0:T(1024)S(1)}, u32[]{:S(2)}) copy-start(f32[768]{0:T(1024)S(1)} %convert_element_type.169) | copy-start | bytes 9220
  276.8 233.3 %copy-start.36 = (f32[768]{0:T(1024)}, f32[768]{0:T(1024)S(1)}, u32[]{:S(2)}) copy-start(f32[768]{0:T(1024)S(1)} %convert_element_type.170) | copy-start | bytes 9220
  288.6 65.3 %copy-start.2 = (bf16[512,768]{1,0:T(8,128)(2,1)S(1)}, bf16[512,768]{1,0:T(8,128)(2,1)}, u32[]{:S(2)}) copy-start(bf16[512,768]{1,0:T(8,128)(2,1)} %reduce-scatter.31.cloned.1.call-done) | copy-start | bytes 2359300
  290.3 65.7 %copy-start.76 = (bf16[6,128]{1,0:T(8,128)(2,1)S(1)}, bf16[6,128]{1,0:T(8,128)(2,1)}, u32[]{:S(2)}) copy-start(bf16[6,128]{1,0:T(8,128)(2,1)} %param.38) | copy-start | bytes 4612
  290.3 219.7 %copy-start.39 = (f32[512]{0:T(512)}, f32[512]{0:T(512)S(1)}, u32[]{:S(2)}) copy-start(f32[512]{0:T(512)S(1)} %broadcast_multiply_fusion.1) | copy-start | bytes 6148
  353.9 82.9 %copy-start.61 = (f32[512]{0:T(512)}, f32[512]{0:T(512)S(1)}, u32[]{:S(2)}) copy-start(f32[512]{0:T(512)S(1)} %get-tuple-element.244) | copy-start | bytes 6148
  353.9 156.2 %copy-start.43 = (f32[512]{0:T(512)}, f32[512]{0:T(512)S(1)}, u32[]{:S(2)}) copy-start(f32[512]{0:T(512)S(1)} %fusion.113) | copy-start | bytes 6148
  355.3 87.8 %all-gather.25.cloned.1.call-start = ((), (), s32[]{:S(2)}) async-start(), calls=%async_computation.23 | async-start | bytes 1327104 | tf_op jit(solution)/shard_map/all_gather | solution.py:145
  355.9 154.1 %reduce-scatter.33.cloned.1.call-start = ((), (), s32[]{:S(2)}) async-start(), calls=%async_computation.24 | async-start | bytes 3932160 | tf_op jit(solution)/shard_map/reduce_scatter | solution.py:182
  356.0 80.7 %copy-start.71 = (f32[768]{0:T(1024)}, f32[768]{0:T(1024)S(1)}, u32[]{:S(2)}) copy-start(f32[768]{0:T(1024)S(1)} %bitcast_convert_fusion) | copy-start | bytes 9220
  449.7 62.8 %copy-start.15 = (bf16[512,768]{1,0:T(8,128)(2,1)S(1)}, bf16[512,768]{1,0:T(8,128)(2,1)}, u32[]{:S(2)}) copy-start(bf16[512,768]{1,0:T(8,128)(2,1)} %param.29) | copy-start | bytes 2359300
  449.7 129.3 %all-gather.27.cloned.1.call-start = ((), (), s32[]{:S(2)}) async-start(), calls=%async_computation.25 | async-start | bytes 3932160 | tf_op jit(solution)/shard_map/all_gather | solution.py:233
  450.4 63.4 %copy-start.47 = (f32[768]{0:T(1024)}, f32[768]{0:T(1024)S(1)}, u32[]{:S(2)}) copy-start(f32[768]{0:T(1024)S(1)} %convert_element_type.175) | copy-start | bytes 9220
  450.5 63.4 %copy-start.41 = (f32[768]{0:T(1024)}, f32[768]{0:T(1024)S(1)}, u32[]{:S(2)}) copy-start(f32[768]{0:T(1024)S(1)} %convert_element_type.176) | copy-start | bytes 9220
  450.6 63.3 %copy-start.51 = (f32[512]{0:T(512)}, f32[512]{0:T(512)S(1)}, u32[]{:S(2)}) copy-start(f32[512]{0:T(512)S(1)} %dynamic-slice_convert_fusion) | copy-start | bytes 6148
  516.9 139.2 %reduce-scatter.35.cloned.1.call-start = ((), (), s32[]{:S(2)}) async-start(), calls=%async_computation.26 | async-start | bytes 3932160 | tf_op jit(solution)/shard_map/reduce_scatter | solution.py:242
  595.8 131.0 %all-gather.29.cloned.1.call-start = ((), (), s32[]{:S(2)}) async-start(), calls=%async_computation.27 | async-start | bytes 3932160 | tf_op jit(solution)/shard_map/all_gather | solution.py:252
  664.5 161.4 %all-gather.15.cloned.1.call-start = ((), (), s32[]{:S(2)}) async-start(), calls=%async_computation.16 | async-start | bytes 1327104 | tf_op jit(solution)/shard_map/all_gather | solution.py:144
  665.1 160.9 %all-gather.17.cloned.1.call-start = ((), (), s32[]{:S(2)}) async-start(), calls=%async_computation.17 | async-start | bytes 1327104 | tf_op jit(solution)/shard_map/all_gather | solution.py:145
  665.9 177.5 %all-gather.13.cloned.1.call-start = ((), (), s32[]{:S(2)}) async-start(), calls=%async_computation.15 | async-start | bytes 3932160 | tf_op jit(solution)/shard_map/all_gather | solution.py:177
  666.6 222.9 %reduce-scatter.51.cloned.1.call-start = ((), (), s32[]{:S(2)}) async-start(), calls=%async_computation.35 | async-start | bytes 73728
  667.5 242.1 %reduce-scatter.49.cloned.1.call-start = ((), (), s32[]{:S(2)}) async-start(), calls=%async_computation.34 | async-start | bytes 884736
  816.4 97.6 %reduce-scatter.37.cloned.1.call-start = ((), (), s32[]{:S(2)}) async-start(), calls=%async_computation.28 | async-start | bytes 3932160 | tf_op jit(solution)/shard_map/reduce_scatter | solution.py:291
  825.9 150.7 %reduce-scatter.29.cloned.1.call-start = ((), (), s32[]{:S(2)}) async-start(), calls=%async_computation.18 | async-start | bytes 3932160 | tf_op jit(solution)/shard_map/reduce_scatter | solution.py:182
  864.3 159.0 %reduce-scatter.41.cloned.1.call-start = ((), (), s32[]{:S(2)}) async-start(), calls=%async_computation.30 | async-start | bytes 2654208 | tf_op jit(solution)/shard_map/reduce_scatter | solution.py:319
  871.6 198.2 %reduce-scatter.39.cloned.1.call-start = ((), (), s32[]{:S(2)}) async-start(), calls=%async_computation.29 | async-start | bytes 2654208 | tf_op jit(solution)/shard_map/reduce_scatter | solution.py:318
  878.6 230.0 %reduce-scatter.43.cloned.1.call-start = ((), (), s32[]{:S(2)}) async-start(), calls=%async_computation.31 | async-start | bytes 884736
  885.7 91.0 %copy-start.7 = (bf16[512,768]{1,0:T(8,128)(2,1)S(1)}, bf16[512,768]{1,0:T(8,128)(2,1)}, u32[]{:S(2)}) copy-start(bf16[512,768]{1,0:T(8,128)(2,1)} %reduce-scatter.27.cloned.1.call-done) | copy-start | bytes 2359300
  885.7 91.0 %copy-start.35 = (f32[768]{0:T(1024)S(1)}, f32[768]{0:T(1024)}, u32[]{:S(2)}) copy-start(f32[768]{0:T(1024)} %copy-done.33) | copy-start | bytes 9220
  885.7 91.0 %copy-start.38 = (f32[768]{0:T(1024)S(1)}, f32[768]{0:T(1024)}, u32[]{:S(2)}) copy-start(f32[768]{0:T(1024)} %copy-done.36) | copy-start | bytes 9220
  885.7 91.0 %copy-start.48 = (f32[768]{0:T(1024)S(1)}, f32[768]{0:T(1024)}, u32[]{:S(2)}) copy-start(f32[768]{0:T(1024)} %copy-done.47) | copy-start | bytes 9220
  885.7 91.0 %copy-start.50 = (f32[512]{0:T(512)S(1)}, f32[512]{0:T(512)}, u32[]{:S(2)}) copy-start(f32[512]{0:T(512)} %broadcast_multiply_fusion.3) | copy-start | bytes 6148
  885.7 91.0 %copy-start.58 = (pred[512]{0:T(512)(128)(4,1)S(1)}, pred[512]{0:T(512)(128)(4,1)}, u32[]{:S(2)}) copy-start(pred[512]{0:T(512)(128)(4,1)} %copy-done.55) | copy-start | bytes 1540
  885.7 91.0 %copy-start.60 = (f32[512]{0:T(512)S(1)}, f32[512]{0:T(512)}, u32[]{:S(2)}) copy-start(f32[512]{0:T(512)} %copy-done.59) | copy-start | bytes 6148
  885.7 91.0 %copy-start.64 = (f32[512]{0:T(512)S(1)}, f32[512]{0:T(512)}, u32[]{:S(2)}) copy-start(f32[512]{0:T(512)} %copy-done.63) | copy-start | bytes 6148
  885.7 261.9 %reduce-scatter.45.cloned.1.call-start = ((), (), s32[]{:S(2)}) async-start(), calls=%async_computation.32 | async-start | bytes 884736
  888.2 298.6 %reduce-scatter.47.cloned.1.call-start = ((), (), s32[]{:S(2)}) async-start(), calls=%async_computation.33 | async-start | bytes 884736
  911.1 109.4 %copy-start.42 = (f32[768]{0:T(1024)S(1)}, f32[768]{0:T(1024)}, u32[]{:S(2)}) copy-start(f32[768]{0:T(1024)} %copy-done.41) | copy-start | bytes 9220
  911.1 109.4 %copy-start.52 = (f32[512]{0:T(512)S(1)}, f32[512]{0:T(512)}, u32[]{:S(2)}) copy-start(f32[512]{0:T(512)} %copy-done.51) | copy-start | bytes 6148
  (71 other events, 402.8 us)
Sparse Core Ops, SparseCore 0:
  13.5 63.2 all-gather.18
  79.0 62.1 all-gather.10
  228.2 60.2 reduce-scatter.30
  290.7 60.2 reduce-scatter.26
  664.7 62.1 all-gather.28
  728.7 24.0 all-gather.14
  754.9 24.0 all-gather.16
  781.2 62.1 all-gather.12
Sparse Core Ops, SparseCore 1:
  278.4 23.9 all-gather.22
  355.4 62.0 all-gather.20
  419.2 23.8 all-gather.24
  449.8 60.2 reduce-scatter.32
  517.0 62.0 all-gather.26
  595.9 60.1 reduce-scatter.34
  670.7 33.2 reduce-scatter.50
  816.5 34.9 reduce-scatter.48
  853.8 60.2 reduce-scatter.36
  916.4 60.2 reduce-scatter.28
  980.8 42.4 reduce-scatter.40
  1027.2 42.5 reduce-scatter.38
  1073.6 34.9 reduce-scatter.42
  1112.7 34.9 reduce-scatter.44
  1151.7 34.9 reduce-scatter.46
where the time goes:
time: 1200 us; the launch traced here: 1190 us
  waiting for transfers between devices  676 us (56%)
  matrix products  216 us (18%)
  blocking collectives  128 us (11%)
  local copies, waits for them, and re-layouts  94.9 us (8%)
  other arithmetic  59.8 us (5%)
  between operations  18.2 us (2%)
    reduce_scatter x2, waiting for transfers between devices, run_forward(): lax.psum_scatter(jnp.dot(piece, down_full, preferred_element_type=jnp.flo...  122 us
    unnamed x28, waiting for transfers between devices  121 us
    all_gather x2, waiting for transfers between devices, run_forward(): ffn_inputs = lax.all_gather(normed_low, 'mp', axis=0, tiled=True)  78.8 us
    reduce_scatter x2, waiting for transfers between devices, run_forward(): lax.psum_scatter(jnp.dot(piece, out_full, preferred_element_type=jnp.floa...  72.5 us
    all_gather x1, waiting for transfers between devices, shards(): grad_branch_all = lax.all_gather(grad_branch_two, 'mp', axis=0, tiled=True)  61.7 us
    all_gather x1, waiting for transfers between devices, shards(): lax.all_gather(grad_one.astype(jnp.bfloat16), 'mp', axis=0, tiled=True)  59.2 us
    reduce_scatter x1, waiting for transfers between devices, shards(): lax.psum_scatter(jnp.einsum('gf,df->gd', piece, up_mats[0], preferred_ele...  59 us
    unnamed x2, blocking collectives  52.9 us
  transfers between devices with their start and end apart: 23, of which 17 were waited for; matrix products, arithmetic and copies ran while one was open for 20% of the time, Pallas kernels for 0%

commit v1 on v0

v1 whole, which is shorter than its diff:
```python
import functools
import math

import jax
import jax.numpy as jnp
from jax import lax
from jax.experimental import pallas as pl
from jax.experimental.pallas import tpu as pltpu
from jax.sharding import PartitionSpec as P

HEAD_DIM = 64
SPAN = 10
LEN = 1024
EPSILON = 1e-05
NEGATIVE = -1e30
SCALE = 1.0 / math.sqrt(HEAD_DIM)

F32 = jnp.float32
BF16 = jnp.bfloat16
MESH = pl.DeviceIdType.MESH
VMEM_LIMIT = 62 * 1024 * 1024

ATT, UP, DOWN = 0, 1, 2
PROJ = 640


def dot(left, right, contract=(1, 0)):
    return lax.dot_general(
        left, right, (((contract[0],), (contract[1],)), ((), ())), preferred_element_type=F32
    )


def hbm():
    return pl.BlockSpec(memory_space=pl.ANY)


def vmem():
    return pl.BlockSpec(memory_space=pltpu.VMEM)


class Place:
    def __init__(self):
        self.dp = lax.axis_index("dp")
        self.z = lax.axis_index("mp")
        self.c = lax.rem(self.dp, 2)
        self.x = lax.rem(self.dp // 2, 2)
        self.y = self.dp // 4
        self.core = (self.dp + 1 - 2 * self.c, self.z)
        self.across_x = (self.dp + 2 - 4 * self.x, self.z)
        self.across_y = (self.dp + 4 - 8 * self.y, self.z)
        self.right = (self.dp, self.z + 1)
        self.left = (self.dp, self.z - 1)
        self.mate = (self.dp, self.z + 1 - 2 * lax.rem(self.z, 2))
        self.far = (self.dp, lax.rem(self.z + 2, 4))

    def greet(self, far):
        barrier = pltpu.get_barrier_semaphore()

        def signal(device):
            pl.semaphore_signal(barrier, inc=1, device_id=device, device_id_type=MESH)

        signal(self.core)
        signal(self.across_x)
        signal(self.across_y)
        if far:
            signal(self.far)
        pl.when(self.z < 3)(lambda: signal(self.right))
        pl.when(self.z > 0)(lambda: signal(self.left))
        ends = jnp.where((self.z == 0) | (self.z == 3), 1, 2)
        pl.semaphore_wait(barrier, (4 if far else 3) + ends)


def remote(src, dst, send, recv, device):
    return pltpu.make_async_remote_copy(
        src_ref=src, dst_ref=dst, send_sem=send, recv_sem=recv, device_id=device, device_id_type=MESH
    )


class Gather:
    def __init__(self, at, blocks, biases, z_send, z_recv, p_send, p_recv):
        self.at, self.blocks, self.biases = at, blocks, biases
        self.z_send, self.z_recv, self.p_send, self.p_recv = z_send, z_recv, p_send, p_recv

    def z_copy(self, kind, m, direction, step):
        at = self.at
        if kind == 3:
            ref = self.biases.at[m]
        else:
            ref = self.blocks.at[kind, m, at.y, at.x, at.c]
        device = at.right if direction == 0 else at.left
        return remote(ref, ref, self.z_send.at[kind, direction, step], self.z_recv.at[kind, m], device)

    def z_step(self, kind, step):
        z = self.at.z
        if step == 0:
            pl.when(z < 3)(lambda: self.z_copy(kind, z, 0, 0).start())
            pl.when(z > 0)(lambda: self.z_copy(kind, z, 1, 0).start())
            return

        @pl.when(z >= step)
        def _():
            self.z_copy(kind, z - step, 0, 0).wait_recv()
            if step < 3:
                pl.when(z < 3)(lambda: self.z_copy(kind, z - step, 0, step).start())

        @pl.when(z + step <= 3)
        def _():
            self.z_copy(kind, z + step, 1, 0).wait_recv()
            if step < 3:
                pl.when(z > 0)(lambda: self.z_copy(kind, z + step, 1, step).start())

    def plane_copy(self, kind, which):
        at, blocks = self.at, self.blocks.at[kind]
        x, y, c = at.x, at.y, at.c
        low, high = pl.ds(0, 48), pl.ds(48, 48)
        ref, device = {
            0: lambda: (blocks.at[:, y, x, c, low], at.across_x),
            1: lambda: (blocks.at[:, y, x, c, high], at.across_y),
            2: lambda: (blocks.at[:, y, :, c, low], at.across_y),
            3: lambda: (blocks.at[:, :, x, c, high], at.across_x),
            4: lambda: (blocks.at[:, y, x, c], at.core),
            5: lambda: (blocks.at[:, y, 1 - x, c, low], at.core),
            6: lambda: (blocks.at[:, 1 - y, x, c, high], at.core),
            7: lambda: (blocks.at[:, 1 - y, :, c, low], at.core),
            8: lambda: (blocks.at[:, :, 1 - x, c, high], at.core),
        }[which]()
        return remote(ref, ref, self.p_send.at[kind, which], self.p_recv.at[kind, which], device)

    def first(self, kind):
        for which in (0, 1, 4):
            self.plane_copy(kind, which).start()

    def second(self, kind):
        self.plane_copy(kind, 0).wait_recv()
        self.plane_copy(kind, 2).start()
        self.plane_copy(kind, 5).start()
        self.plane_copy(kind, 1).wait_recv()
        self.plane_copy(kind, 3).start()
        self.plane_copy(kind, 6).start()

    def third(self, kind):
        self.plane_copy(kind, 2).wait_recv()
        self.plane_copy(kind, 7).start()
        self.plane_copy(kind, 3).wait_recv()
        self.plane_copy(kind, 8).start()

    def last(self, kind):
        for which in range(4, 9):
            self.plane_copy(kind, which).wait_recv()

    def drain(self):
        z = self.at.z
        for kind in range(4):
            for step in range(3):
                pl.when((z < 3) & (z >= step))(
                    lambda k=kind, s=step: self.z_copy(k, z - s, 0, s).wait_send()
                )
                pl.when((z > 0) & (z + step <= 3))(
                    lambda k=kind, s=step: self.z_copy(k, z + s, 1, s).wait_send()
                )
        for kind in range(3):
            for which in range(9):
                self.plane_copy(kind, which).wait_send()


def block_of(blocks, kind, m, low=0, width=768):
    return blocks[kind, m, :, :, :, :, pl.ds(low, width)].reshape(768, width)


def lane_mask(rows, lower):
    lanes = lax.broadcasted_iota(jnp.int32, (rows, 128), 1)
    return (lanes < 64) if lower else (lanes >= 64)


def forward_compute(
    blocks,
    biases,
    xs,
    keybias_ref,
    valid_ref,
    cot_ref,
    vec_ref,
    probs_hbm,
    out_ref,
    recip_ref,
    headout_ref,
    xt_ref,
    qm_ref,
    kt_ref,
    v_ref,
    att_ref,
    acted_ref,
    slope_ref,
    n1t_ref,
    n1_ref,
    rs1_ref,
    gb2_ref,
    gb2t_ref,
    g2_ref,
    sums_ref,
    k_ref,
    vt_ref,
    att_t,
    probs,
    probs_sem,
    total,
    low,
    hooks,
):
    rows = xs.shape[1]
    for side in range(2):
        xt_ref[side] = xs[side].T
    ones_lane = jnp.where(lax.broadcasted_iota(jnp.int32, (rows, 128), 1) == 0, 1.0, 0.0).astype(BF16)

    def probs_copy(head, slot):
        return pltpu.make_async_copy(probs.at[slot], probs_hbm.at[head], probs_sem.at[slot])

    def project(m, _):
        bias = biases[m, 0:1, :].astype(F32)[:, :PROJ]
        own = dot(xs[0], block_of(blocks, ATT, m, 0, PROJ)) + bias
        other = dot(xs[1], block_of(blocks, ATT, m, 128, 512)) + bias[:, 128:]
        k_ref[2 * m, :rows] = own[:, 128:256].astype(BF16)
        k_ref[2 * m, rows:] = other[:, 0:128].astype(BF16)
        v_ref[2 * m, :rows] = own[:, 256:384].astype(BF16)
        v_ref[2 * m, rows:] = other[:, 128:256].astype(BF16)
        k_ref[2 * m + 1, :rows] = own[:, 384:512].astype(BF16)
        k_ref[2 * m + 1, rows:] = other[:, 256:384].astype(BF16)
        v_ref[2 * m + 1, :rows] = own[:, 512:640].astype(BF16)
        v_ref[2 * m + 1, rows:] = other[:, 384:512].astype(BF16)
        lower, upper = lane_mask(rows, True), lane_mask(rows, False)
        pair = own[:, 0:128].astype(BF16).astype(F32) * SCALE
        single = pltpu.roll(own[:, 384:512].astype(BF16).astype(F32) * SCALE, 64, 1)
        qm_ref[3 * m] = jnp.where(lower, pair, 0.0).astype(BF16)
        qm_ref[3 * m + 1] = jnp.where(upper, pair, 0.0).astype(BF16)
        qm_ref[3 * m + 2] = jnp.where(upper, single, 0.0).astype(BF16)
        for tile in range(2):
            kt_ref[2 * m + tile] = k_ref[2 * m + tile].T
            vt_ref[2 * m + tile] = v_ref[2 * m + tile].T
        return 0

    def attend(m, _):
        att_t[0:64, :] = jnp.zeros((64, rows), BF16)
        for j in range(3):
            tile = 2 * m + j // 2
            head = 3 * m + j
            keys = jnp.concatenate([k_ref[tile], keybias_ref[...]], axis=1)
            queries = jnp.concatenate([qm_ref[head], ones_lane], axis=1)
            scores = dot(keys, queries, (1, 1))
            weights = jnp.exp(scores - jnp.max(scores, axis=0, keepdims=True))
            recip = 1.0 / jnp.sum(weights, axis=0, keepdims=True)
            weights = weights.astype(BF16)
            pl.when(m > 0)(lambda h=head, s=j: probs_copy(h, s).wait())
            probs[j] = weights
            probs_copy(head, j).start()
            side = 64 * (j % 2)
            head_out = dot(vt_ref[tile, side : side + 64, :], weights) * recip
            recip_ref[head] = jnp.broadcast_to(recip, (8, rows))
            headout_ref[head] = head_out
            place = (128, 192, 64)[j]
            att_t[place : place + 64, :] = head_out.astype(BF16)
        att_ref[m] = att_t[...].T
        part = dot(att_ref[m], block_of(blocks, ATT, m, 512, 256), (1, 1))

        @pl.when(m == 0)
        def _():
            total[...] = part

        @pl.when(m > 0)
        def _():
            total[...] += part

        hooks.in_attend(m)
        return 0

    hooks.before_project()
    lax.fori_loop(0, 4, project, 0)
    hooks.before_attend()
    lax.fori_loop(0, 4, attend, 0)
    for j in range(3):
        probs_copy(9 + j, j).wait()

    chunk = 64

    def norm_one(i, _):
        r = pl.ds(pl.multiple_of(i * chunk, chunk), chunk)
        resid = xs[0, r, :].astype(F32) + total[r, :] + vec_ref[0:1, :]
        centered = resid - jnp.mean(resid, axis=1, keepdims=True)
        rstd = lax.rsqrt(jnp.mean(centered * centered, axis=1, keepdims=True) + EPSILON)
        unit = centered * rstd
        n1_ref[r, :] = unit
        rs1_ref[r, :] = rstd
        low[r, :] = (unit * vec_ref[2:3, :] + vec_ref[3:4, :]).astype(BF16)
        return 0

    lax.fori_loop(0, rows // chunk, norm_one, 0)
    n1t_ref[...] = low[...].T
    hooks.before_up()

    def feed(m, _):
        pre = dot(low[...], block_of(blocks, UP, m)) + biases[m, 1:2, :].astype(F32)
        phi = 0.5 * (1.0 + lax.erf(pre * (1.0 / math.sqrt(2.0))))
        acted_ref[m] = (pre * phi).astype(BF16)
        slope_ref[m] = (phi + pre * jnp.exp(-0.5 * pre * pre) * (1.0 / math.sqrt(2.0 * math.pi))).astype(BF16)
        hooks.in_feed(m)
        return 0

    lax.fori_loop(0, 4, feed, 0)
    hooks.before_down()

    def down(m, _):
        part = dot(acted_ref[m], block_of(blocks, DOWN, m), (1, 1))

        @pl.when(m == 0)
        def _():
            total[...] = part

        @pl.when(m > 0)
        def _():
            total[...] += part

        return 0

    lax.fori_loop(0, 4, down, 0)

    def norm_two(i, sums):
        r = pl.ds(pl.multiple_of(i * chunk, chunk), chunk)
        normed = n1_ref[r, :] * vec_ref[2:3, :] + vec_ref[3:4, :]
        resid = normed + total[r, :] + vec_ref[1:2, :]
        centered = resid - jnp.mean(resid, axis=1, keepdims=True)
        rstd = lax.rsqrt(jnp.mean(centered * centered, axis=1, keepdims=True) + EPSILON)
        unit = centered * rstd
        valid = valid_ref[r, :]
        out_ref[r, :] = (valid * (unit * vec_ref[4:5, :] + vec_ref[5:6, :])).astype(BF16)
        grad = valid * cot_ref[r, :].astype(F32)
        scaled = grad * vec_ref[4:5, :]
        grad_in = (
            scaled
            - jnp.mean(scaled, axis=1, keepdims=True)
            - unit * jnp.mean(scaled * unit, axis=1, keepdims=True)
        ) * rstd
        g2_ref[r, :] = grad_in
        gb2_ref[r, :] = grad_in.astype(BF16)
        return (
            sums[0] + jnp.sum(grad_in, axis=0, keepdims=True),
            sums[1] + jnp.sum(grad * unit, axis=0, keepdims=True),
            sums[2] + jnp.sum(grad, axis=0, keepdims=True),
        )

    zero = jnp.zeros((1, 768), F32)
    sums = lax.fori_loop(0, rows // chunk, norm_two, (zero, zero, zero))
    sums_ref[...] = jnp.concatenate([*sums, jnp.zeros((5, 768), F32)], axis=0)
    gb2t_ref[...] = gb2_ref[...].T


class NoHooks:
    def before_project(self):
        pass

    def before_attend(self):
        pass

    def in_attend(self, m):
        pass

    def before_up(self):
        pass

    def in_feed(self, m):
        pass

    def before_down(self):
        pass


N_FORWARD_OUTS = 18


def forward_linked(pack_ref, bias_ref, x_ref, *refs):
    keybias, valid, cot, vec = refs[:4]
    blocks_hbm, probs_hbm, *outs = refs[4 : 4 + 2 + N_FORWARD_OUTS - 1]
    scratch = refs[4 + 2 + N_FORWARD_OUTS - 1 :]
    blocks, biases, xs, k_ref, vt_ref, att_t, probs, probs_sem, total, low = scratch[:10]
    z_send, z_recv, p_send, p_recv, x_send, x_recv, keep_sem = scratch[10:]
    at = Place()
    at.greet(False)
    gather = Gather(at, blocks, biases, z_send, z_recv, p_send, p_recv)
    for kind in range(3):
        blocks[kind, at.z, at.y, at.x, at.c] = pack_ref[kind]
    biases[at.z] = bias_ref[...]
    xs[0] = x_ref[...]
    swap = remote(x_ref, xs.at[1], x_send, x_recv, at.mate)
    gather.z_step(ATT, 0)
    gather.z_step(3, 0)
    gather.z_step(ATT, 1)
    gather.z_step(3, 1)
    gather.z_step(ATT, 2)
    gather.z_step(3, 2)
    gather.z_step(ATT, 3)
    gather.z_step(3, 3)
    gather.first(ATT)
    swap.start()
    gather.z_step(UP, 0)
    gather.second(ATT)
    gather.z_step(UP, 1)
    gather.z_step(UP, 2)
    gather.z_step(UP, 3)
    gather.first(UP)
    gather.z_step(DOWN, 0)
    gather.third(ATT)
    gather.second(UP)
    gather.z_step(DOWN, 1)
    gather.z_step(DOWN, 2)
    gather.z_step(DOWN, 3)
    gather.first(DOWN)
    gather.last(ATT)
    swap.wait()
    gather.third(UP)
    gather.second(DOWN)
    gather.last(UP)
    gather.third(DOWN)
    gather.last(DOWN)
    keep = pltpu.make_async_copy(blocks, blocks_hbm, keep_sem)
    keep.start()
    forward_compute(
        blocks, biases, xs, keybias, valid, cot, vec, probs_hbm, *outs,
        k_ref, vt_ref, att_t, probs, probs_sem, total, low, NoHooks(),
    )
    keep.wait()
    gather.drain()


def forward_alone(blocks_in, biases, xs, *refs):
    keybias, valid, cot, vec = refs[:4]
    probs_hbm, *outs = refs[4 : 4 + 1 + N_FORWARD_OUTS - 1]
    scratch = refs[4 + 1 + N_FORWARD_OUTS - 1 :]
    blocks, k_ref, vt_ref, att_t, probs, probs_sem, total, low, keep_sem = scratch
    load = pltpu.make_async_copy(blocks_in, blocks, keep_sem)
    load.start()
    load.wait()
    forward_compute(
        blocks, biases, xs, keybias, valid, cot, vec, probs_hbm, *outs,
        k_ref, vt_ref, att_t, probs, probs_sem, total, low, NoHooks(),
    )


BLOCKS = (3, 4, 2, 2, 2, 96, 768)


def forward_outs(rows):
    def of(shape, dtype):
        return jax.ShapeDtypeStruct(shape, dtype)

    return [
        of((12, LEN, rows), BF16),
        of((rows, 768), BF16),
        of((12, 8, rows), F32),
        of((12, 64, rows), F32),
        of((2, 768, rows), BF16),
        of((12, rows, 128), BF16),
        of((8, 128, LEN), BF16),
        of((8, LEN, 128), BF16),
        of((4, rows, 256), BF16),
        of((4, rows, 768), BF16),
        of((4, rows, 768), BF16),
        of((768, rows), BF16),
        of((rows, 768), F32),
        of((rows, 1), F32),
        of((rows, 768), BF16),
        of((768, rows), BF16),
        of((rows, 768), F32),
        of((8, 768), F32),
    ]


def forward_scratch(rows):
    return [
        pltpu.VMEM((8, LEN, 128), BF16),
        pltpu.VMEM((8, 128, LEN), BF16),
        pltpu.VMEM((256, rows), BF16),
        pltpu.VMEM((3, LEN, rows), BF16),
        pltpu.SemaphoreType.DMA((3,)),
        pltpu.VMEM((rows, 768), F32),
        pltpu.VMEM((rows, 768), BF16),
    ]


def run_forward(linked, weights, bias, x, keybias, valid, cot, vec):
    rows = valid.shape[0]
    outs = forward_outs(rows)
    if linked:
        return pl.pallas_call(
            forward_linked,
            name="forward",
            out_shape=[jax.ShapeDtypeStruct(BLOCKS, BF16), *outs],
            in_specs=[vmem()] * 7,
            out_specs=[hbm(), hbm()] + [vmem()] * (N_FORWARD_OUTS - 1),
            scratch_shapes=[
                pltpu.VMEM(BLOCKS, BF16),
                pltpu.VMEM((4, 16, 768), BF16),
                pltpu.VMEM((2, rows, 768), BF16),
                *forward_scratch(rows),
                pltpu.SemaphoreType.DMA((4, 2, 3)),
                pltpu.SemaphoreType.DMA((4, 4)),
                pltpu.SemaphoreType.DMA((3, 9)),
                pltpu.SemaphoreType.DMA((3, 9)),
                pltpu.SemaphoreType.DMA,
                pltpu.SemaphoreType.DMA,
                pltpu.SemaphoreType.DMA,
            ],
            compiler_params=pltpu.CompilerParams(
                collective_id=0, has_side_effects=True, vmem_limit_bytes=VMEM_LIMIT
            ),
        )(weights, bias, x, keybias, valid, cot, vec)
    outs = pl.pallas_call(
        forward_alone,
        name="forward",
        out_shape=outs,
        in_specs=[hbm()] + [vmem()] * 6,
        out_specs=[hbm()] + [vmem()] * (N_FORWARD_OUTS - 1),
        scratch_shapes=[
            pltpu.VMEM(BLOCKS, BF16),
            *forward_scratch(rows),
            pltpu.SemaphoreType.DMA,
        ],
        compiler_params=pltpu.CompilerParams(vmem_limit_bytes=VMEM_LIMIT),
    )(weights, bias, x, keybias, valid, cot, vec)
    return [weights, *outs]


class Scatter:
    def __init__(self, at, grads, core_in, first_in, second_in, z_in, out, send, recv, z_send, z_recv):
        self.at, self.grads, self.out = at, grads, out
        self.core_in, self.first_in, self.second_in, self.z_in = core_in, first_in, second_in, z_in
        self.send, self.recv, self.z_send, self.z_recv = send, recv, z_send, z_recv

    def copy(self, kind, m, which):
        at, grads = self.at, self.grads.at[kind, m]
        x, y, c = at.x, at.y, at.c
        low, high = pl.ds(0, 48), pl.ds(48, 48)
        src, dst, device = {
            0: lambda: (grads.at[:, :, 1 - c], self.core_in.at[kind, m], at.core),
            1: lambda: (grads.at[:, 1 - x, c, low], self.first_in.at[kind, m, 0], at.across_x),
            2: lambda: (grads.at[1 - y, :, c, high], self.first_in.at[kind, m, 1], at.across_y),
            3: lambda: (grads.at[1 - y, x, c, low], self.second_in.at[kind, m, 0], at.across_y),
            4: lambda: (grads.at[y, 1 - x, c, high], self.second_in.at[kind, m, 1], at.across_x),
        }[which]()
        return remote(src, dst, self.send.at[kind, m, which], self.recv.at[kind, m, which], device)

    def add(self, ref, got):
        ref[...] = (ref[...].astype(F32) + got[...].astype(F32)).astype(BF16)

    def begin(self, kind, m):
        self.copy(kind, m, 0).start()

    def first(self, kind, m):
        at, grads = self.at, self.grads.at[kind, m]
        self.copy(kind, m, 0).wait_recv()
        for y in range(2):
            for x in range(2):
                self.add(grads.at[y, x, at.c], self.core_in.at[kind, m, y, x])
        self.copy(kind, m, 1).start()
        self.copy(kind, m, 2).start()

    def second(self, kind, m):
        at, grads = self.at, self.grads.at[kind, m]
        low, high = pl.ds(0, 48), pl.ds(48, 48)
        self.copy(kind, m, 1).wait_recv()
        for y in range(2):
            self.add(grads.at[y, at.x, at.c, low], self.first_in.at[kind, m, 0, y])
        self.copy(kind, m, 3).start()
        self.copy(kind, m, 2).wait_recv()
        for x in range(2):
            self.add(grads.at[at.y, x, at.c, high], self.first_in.at[kind, m, 1, x])
        self.copy(kind, m, 4).start()

    def third(self, kind, m):
        at = self.at
        grads = self.grads.at[kind, m, at.y, at.x, at.c]
        self.copy(kind, m, 3).wait_recv()
        self.add(grads.at[pl.ds(0, 48)], self.second_in.at[kind, m, 0])
        self.copy(kind, m, 4).wait_recv()
        self.add(grads.at[pl.ds(48, 48)], self.second_in.at[kind, m, 1])

    def z_copy(self, kind, m, direction):
        at = self.at
        src = self.grads.at[kind, m, at.y, at.x, at.c]
        device = at.right if direction == 0 else at.left
        slot = m if direction == 0 else jnp.where(m == at.z - 1, 4, m)
        return remote(src, self.z_in.at[kind, slot], self.z_send.at[kind, m], self.z_recv.at[kind, slot], device)

    def z_landed(self, kind, m, slot, direction):
        at = self.at
        src = self.grads.at[kind, m, at.y, at.x, at.c]
        device = at.right if direction == 0 else at.left
        return remote(src, self.z_in.at[kind, slot], self.z_send.at[kind, m], self.z_recv.at[kind, slot], device)

    def relay(self, kind, m, direction):
        at = self.at
        self.z_landed(kind, m, m, direction).wait_recv()
        self.add(self.grads.at[kind, m, at.y, at.x, at.c], self.z_in.at[kind, m])
        self.z_copy(kind, m, direction).start()

    def z_step(self, kind, step):
        z = self.at.z
        if step == 0:

            @pl.when(z == 0)
            def _():
                for m in (3, 2, 1):
                    self.z_copy(kind, m, 0).start()

            @pl.when(z == 3)
            def _():
                for m in (0, 1, 2):
                    self.z_copy(kind, m, 1).start()

        elif step == 1:

            @pl.when(z == 1)
            def _():
                for m in (3, 2):
                    self.relay(kind, m, 0)

            @pl.when(z == 2)
            def _():
                for m in (0, 1):
                    self.relay(kind, m, 1)

        elif step == 2:
            pl.when(z == 2)(lambda: self.relay(kind, 3, 0))
            pl.when(z == 1)(lambda: self.relay(kind, 0, 1))
        else:
            at = self.at
            self.out[kind] = self.grads[kind, z, at.y, at.x, at.c].astype(F32)

            @pl.when(z > 0)
            def _():
                self.z_landed(kind, z, z, 0).wait_recv()
                self.out[kind] += self.z_in[kind, z].astype(F32)

            @pl.when(z < 3)
            def _():
                self.z_landed(kind, z, 4, 1).wait_recv()
                self.out[kind] += self.z_in[kind, 4].astype(F32)

    def drain(self):
        z = self.at.z
        for kind in range(3):

            def of_index(m, _, kind=kind):
                for which in range(5):
                    self.copy(kind, m, which).wait_send()
                pl.when(m > z)(lambda: self.z_copy(kind, m, 0).wait_send())
                pl.when(m < z)(lambda: self.z_copy(kind, m, 1).wait_send())
                return 0

            lax.fori_loop(0, 4, of_index, 0)


class Totals:
    def __init__(self, at, rows, got, send, recv):
        self.rows, self.got, self.send, self.recv = rows, got, send, recv
        self.partners = (at.core, at.across_x, at.across_y, at.mate, at.far)

    def copy(self, stage):
        return remote(
            self.rows.at[stage], self.got.at[stage], self.send.at[stage], self.recv.at[stage], self.partners[stage]
        )

    def start(self, stage):
        self.copy(stage).start()

    def finish(self, stage):
        self.copy(stage).wait()
        self.rows[stage + 1] = self.rows[stage] + self.got[stage]


def backward_compute(
    blocks_hbm,
    probs_hbm,
    acted_hbm,
    slope_hbm,
    recip_ref,
    headout_ref,
    xt_ref,
    qm_ref,
    kt_ref,
    v_ref,
    att_ref,
    n1t_ref,
    n1_hbm,
    rs1_ref,
    gb2_ref,
    gb2t_ref,
    g2_hbm,
    sums_ref,
    masked_ref,
    vec_ref,
    grads,
    rows_ref,
    weight,
    weight_sem,
    acts,
    acts_sem,
    probs,
    probs_sem,
    gb1,
    gb1t,
    grad_one,
    parts,
    g2_ref,
    state_sem,
    hooks,
):
    rows = g2_ref.shape[0]
    g2_load = pltpu.make_async_copy(g2_hbm, g2_ref, state_sem.at[0])
    n1_load = pltpu.make_async_copy(n1_hbm, grad_one, state_sem.at[1])

    def weight_load(kind, m, slot):
        return pltpu.make_async_copy(blocks_hbm.at[kind, m], weight.at[slot], weight_sem.at[slot])

    def act_loads(m, slot):
        return (
            pltpu.make_async_copy(acted_hbm.at[m], acts.at[slot, 0], acts_sem.at[slot, 0]),
            pltpu.make_async_copy(slope_hbm.at[m], acts.at[slot, 1], acts_sem.at[slot, 1]),
        )

    def probs_load(head, slot):
        return pltpu.make_async_copy(probs_hbm.at[head], probs.at[slot], probs_sem.at[slot])

    def feed_loads(m, slot):
        return (weight_load(DOWN, m, 2 * slot), weight_load(UP, m, 2 * slot + 1), *act_loads(m, slot))

    def begin(copies):
        for copy in copies:
            copy.start()

    def finish(copies):
        for copy in copies:
            copy.wait()

    def block(slot, low=0, width=768):
        return weight[slot, :, :, :, :, pl.ds(low, width)].reshape(768, width)

    def put(kind, m, value, low=0):
        width = value.shape[1]
        grads[kind, m, :, :, :, :, pl.ds(low, width)] = value.astype(BF16).reshape(2, 2, 2, 96, width)

    begin(feed_loads(0, 0))
    begin((g2_load, n1_load))
    for j in range(3):
        probs_load(j, j).start()
    parts[...] = jnp.zeros_like(parts)
    finish((g2_load, n1_load))

    def feed(m, _):
        slot = lax.rem(m, 2)
        pl.when(m < 3)(lambda: begin(feed_loads(m + 1, 1 - slot)))
        finish(feed_loads(m, slot))
        grad_acted = dot(gb2_ref[...], block(2 * slot))
        grad_pre = (grad_acted * acts[slot, 1].astype(F32)).astype(BF16)
        acts[slot, 1] = grad_pre
        parts[m, 0:1, :] = jnp.sum(grad_pre.astype(F32), axis=0, keepdims=True)
        put(DOWN, m, dot(gb2t_ref[...], acts[slot, 0]))
        hooks.down_ready(m)
        put(UP, m, dot(n1t_ref[...], acts[slot, 1]))
        hooks.up_ready(m)
        g2_ref[...] += dot(acts[slot, 1], block(2 * slot + 1), (1, 1))
        return 0

    lax.fori_loop(0, 4, feed, 0)
    for m in range(4):
        weight_load(ATT, m, m).start()

    chunk = 64

    def norm_back(i, sums):
        r = pl.ds(pl.multiple_of(i * chunk, chunk), chunk)
        grad = g2_ref[r, :]
        unit = grad_one[r, :]
        scaled = grad * vec_ref[2:3, :]
        grad_in = (
            scaled
            - jnp.mean(scaled, axis=1, keepdims=True)
            - unit * jnp.mean(scaled * unit, axis=1, keepdims=True)
        ) * rs1_ref[r, :]
        grad_one[r, :] = grad_in
        gb1[r, :] = grad_in.astype(BF16)
        return (
            sums[0] + jnp.sum(grad_in, axis=0, keepdims=True),
            sums[1] + jnp.sum(grad * unit, axis=0, keepdims=True),
            sums[2] + jnp.sum(grad, axis=0, keepdims=True),
        )

    zero = jnp.zeros((1, 768), F32)
    sums = lax.fori_loop(0, rows // chunk, norm_back, (zero, zero, zero))
    rows_ref[0, 0:1, :] = sums[0]
    rows_ref[0, 1:2, :] = sums_ref[0:1, :]
    rows_ref[0, 2:3, :] = sums[1]
    rows_ref[0, 3:4, :] = sums[2]
    rows_ref[0, 4:5, :] = sums_ref[1:2, :]
    rows_ref[0, 5:6, :] = sums_ref[2:3, :]
    gb1t[...] = gb1[...].T
    g2_ref[...] = jnp.zeros_like(g2_ref)

    def attend_back(m, _):
        weight_load(ATT, m, m).wait()
        w_out = block(m, 512, 256)
        grad_att_t = dot(gb1[...], w_out).T
        zeros = jnp.zeros((64, rows), BF16)
        sides = []
        for j in range(3):
            place = (128, 192, 64)[j]
            scaled = (grad_att_t[place : place + 64, :] * recip_ref[3 * m + j, 0:1, :]).astype(BF16)
            sides.append(scaled)
        wide = [
            jnp.concatenate([sides[0], zeros], axis=0),
            jnp.concatenate([zeros, sides[1]], axis=0),
            jnp.concatenate([sides[2], zeros], axis=0),
        ]
        dk, dv, dq = [None, None], [None, None], [None, None]
        for j in range(3):
            t = j // 2
            tile, head = 2 * m + t, 3 * m + j
            shift = jnp.sum(sides[j].astype(F32) * headout_ref[head], axis=0, keepdims=True)
            probs_load(head, j).wait()
            weights = probs[j]
            grad_weights = dot(v_ref[tile], wide[j])
            grad_scores = (weights.astype(F32) * (grad_weights - shift)).astype(BF16)
            grad_v = dot(weights, wide[j].T)
            pl.when(m < 3)(lambda h=head, s=j: probs_load(h + 3, s).start())
            grad_k = dot(grad_scores, qm_ref[head])
            half = 64 * (j % 2) if j < 2 else 64
            grad_q = dot(kt_ref[tile, half : half + 64, :], grad_scores) * SCALE
            dk[t] = grad_k if dk[t] is None else dk[t] + grad_k
            dv[t] = grad_v if dv[t] is None else dv[t] + grad_v
            dq[t] = grad_q if dq[t] is None else jnp.concatenate([dq[t], grad_q], axis=0)
        dq_pair = dq[0].T.astype(BF16)
        dq_single = jnp.concatenate([dq[1], jnp.zeros((64, rows), F32)], axis=0).T.astype(BF16)
        dk = [d.astype(BF16) for d in dk]
        dv = [d.astype(BF16) for d in dv]
        own = acts.at[0, 0, :, pl.ds(0, PROJ)]
        own[:, 0:128] = dq_pair
        own[:, 128:256] = dk[0][:rows]
        own[:, 256:384] = dv[0][:rows]
        own[:, 384:512] = dq_single + dk[1][:rows]
        own[:, 512:640] = dv[1][:rows]
        other = acts.at[0, 1, :, pl.ds(0, PROJ)]
        other[:, 128:256] = dk[0][rows:]
        other[:, 256:384] = dv[0][rows:]
        other[:, 384:512] = dk[1][rows:]
        other[:, 512:640] = dv[1][rows:]
        wide_sum = jnp.sum(own[...].astype(F32), axis=0, keepdims=True)
        narrow_sum = jnp.sum(other[:, 128:640].astype(F32), axis=0, keepdims=True)
        parts[4 + m, 0:1, 0:128] = wide_sum[:, :128]
        parts[4 + m, 0:1, 128:640] = wide_sum[:, 128:] + narrow_sum
        grad_proj = dot(xt_ref[0], own[...])
        grad_other = dot(xt_ref[1], other[:, 128:640])
        grad_out_w = dot(gb1t[...], att_ref[m])
        put(ATT, m, grad_proj[:, :128], 0)
        put(ATT, m, grad_proj[:, 128:512] + grad_other[:, :384], 128)
        put(ATT, m, grad_proj[:, 512:] + grad_other[:, 384:] + grad_out_w[:, :128], 512)
        put(ATT, m, grad_out_w[:, 128:], 640)
        hooks.att_ready(m)
        grad_one[...] += dot(own[...], block(m, 0, PROJ), (1, 1))
        g2_ref[...] += dot(other[:, 128:640], block(m, 128, 512), (1, 1))
        return 0

    lax.fori_loop(0, 4, attend_back, 0)

    def fill(i, total):
        r = pl.ds(pl.multiple_of(i * chunk, chunk), chunk)
        other = g2_ref[r, :]
        gb1[r, :] = other.astype(BF16)
        return total + jnp.sum(
            grad_one[r, :] * masked_ref[0, r, :] + other * masked_ref[1, r, :], axis=0, keepdims=True
        )

    rows_ref[0, 6:7, :] = lax.fori_loop(0, rows // chunk, fill, zero)
    rows_ref[0, 7:8, :] = zero
    for row in range(8):
        rows_ref[0, 8 + row : 9 + row, :] = parts[row, 0:1, :]


def finish_frames(grad_one, got, masked_ref, frames_ref):
    chunk = 64

    def body(i, _):
        r = pl.ds(pl.multiple_of(i * chunk, chunk), chunk)
        total = grad_one[r, :] + got[r, :].astype(F32)
        frames_ref[r, :] = jnp.where(masked_ref[0, r, :] > 0, 0.0, total).astype(BF16)
        return 0

    lax.fori_loop(0, grad_one.shape[0] // chunk, body, 0)


class NoScatter:
    def down_ready(self, m):
        pass

    def up_ready(self, m):
        pass

    def att_ready(self, m):
        pass


N_BACKWARD_INS = 20


def backward_linked(*refs):
    ins = refs[:N_BACKWARD_INS]
    out_ref, rows_out, frames_ref = refs[N_BACKWARD_INS : N_BACKWARD_INS + 3]
    scratch = refs[N_BACKWARD_INS + 3 :]
    grads, rows_ref, weight, weight_sem, acts, acts_sem, probs, probs_sem = scratch[:8]
    gb1, gb1t, grad_one, parts, g2, state_sem = scratch[8:14]
    core_in, first_in, second_in, z_in, rows_in, mate_in = scratch[14:20]
    send, recv, z_send, z_recv, t_send, t_recv, m_send, m_recv = scratch[20:]
    at = Place()
    at.greet(True)
    scatter = Scatter(at, grads, core_in, first_in, second_in, z_in, out_ref, send, recv, z_send, z_recv)
    totals = Totals(at, rows_ref, rows_in, t_send, t_recv)
    backward_compute(
        *ins, grads, rows_ref, weight, weight_sem, acts, acts_sem, probs, probs_sem,
        gb1, gb1t, grad_one, parts, g2, state_sem, NoScatter(),
    )
    swap = remote(gb1, mate_in, m_send, m_recv, at.mate)
    swap.start()
    totals.start(0)

    def each(step, kind):
        def body(m, _):
            step(kind, m)
            return 0

        lax.fori_loop(0, 4, body, 0)

    for kind in range(3):
        each(scatter.begin, kind)
    for kind in range(3):
        each(scatter.first, kind)
    for kind in range(3):
        each(scatter.second, kind)
    for kind in range(3):
        each(scatter.third, kind)
        scatter.z_step(kind, 0)
    for step in range(1, 4):
        for kind in range(3):
            scatter.z_step(kind, step)
    for stage in range(5):
        totals.finish(stage)
        if stage < 4:
            totals.start(stage + 1)
    rows_out[...] = rows_ref[5]
    swap.wait()
    finish_frames(grad_one, mate_in, ins[18], frames_ref)
    scatter.drain()


def backward_alone(*refs):
    ins = refs[:N_BACKWARD_INS]
    grads_out, rows_out, mate_out, grad_one_out = refs[N_BACKWARD_INS : N_BACKWARD_INS + 4]
    scratch = refs[N_BACKWARD_INS + 4 :]
    grads, rows_ref, weight, weight_sem, acts, acts_sem, probs, probs_sem = scratch[:8]
    gb1, gb1t, grad_one, parts, g2, state_sem, keep_sem = scratch[8:]
    backward_compute(
        *ins, grads, rows_ref, weight, weight_sem, acts, acts_sem, probs, probs_sem,
        gb1, gb1t, grad_one, parts, g2, state_sem, NoScatter(),
    )
    keep = pltpu.make_async_copy(grads, grads_out, keep_sem)
    keep.start()
    rows_out[...] = rows_ref[0]
    mate_out[...] = gb1[...]
    grad_one_out[...] = grad_one[...]
    keep.wait()


def backward_scratch(rows):
    return [
        pltpu.VMEM(BLOCKS, BF16),
        pltpu.VMEM((6, 16, 768), F32),
        pltpu.VMEM((4, *BLOCKS[2:]), BF16),
        pltpu.SemaphoreType.DMA((4,)),
        pltpu.VMEM((2, 2, rows, 768), BF16),
        pltpu.SemaphoreType.DMA((2, 2)),
        pltpu.VMEM((3, LEN, rows), BF16),
        pltpu.SemaphoreType.DMA((3,)),
        pltpu.VMEM((rows, 768), BF16),
        pltpu.VMEM((768, rows), BF16),
        pltpu.VMEM((rows, 768), F32),
        pltpu.VMEM((8, 8, 768), F32),
        pltpu.VMEM((rows, 768), F32),
        pltpu.SemaphoreType.DMA((2,)),
    ]


def run_backward(linked, saved, masked, vec):
    blocks, probs, _, recip, headout, xt, qm, kt, v, att, acted, slope, n1t, n1, rs1, gb2, gb2t, g2, sums = saved
    rows = gb2.shape[0]
    ins = (
        blocks, probs, acted, slope, recip, headout, xt, qm, kt, v, att, n1t, n1, rs1, gb2, gb2t, g2, sums, masked, vec
    )
    in_specs = [hbm() if i in (0, 1, 2, 3, 12, 16) else vmem() for i in range(20)]
    if linked:
        return pl.pallas_call(
            backward_linked,
            name="backward",
            out_shape=[
                jax.ShapeDtypeStruct((3, 96, 768), F32),
                jax.ShapeDtypeStruct((16, 768), F32),
                jax.ShapeDtypeStruct((rows, 768), BF16),
            ],
            in_specs=in_specs,
            out_specs=[vmem()] * 3,
            scratch_shapes=[
                *backward_scratch(rows),
                pltpu.VMEM((3, 4, 2, 2, 96, 768), BF16),
                pltpu.VMEM((3, 4, 2, 2, 48, 768), BF16),
                pltpu.VMEM((3, 4, 2, 48, 768), BF16),
                pltpu.VMEM((3, 5, 96, 768), BF16),
                pltpu.VMEM((5, 16, 768), F32),
                pltpu.VMEM((rows, 768), BF16),
                pltpu.SemaphoreType.DMA((3, 4, 5)),
                pltpu.SemaphoreType.DMA((3, 4, 5)),
                pltpu.SemaphoreType.DMA((3, 4)),
                pltpu.SemaphoreType.DMA((3, 5)),
                pltpu.SemaphoreType.DMA((5,)),
                pltpu.SemaphoreType.DMA((5,)),
                pltpu.SemaphoreType.DMA,
                pltpu.SemaphoreType.DMA,
            ],
            compiler_params=pltpu.CompilerParams(
                collective_id=1, has_side_effects=True, vmem_limit_bytes=VMEM_LIMIT
            ),
        )(*ins)
    return pl.pallas_call(
        backward_alone,
        name="backward",
        out_shape=[
            jax.ShapeDtypeStruct(BLOCKS, BF16),
            jax.ShapeDtypeStruct((16, 768), F32),
            jax.ShapeDtypeStruct((rows, 768), BF16),
            jax.ShapeDtypeStruct((rows, 768), F32),
        ],
        in_specs=in_specs,
        out_specs=[hbm()] + [vmem()] * 3,
        scratch_shapes=[*backward_scratch(rows), pltpu.SemaphoreType.DMA],
        compiler_params=pltpu.CompilerParams(vmem_limit_bytes=VMEM_LIMIT),
    )(*ins)


def shards(
    linked,
    frames,
    lengths,
    span_starts,
    cotangent,
    query_weight,
    key_weight,
    value_weight,
    out_weight,
    up_weight,
    down_weight,
    query_bias,
    value_bias,
    up_bias,
    out_bias,
    down_bias,
    first_gain,
    first_shift,
    second_gain,
    second_shift,
    mask_vector,
):
    rows = frames.shape[0]
    dims = query_weight.shape[0]
    z = lax.axis_index("mp")
    clip = z // 2
    half = z % 2
    length = lax.dynamic_index_in_dim(lengths, clip, keepdims=False)
    starts = lax.dynamic_index_in_dim(span_starts, clip, keepdims=False)
    slots = (jnp.arange(LEN, dtype=jnp.int32) + half * rows) % LEN
    valid = slots < length
    masked = jnp.any((slots[:, None] >= starts[None, :]) & (slots[:, None] < starts[None, :] + SPAN), axis=1)
    keybias = jnp.where(
        (jnp.arange(128) == 0)[None, :] & ~valid[:, None], jnp.float32(NEGATIVE), 0.0
    ).astype(BF16)
    valid_rows = valid[:rows].astype(F32)[:, None]
    masked_rows = masked.astype(F32).reshape(2, rows, 1)
    x = jnp.where(masked[:rows, None], mask_vector[None, :], frames)
    out_t = out_weight.T
    pair, single = 2 * HEAD_DIM, 3 * HEAD_DIM
    pack = jnp.stack(
        [
            jnp.concatenate(
                [
                    query_weight[:, :pair], key_weight[:, :pair], value_weight[:, :pair],
                    query_weight[:, pair:], key_weight[:, pair:], value_weight[:, pair:],
                    out_t[:, pair:], out_t[:, :pair],
                ],
                axis=1,
            ),
            up_weight,
            down_weight.T,
        ]
    )
    q_shift, v_shift = query_bias.reshape(-1), value_bias.reshape(-1)
    blank = jnp.zeros((pair,), BF16)
    short = blank[:HEAD_DIM]
    bias = jnp.stack(
        [
            jnp.concatenate([q_shift[:pair], blank, v_shift[:pair], q_shift[pair:], short, v_shift[pair:], short, blank]),
            up_bias.reshape(-1),
        ]
    )
    bias = jnp.pad(bias, ((0, 14), (0, 0)))
    vec = jnp.stack([out_bias, down_bias, first_gain, first_shift, second_gain, second_shift]).astype(F32)
    vec = jnp.pad(vec, ((0, 2), (0, 0)))
    if linked:
        saved = run_forward(True, pack, bias, x, keybias, valid_rows, cotangent, vec)
        grads, totals, grad_frames = run_backward(True, saved, masked_rows, vec)
    else:
        mates = [(0, 1), (1, 0), (2, 3), (3, 2)]
        blocks = lax.all_gather(lax.all_gather(pack, "dp", axis=1, tiled=True), "mp", axis=1)
        biases = lax.all_gather(bias, "mp", axis=0)
        both = jnp.stack([x, lax.ppermute(x, "mp", mates)])
        saved = run_forward(False, blocks.reshape(BLOCKS), biases, both, keybias, valid_rows, cotangent, vec)
        grads, totals, mate, grad_one = run_backward(False, saved, masked_rows, vec)
        grads = grads.reshape(3, 4, 768, 768).astype(F32)
        grads = lax.psum_scatter(grads, "mp", scatter_dimension=1, tiled=False)
        grads = lax.psum_scatter(grads, "dp", scatter_dimension=1, tiled=True)
        totals = lax.psum(totals, ("dp", "mp"))
        grad_frames = grad_one + lax.ppermute(mate, "mp", mates).astype(F32)
        grad_frames = jnp.where(masked[:rows, None], 0.0, grad_frames).astype(BF16)
    out_frames = saved[2]
    att, grad_up, grad_down = grads[0], grads[1], grads[2].T
    grad_query = jnp.concatenate([att[:, 0:128], att[:, 384:448]], axis=1)
    grad_key = jnp.concatenate([att[:, 128:256], att[:, 448:512]], axis=1)
    grad_value = jnp.concatenate([att[:, 256:384], att[:, 512:576]], axis=1)
    grad_out = jnp.concatenate([att[:, 640:768], att[:, 576:640]], axis=1).T
    dp, n_dp = lax.axis_index("dp"), 768 // dims
    part = 768 // (n_dp * 4)
    row_parts = lax.dynamic_slice(totals, (0, (dp * 4 + z) * part), (7, part))
    head_row = lax.dynamic_slice(totals, (12 + z, 0), (1, 768))[0]
    q_row = jnp.concatenate([head_row[0:128], head_row[384:448]]).reshape(3, HEAD_DIM)
    v_row = jnp.concatenate([head_row[256:384], head_row[512:576]]).reshape(3, HEAD_DIM)
    up_row = lax.dynamic_slice(totals, (8 + z, 0), (1, 768)).reshape(6, 128)
    step = HEAD_DIM // n_dp
    grad_query_bias = lax.dynamic_slice(q_row, (0, dp * step), (3, step))
    grad_value_bias = lax.dynamic_slice(v_row, (0, dp * step), (3, step))
    grad_up_bias = lax.dynamic_slice(up_row, (0, dp * 2 * step), (6, 2 * step))
    return (
        out_frames,
        grad_frames,
        grad_query,
        grad_key,
        grad_value,
        grad_out,
        grad_up,
        grad_down,
        grad_query_bias,
        grad_value_bias,
        grad_up_bias,
        *(row_parts[i] for i in range(7)),
    )


def solution(mesh):
    linked = mesh.shape["dp"] == 8 and mesh.shape["mp"] == 4
    split = P(("dp", "mp"))
    return jax.shard_map(
        functools.partial(shards, linked),
        mesh=mesh,
        in_specs=(
            P(("dp", "mp"), None),
            P("dp"),
            P("dp", None),
            P(("dp", "mp"), None),
            P("dp", "mp"),
            P("dp", "mp"),
            P("dp", "mp"),
            P("mp", "dp"),
            P("dp", "mp"),
            P("mp", "dp"),
            P("mp", None),
            P("mp", None),
            P("mp", None),
            *([P()] * 7),
        ),
        out_specs=(
            P(("dp", "mp"), None),
            P(("dp", "mp"), None),
            P("dp", "mp"),
            P("dp", "mp"),
            P("dp", "mp"),
            P("mp", "dp"),
            P("dp", "mp"),
            P("mp", "dp"),
            P("mp", "dp"),
            P("mp", "dp"),
            P("mp", "dp"),
            *([split] * 7),
        ),
        check_vma=False,
    )
```

time: 1200 us -> 320 us (0.27)
  waiting for transfers between devices: 676 us -> 0 us
  Pallas kernels: 0 us -> 283 us
  matrix products: 216 us -> 0 us
  blocking collectives: 128 us -> 0 us
  local copies, waits for them, and re-layouts: 94.9 us -> 21.6 us
  other arithmetic: 59.8 us -> 9.14 us
  between operations: 18.2 us -> 0.93 us
    reduce_scatter x8 -> x0, waiting for transfers between devices: 304 us -> none  [the longest x2 122 us: run_forward(): lax.psum_scatter(jnp.dot(piece, down_full, preferred_element_type=jnp.flo...]
    pallas_call x0 -> x2, Pallas kernels: none -> 283 us  [the longest x1 160 us: run_backward(): pl.pallas_call(backward_linked, name='backward', out_shape=[jax.ShapeDtyp...]
    all_gather x10 -> x0, waiting for transfers between devices: 250 us -> none  [the longest x2 78.8 us: run_forward(): ffn_inputs = lax.all_gather(normed_low, 'mp', axis=0, tiled=True)]
    dot_general x68 -> x0, matrix products: 212 us -> none  [the longest x12 42.4 us: attend_block(): attended = jnp.dot(attention, values, preferred_element_type=jnp.float32)]
    unnamed x28 -> x0, waiting for transfers between devices: 121 us -> none
    all_gather x8 -> x0, blocking collectives: 74.8 us -> none  [the longest x2 19.4 us: run_forward(): lax.all_gather(weight_set[3], 'dp', axis=1, tiled=True)]
    unnamed x2 -> x0, blocking collectives: 52.9 us -> none
    reduce_sum x24 -> x0, other arithmetic: 32.4 us -> none  [the longest x12 10.9 us: attend_block(): row_total = jnp.sum(shifted, axis=1, keepdims=True)]
  transfers between devices with their start and end apart: 23 -> 0, of which waited for: 17 -> 0; matrix products, arithmetic and copies ran while one was open for 20% -> 0% of each run, Pallas kernels for 0% -> 0%
where the time goes in v1:
time: 320 us; the launch traced here: 314 us
  Pallas kernels  283 us (88%)
  local copies, waits for them, and re-layouts  21.6 us (7%)
  other arithmetic  9.14 us (3%)
    pallas_call x1, Pallas kernels, run_backward(): pl.pallas_call(backward_linked, name='backward', out_shape=[jax.ShapeDtyp...  160 us
    pallas_call x1, Pallas kernels, run_forward(): pl.pallas_call(forward_linked, name='forward', out_shape=[jax.ShapeDtypeS...  123 us

profile of v1, /device:TPU:16, one launch (start us, length us, event | category | flops | bytes accessed | tf_op | source)
XLA Modules:
  0.0 314.4 jit_solution(8560454475581111575)
XLA Ops:
  0.7 0.0 copy-start
  0.7 0.0 copy-start.9
  0.7 0.8 slice.135
  1.5 0.7 slice.136
  2.3 0.7 slice.137
  3.0 0.7 slice.138
  3.8 0.7 slice.139
  4.5 0.7 slice.140
  5.2 0.9 copy.44
  6.2 0.1 concatenate.24
  6.3 1.8 pad_maximum_fusion.pack_ref
  8.1 0.7 copy.50
  8.7 0.7 slice.143
  9.4 0.1 slice.144
  9.5 0.7 slice.145
  10.2 0.1 slice.146
  10.3 0.7 slice_bitcast_fusion.10
  11.0 0.1 concatenate.25
  11.1 0.6 fusion.2.bias_ref
  11.7 0.7 fusion.8
  12.4 0.2 and_reduce_fusion
  12.6 1.7 broadcast_select_fusion.x_ref
  14.3 0.6 dynamic_slice.27
  14.9 0.7 broadcast_compare_fusion
  15.5 0.9 select_convert_fusion.refs_0_
  16.5 0.9 copy.45.refs_1_
  17.5 0.6 pad_convert_fusion.refs_3_.refs_19_
  18.1 122.7 %forward.1 = (bf16[3,4,2,2,2,96,768]{6,5,4,3,2,1,0:T(8,128)(2,1)}, bf16[12,1024,512]{2,1,0:T(8,128)(2,1)}, bf16[512,768]{1,0:T(8,128)(2,1)}, f32[12,8,512]{2,1,0...) custom-call(bf16[3,96,768]{2,1,0:T(8,128)(2,1)} %pad_maximum_fusion., ...), custom_call_target="tpu_custom_call" | custom-call | tf_op jit(solution)/shard_map/forward/pallas_call | solution.py:491
  140.9 1.1 reshape.99.refs_18_
  142.0 160.0 %backward.1 = (f32[3,96,768]{2,1,0:T(8,128)}, f32[16,768]{1,0:T(8,128)}, bf16[512,768]{1,0:T(8,128)(2,1)}) custom-call(bf16[3,4,2,2,2,96,768]{6,5,4,3,2,1,0:T(8,128)(2,1)} %get-tuple-element.41.refs_0_, bf16[12,1024,512]{2,1,0:T(8,128)(2,1)} %get-tuple-element.42.refs_1_, bf16[4,512,768]{2,1,0:T(8,128)(2,1)} %get-tuple-element.43.refs_2_, ...), custom_call_target="tpu_custom_call" | custom-call | tf_op jit(solution)/shard_map/backward/pallas_call | solution.py:1005
  302.0 2.1 slice_bitcast_fusion
  304.1 0.1 fusion.11
  304.2 0.6 pad_maximum_fusion.1
  304.8 0.6 pad_maximum_fusion.2
  305.5 0.6 pad_maximum_fusion.3
  306.1 0.7 copy.47
  306.9 0.8 dynamic-slice_bitcast_fusion
  307.6 0.8 dynamic-slice_bitcast_fusion.1
  308.4 0.1 reshape.94
  308.5 0.7 constant_dynamic-slice_fusion.4
  309.1 0.1 reshape.95
  309.2 0.7 constant_dynamic-slice_fusion.3
  309.9 0.8 dynamic-slice_reduce_fusion
  310.6 0.7 constant_dynamic-slice_fusion.2
  311.3 0.8 constant_dynamic-slice_fusion.1
  312.1 0.5 slice_bitcast_fusion.3
  312.6 0.9 copy.53
  313.5 0.9 copy.54
  (39 shorter events, 0.2 us)
Async XLA Ops:
  0.7 11.9 %copy-start = (bf16[512,768]{1,0:T(8,128)(2,1)S(1)}, bf16[512,768]{1,0:T(8,128)(2,1)}, u32[]{:S(2)}) copy-start(bf16[512,768]{1,0:T(8,128)(2,1)} %param.20) | copy-start | bytes 2359300
  0.7 13.6 %copy-start.9 = (s32[2]{0:T(128)S(1)}, s32[2]{0:T(128)}, u32[]{:S(2)}) copy-start(s32[2]{0:T(128)} %param.21) | copy-start | bytes 28
  0.7 16.6 %copy-start.3 = (bf16[768]{0:T(1024)(128)(2,1)S(1)}, bf16[768]{0:T(1024)(128)(2,1)}, u32[]{:S(2)}) copy-start(bf16[768]{0:T(1024)(128)(2,1)} %param.33) | copy-start | bytes 4612
  0.7 16.6 %copy-start.4 = (bf16[768]{0:T(1024)(128)(2,1)S(1)}, bf16[768]{0:T(1024)(128)(2,1)}, u32[]{:S(2)}) copy-start(bf16[768]{0:T(1024)(128)(2,1)} %param.34) | copy-start | bytes 4612
  0.7 16.6 %copy-start.5 = (bf16[768]{0:T(1024)(128)(2,1)S(1)}, bf16[768]{0:T(1024)(128)(2,1)}, u32[]{:S(2)}) copy-start(bf16[768]{0:T(1024)(128)(2,1)} %param.35) | copy-start | bytes 4612
  0.7 16.7 %copy-start.6 = (bf16[768]{0:T(1024)(128)(2,1)S(1)}, bf16[768]{0:T(1024)(128)(2,1)}, u32[]{:S(2)}) copy-start(bf16[768]{0:T(1024)(128)(2,1)} %param.36) | copy-start | bytes 4612
  0.7 16.7 %copy-start.7 = (bf16[768]{0:T(1024)(128)(2,1)S(1)}, bf16[768]{0:T(1024)(128)(2,1)}, u32[]{:S(2)}) copy-start(bf16[768]{0:T(1024)(128)(2,1)} %param.37) | copy-start | bytes 4612
  0.7 16.7 %copy-start.8 = (bf16[768]{0:T(1024)(128)(2,1)S(1)}, bf16[768]{0:T(1024)(128)(2,1)}, u32[]{:S(2)}) copy-start(bf16[768]{0:T(1024)(128)(2,1)} %param.38) | copy-start | bytes 4612
  302.0 10.6 %copy-start.1 = (bf16[512,768]{1,0:T(8,128)(2,1)S(1)}, bf16[512,768]{1,0:T(8,128)(2,1)}, u32[]{:S(2)}) copy-start(bf16[512,768]{1,0:T(8,128)(2,1)} %get-tuple-element.162) | copy-start | bytes 2359300
  304.1 9.4 %copy-start.2 = (bf16[512,768]{1,0:T(8,128)(2,1)S(1)}, bf16[512,768]{1,0:T(8,128)(2,1)}, u32[]{:S(2)}) copy-start(bf16[512,768]{1,0:T(8,128)(2,1)} %get-tuple-element.163) | copy-start | bytes 2359300

commit v2 on v1

--- a/solution.py
+++ b/solution.py
@@ -18,7 +18,7 @@
 F32 = jnp.float32
 BF16 = jnp.bfloat16
 MESH = pl.DeviceIdType.MESH
-VMEM_LIMIT = 62 * 1024 * 1024
+VMEM_LIMIT = 63 * 1024 * 1024
 
 ATT, UP, DOWN = 0, 1, 2
 PROJ = 640
@@ -77,9 +77,10 @@
 
 
 class Gather:
-    def __init__(self, at, blocks, biases, z_send, z_recv, p_send, p_recv):
+    def __init__(self, at, blocks, biases, z_send, z_recv, f_send, f_recv, p_send, p_recv):
         self.at, self.blocks, self.biases = at, blocks, biases
-        self.z_send, self.z_recv, self.p_send, self.p_recv = z_send, z_recv, p_send, p_recv
+        self.z_send, self.z_recv = z_send, z_recv
+        self.f_send, self.f_recv, self.p_send, self.p_recv = f_send, f_recv, p_send, p_recv
 
     def z_copy(self, kind, m, direction, step):
         at = self.at
@@ -95,6 +96,7 @@
         if step == 0:
             pl.when(z < 3)(lambda: self.z_copy(kind, z, 0, 0).start())
             pl.when(z > 0)(lambda: self.z_copy(kind, z, 1, 0).start())
+            self.first(kind, z)
             return
 
         @pl.when(z >= step)
@@ -102,50 +104,65 @@
             self.z_copy(kind, z - step, 0, 0).wait_recv()
             if step < 3:
                 pl.when(z < 3)(lambda: self.z_copy(kind, z - step, 0, step).start())
+            self.first(kind, z - step)
 
         @pl.when(z + step <= 3)
         def _():
             self.z_copy(kind, z + step, 1, 0).wait_recv()
             if step < 3:
                 pl.when(z > 0)(lambda: self.z_copy(kind, z + step, 1, step).start())
+            self.first(kind, z + step)
+
+    def first_copy(self, kind, m, which):
+        at = self.at
+        ref = self.blocks.at[kind, m, at.y, at.x, at.c]
+        ref, device = {
+            0: lambda: (ref.at[pl.ds(0, 48)], at.across_x),
+            1: lambda: (ref.at[pl.ds(48, 48)], at.across_y),
+            2: lambda: (ref, at.core),
+        }[which]()
+        return remote(ref, ref, self.f_send.at[kind, m, which], self.f_recv.at[kind, m, which], device)
+
+    def first(self, kind, m):
+        if kind == 3:
+            return
+        for which in range(3):
+            self.first_copy(kind, m, which).start()
 
     def plane_copy(self, kind, which):
         at, blocks = self.at, self.blocks.at[kind]
         x, y, c = at.x, at.y, at.c
         low, high = pl.ds(0, 48), pl.ds(48, 48)
         ref, device = {
-            0: lambda: (blocks.at[:, y, x, c, low], at.across_x),
-            1: lambda: (blocks.at[:, y, x, c, high], at.across_y),
-            2: lambda: (blocks.at[:, y, :, c, low], at.across_y),
-            3: lambda: (blocks.at[:, :, x, c, high], at.across_x),
-            4: lambda: (blocks.at[:, y, x, c], at.core),
-            5: lambda: (blocks.at[:, y, 1 - x, c, low], at.core),
-            6: lambda: (blocks.at[:, 1 - y, x, c, high], at.core),
-            7: lambda: (blocks.at[:, 1 - y, :, c, low], at.core),
-            8: lambda: (blocks.at[:, :, 1 - x, c, high], at.core),
+            0: lambda: (blocks.at[:, y, :, c, low], at.across_y),
+            1: lambda: (blocks.at[:, :, x, c, high], at.across_x),
+            2: lambda: (blocks.at[:, y, 1 - x, c, low], at.core),
+            3: lambda: (blocks.at[:, 1 - y, x, c, high], at.core),
+            4: lambda: (blocks.at[:, 1 - y, :, c, low], at.core),
+            5: lambda: (blocks.at[:, :, 1 - x, c, high], at.core),
         }[which]()
         return remote(ref, ref, self.p_send.at[kind, which], self.p_recv.at[kind, which], device)
 
-    def first(self, kind):
-        for which in (0, 1, 4):
-            self.plane_copy(kind, which).start()
-
     def second(self, kind):
+        for m in range(4):
+            self.first_copy(kind, m, 0).wait_recv()
+        self.plane_copy(kind, 0).start()
+        for m in range(4):
+            self.first_copy(kind, m, 1).wait_recv()
+        self.plane_copy(kind, 1).start()
+        self.plane_copy(kind, 2).start()
+        self.plane_copy(kind, 3).start()
+
+    def third(self, kind):
         self.plane_copy(kind, 0).wait_recv()
-        self.plane_copy(kind, 2).start()
+        self.plane_copy(kind, 4).start()
+        self.plane_copy(kind, 1).wait_recv()
         self.plane_copy(kind, 5).start()
-        self.plane_copy(kind, 1).wait_recv()
-        self.plane_copy(kind, 3).start()
-        self.plane_copy(kind, 6).start()
-
-    def third(self, kind):
-        self.plane_copy(kind, 2).wait_recv()
-        self.plane_copy(kind, 7).start()
-        self.plane_copy(kind, 3).wait_recv()
-        self.plane_copy(kind, 8).start()
 
     def last(self, kind):
-        for which in range(4, 9):
+        for m in range(4):
+            self.first_copy(kind, m, 2).wait_recv()
+        for which in range(2, 6):
             self.plane_copy(kind, which).wait_recv()
 
     def drain(self):
@@ -159,7 +176,10 @@
                     lambda k=kind, s=step: self.z_copy(k, z + s, 1, s).wait_send()
                 )
         for kind in range(3):
-            for which in range(9):
+            for m in range(4):
+                for which in range(3):
+                    self.first_copy(kind, m, which).wait_send()
+            for which in range(6):
                 self.plane_copy(kind, which).wait_send()
 
 
@@ -372,6 +392,45 @@
         pass
 
 
+class GatherHooks:
+    def __init__(self, gather, blocks_out, keep_sem):
+        self.gather = gather
+        self.keep = [
+            pltpu.make_async_copy(gather.blocks.at[kind], blocks_out.at[kind], keep_sem.at[kind]) for kind in range(3)
+        ]
+
+    def before_project(self):
+        self.gather.last(ATT)
+        self.keep[ATT].start()
+
+    def before_attend(self):
+        self.gather.second(UP)
+        self.gather.z_step(DOWN, 1)
+
+    def in_attend(self, m):
+        gather = self.gather
+        pl.when(m == 0)(lambda: gather.z_step(DOWN, 2))
+        pl.when(m == 1)(lambda: gather.z_step(DOWN, 3))
+        pl.when(m == 3)(lambda: gather.third(UP))
+
+    def before_up(self):
+        self.gather.last(UP)
+        self.keep[UP].start()
+
+    def in_feed(self, m):
+        pl.when(m == 0)(lambda: self.gather.second(DOWN))
+
+    def before_down(self):
+        self.gather.third(DOWN)
+        self.gather.last(DOWN)
+        self.keep[DOWN].start()
+
+    def finish(self):
+        for copy in self.keep:
+            copy.wait()
+        self.gather.drain()
+
+
 N_FORWARD_OUTS = 18
 
 
@@ -380,53 +439,38 @@
     blocks_hbm, probs_hbm, *outs = refs[4 : 4 + 2 + N_FORWARD_OUTS - 1]
     scratch = refs[4 + 2 + N_FORWARD_OUTS - 1 :]
     blocks, biases, xs, k_ref, vt_ref, att_t, probs, probs_sem, total, low = scratch[:10]
-    z_send, z_recv, p_send, p_recv, x_send, x_recv, keep_sem = scratch[10:]
+    z_send, z_recv, f_send, f_recv, p_send, p_recv, x_send, x_recv, keep_sem = scratch[10:]
     at = Place()
     at.greet(False)
-    gather = Gather(at, blocks, biases, z_send, z_recv, p_send, p_recv)
+    gather = Gather(at, blocks, biases, z_send, z_recv, f_send, f_recv, p_send, p_recv)
     for kind in range(3):
         blocks[kind, at.z, at.y, at.x, at.c] = pack_ref[kind]
     biases[at.z] = bias_ref[...]
-    xs[0] = x_ref[...]
     swap = remote(x_ref, xs.at[1], x_send, x_recv, at.mate)
     gather.z_step(ATT, 0)
     gather.z_step(3, 0)
+    xs[0] = x_ref[...]
     gather.z_step(ATT, 1)
     gather.z_step(3, 1)
     gather.z_step(ATT, 2)
     gather.z_step(3, 2)
     gather.z_step(ATT, 3)
     gather.z_step(3, 3)
-    gather.first(ATT)
+    gather.z_step(UP, 0)
     swap.start()
-    gather.z_step(UP, 0)
     gather.second(ATT)
     gather.z_step(UP, 1)
     gather.z_step(UP, 2)
     gather.z_step(UP, 3)
-    gather.first(UP)
+    gather.third(ATT)
     gather.z_step(DOWN, 0)
-    gather.third(ATT)
-    gather.second(UP)
-    gather.z_step(DOWN, 1)
-    gather.z_step(DOWN, 2)
-    gather.z_step(DOWN, 3)
-    gather.first(DOWN)
-    gather.last(ATT)
     swap.wait()
-    gather.third(UP)
-    gather.second(DOWN)
-    gather.last(UP)
-    gather.third(DOWN)
-    gather.last(DOWN)
-    keep = pltpu.make_async_copy(blocks, blocks_hbm, keep_sem)
-    keep.start()
+    hooks = GatherHooks(gather, blocks_hbm, keep_sem)
     forward_compute(
         blocks, biases, xs, keybias, valid, cot, vec, probs_hbm, *outs,
-        k_ref, vt_ref, att_t, probs, probs_sem, total, low, NoHooks(),
+        k_ref, vt_ref, att_t, probs, probs_sem, total, low, hooks,
     )
-    keep.wait()
-    gather.drain()
+    hooks.finish()
 
 
 def forward_alone(blocks_in, biases, xs, *refs):
@@ -501,11 +545,13 @@
                 *forward_scratch(rows),
                 pltpu.SemaphoreType.DMA((4, 2, 3)),
                 pltpu.SemaphoreType.DMA((4, 4)),
-                pltpu.SemaphoreType.DMA((3, 9)),
-                pltpu.SemaphoreType.DMA((3, 9)),
+                pltpu.SemaphoreType.DMA((3, 4, 3)),
+                pltpu.SemaphoreType.DMA((3, 4, 3)),
+                pltpu.SemaphoreType.DMA((3, 6)),
+                pltpu.SemaphoreType.DMA((3, 6)),
                 pltpu.SemaphoreType.DMA,
                 pltpu.SemaphoreType.DMA,
-                pltpu.SemaphoreType.DMA,
+                pltpu.SemaphoreType.DMA((3,)),
             ],
             compiler_params=pltpu.CompilerParams(
                 collective_id=0, has_side_effects=True, vmem_limit_bytes=VMEM_LIMIT
@@ -527,6 +573,12 @@
     return [weights, *outs]
 
 
+def chunk_at(n):
+    if isinstance(n, int):
+        return (2 - n % 2, n // 2) if n < 8 else (0, n - 8)
+    return jnp.where(n < 8, 2 - lax.rem(n, 2), 0), jnp.where(n < 8, n // 2, n - 8)
+
+
 class Scatter:
     def __init__(self, at, grads, core_in, first_in, second_in, z_in, out, send, recv, z_send, z_recv):
         self.at, self.grads, self.out = at, grads, out
@@ -600,48 +652,45 @@
         self.add(self.grads.at[kind, m, at.y, at.x, at.c], self.z_in.at[kind, m])
         self.z_copy(kind, m, direction).start()
 
-    def z_step(self, kind, step):
+    def z_start(self, kind, m):
         z = self.at.z
-        if step == 0:
-
-            @pl.when(z == 0)
-            def _():
-                for m in (3, 2, 1):
-                    self.z_copy(kind, m, 0).start()
-
-            @pl.when(z == 3)
-            def _():
-                for m in (0, 1, 2):
-                    self.z_copy(kind, m, 1).start()
-
-        elif step == 1:
-
-            @pl.when(z == 1)
-            def _():
-                for m in (3, 2):
-                    self.relay(kind, m, 0)
-
-            @pl.when(z == 2)
-            def _():
-                for m in (0, 1):
-                    self.relay(kind, m, 1)
-
-        elif step == 2:
-            pl.when(z == 2)(lambda: self.relay(kind, 3, 0))
-            pl.when(z == 1)(lambda: self.relay(kind, 0, 1))
-        else:
-            at = self.at
-            self.out[kind] = self.grads[kind, z, at.y, at.x, at.c].astype(F32)
-
-            @pl.when(z > 0)
-            def _():
-                self.z_landed(kind, z, z, 0).wait_recv()
-                self.out[kind] += self.z_in[kind, z].astype(F32)
-
-            @pl.when(z < 3)
-            def _():
-                self.z_landed(kind, z, 4, 1).wait_recv()
-                self.out[kind] += self.z_in[kind, 4].astype(F32)
+        pl.when((z == 0) & (m > 0))(lambda: self.z_copy(kind, m, 0).start())
+        pl.when((z == 3) & (m < 3))(lambda: self.z_copy(kind, m, 1).start())
+
+    def z_one(self, kind, m):
+        z = self.at.z
+        pl.when((z == 1) & (m > 1))(lambda: self.relay(kind, m, 0))
+        pl.when((z == 2) & (m < 2))(lambda: self.relay(kind, m, 1))
+
+    def z_two(self, kind, m):
+        z = self.at.z
+        pl.when((z == 2) & (m == 3))(lambda: self.relay(kind, m, 0))
+        pl.when((z == 1) & (m == 0))(lambda: self.relay(kind, m, 1))
+
+    def finish(self, kind):
+        at, z = self.at, self.at.z
+        self.out[kind] = self.grads[kind, z, at.y, at.x, at.c].astype(F32)
+
+        @pl.when(z > 0)
+        def _():
+            self.z_landed(kind, z, z, 0).wait_recv()
+            self.out[kind] += self.z_in[kind, z].astype(F32)
+
+        @pl.when(z < 3)
+        def _():
+            self.z_landed(kind, z, 4, 1).wait_recv()
+            self.out[kind] += self.z_in[kind, 4].astype(F32)
+
+    def slot(self, n, stages=(0, 1, 2, 3)):
+        if 0 in stages:
+            self.second(*chunk_at(n))
+        if 1 in stages:
+            self.third(*chunk_at(n - 1))
+            self.z_start(*chunk_at(n - 1))
+        if 2 in stages:
+            self.z_one(*chunk_at(n - 2))
+        if 3 in stages:
+            self.z_two(*chunk_at(n - 3))
 
     def drain(self):
         z = self.at.z
@@ -681,17 +730,17 @@
     acted_hbm,
     slope_hbm,
     recip_ref,
-    headout_ref,
-    xt_ref,
-    qm_ref,
-    kt_ref,
-    v_ref,
-    att_ref,
-    n1t_ref,
+    headout_hbm,
+    xt_hbm,
+    qm_hbm,
+    kt_hbm,
+    v_hbm,
+    att_hbm,
+    n1t_hbm,
     n1_hbm,
     rs1_ref,
-    gb2_ref,
-    gb2t_ref,
+    gb2_hbm,
+    gb2t_hbm,
     g2_hbm,
     sums_ref,
     masked_ref,
@@ -710,11 +759,36 @@
     parts,
     g2_ref,
     state_sem,
+    gb2_ref,
+    gb2t_ref,
+    n1t_ref,
+    xt_ref,
+    headout_ref,
+    qm_ref,
+    kt_ref,
+    v_ref,
+    att_ref,
+    head_sem,
     hooks,
 ):
     rows = g2_ref.shape[0]
     g2_load = pltpu.make_async_copy(g2_hbm, g2_ref, state_sem.at[0])
     n1_load = pltpu.make_async_copy(n1_hbm, grad_one, state_sem.at[1])
+    gb2_load = pltpu.make_async_copy(gb2_hbm, gb2_ref, state_sem.at[2])
+    gb2t_load = pltpu.make_async_copy(gb2t_hbm, gb2t_ref, state_sem.at[3])
+    n1t_load = pltpu.make_async_copy(n1t_hbm, n1t_ref, state_sem.at[4])
+    xt_load = pltpu.make_async_copy(xt_hbm, xt_ref, state_sem.at[5])
+
+    def head_loads(m, slot):
+        three, two = pl.ds(3 * m, 3), pl.ds(2 * m, 2)
+        pairs = (
+            (headout_hbm.at[three], headout_ref.at[slot]),
+            (qm_hbm.at[three], qm_ref.at[slot]),
+            (kt_hbm.at[two], kt_ref.at[slot]),
+            (v_hbm.at[two], v_ref.at[slot]),
+            (att_hbm.at[m], att_ref.at[slot]),
+        )
+        return [pltpu.make_async_copy(src, dst, head_sem.at[slot, i]) for i, (src, dst) in enumerate(pairs)]
 
     def weight_load(kind, m, slot):
         return pltpu.make_async_copy(blocks_hbm.at[kind, m], weight.at[slot], weight_sem.at[slot])
@@ -746,17 +820,20 @@
         width = value.shape[1]
         grads[kind, m, :, :, :, :, pl.ds(low, width)] = value.astype(BF16).reshape(2, 2, 2, 96, width)
 
+    begin((gb2_load,))
     begin(feed_loads(0, 0))
-    begin((g2_load, n1_load))
+    begin((gb2t_load, n1t_load, g2_load, n1_load, xt_load))
+    begin(head_loads(0, 0))
     for j in range(3):
         probs_load(j, j).start()
     parts[...] = jnp.zeros_like(parts)
-    finish((g2_load, n1_load))
+    finish((gb2_load, gb2t_load, n1t_load, g2_load))
 
     def feed(m, _):
         slot = lax.rem(m, 2)
         pl.when(m < 3)(lambda: begin(feed_loads(m + 1, 1 - slot)))
         finish(feed_loads(m, slot))
+        hooks.feed_begun(m)
         grad_acted = dot(gb2_ref[...], block(2 * slot))
         grad_pre = (grad_acted * acts[slot, 1].astype(F32)).astype(BF16)
         acts[slot, 1] = grad_pre
@@ -766,6 +843,7 @@
         put(UP, m, dot(n1t_ref[...], acts[slot, 1]))
         hooks.up_ready(m)
         g2_ref[...] += dot(acts[slot, 1], block(2 * slot + 1), (1, 1))
+        hooks.feed_done(m)
         return 0
 
     lax.fori_loop(0, 4, feed, 0)
@@ -793,6 +871,7 @@
         )
 
     zero = jnp.zeros((1, 768), F32)
+    finish((n1_load, xt_load))
     sums = lax.fori_loop(0, rows // chunk, norm_back, (zero, zero, zero))
     rows_ref[0, 0:1, :] = sums[0]
     rows_ref[0, 1:2, :] = sums_ref[0:1, :]
@@ -801,10 +880,14 @@
     rows_ref[0, 4:5, :] = sums_ref[1:2, :]
     rows_ref[0, 5:6, :] = sums_ref[2:3, :]
     gb1t[...] = gb1[...].T
+    hooks.normed()
     g2_ref[...] = jnp.zeros_like(g2_ref)
 
     def attend_back(m, _):
+        slot = lax.rem(m, 2)
+        pl.when(m < 3)(lambda: begin(head_loads(m + 1, 1 - slot)))
         weight_load(ATT, m, m).wait()
+        finish(head_loads(m, slot))
         w_out = block(m, 512, 256)
         grad_att_t = dot(gb1[...], w_out).T
         zeros = jnp.zeros((64, rows), BF16)
@@ -821,20 +904,21 @@
         dk, dv, dq = [None, None], [None, None], [None, None]
         for j in range(3):
             t = j // 2
-            tile, head = 2 * m + t, 3 * m + j
-            shift = jnp.sum(sides[j].astype(F32) * headout_ref[head], axis=0, keepdims=True)
+            head = 3 * m + j
+            shift = jnp.sum(sides[j].astype(F32) * headout_ref[slot, j], axis=0, keepdims=True)
             probs_load(head, j).wait()
             weights = probs[j]
-            grad_weights = dot(v_ref[tile], wide[j])
+            grad_weights = dot(v_ref[slot, t], wide[j])
             grad_scores = (weights.astype(F32) * (grad_weights - shift)).astype(BF16)
             grad_v = dot(weights, wide[j].T)
             pl.when(m < 3)(lambda h=head, s=j: probs_load(h + 3, s).start())
-            grad_k = dot(grad_scores, qm_ref[head])
+            grad_k = dot(grad_scores, qm_ref[slot, j])
             half = 64 * (j % 2) if j < 2 else 64
-            grad_q = dot(kt_ref[tile, half : half + 64, :], grad_scores) * SCALE
+            grad_q = dot(kt_ref[slot, t, half : half + 64, :], grad_scores) * SCALE
             dk[t] = grad_k if dk[t] is None else dk[t] + grad_k
             dv[t] = grad_v if dv[t] is None else dv[t] + grad_v
             dq[t] = grad_q if dq[t] is None else jnp.concatenate([dq[t], grad_q], axis=0)
+            hooks.head_done(m, j)
         dq_pair = dq[0].T.astype(BF16)
         dq_single = jnp.concatenate([dq[1], jnp.zeros((64, rows), F32)], axis=0).T.astype(BF16)
         dk = [d.astype(BF16) for d in dk]
@@ -856,7 +940,7 @@
         parts[4 + m, 0:1, 128:640] = wide_sum[:, 128:] + narrow_sum
         grad_proj = dot(xt_ref[0], own[...])
         grad_other = dot(xt_ref[1], other[:, 128:640])
-        grad_out_w = dot(gb1t[...], att_ref[m])
+        grad_out_w = dot(gb1t[...], att_ref[slot])
         put(ATT, m, grad_proj[:, :128], 0)
         put(ATT, m, grad_proj[:, 128:512] + grad_other[:, :384], 128)
         put(ATT, m, grad_proj[:, 512:] + grad_other[:, 384:] + grad_out_w[:, :128], 512)
@@ -895,65 +979,107 @@
 
 
 class NoScatter:
+    def feed_begun(self, m):
+        pass
+
     def down_ready(self, m):
         pass
 
     def up_ready(self, m):
         pass
 
+    def feed_done(self, m):
+        pass
+
+    def normed(self):
+        pass
+
+    def head_done(self, m, j):
+        pass
+
     def att_ready(self, m):
         pass
 
 
+class ScatterHooks:
+    def __init__(self, scatter):
+        self.scatter = scatter
+
+    def feed_begun(self, m):
+        pl.when(m > 0)(lambda: self.scatter.first(UP, m - 1))
+
+    def down_ready(self, m):
+        self.scatter.begin(DOWN, m)
+
+    def up_ready(self, m):
+        self.scatter.first(DOWN, m)
+        self.scatter.begin(UP, m)
+
+    def feed_done(self, m):
+        pl.when(m == 1)(lambda: self.scatter.slot(0, (0,)))
+        pl.when(m == 2)(lambda: self.scatter.slot(1, (0, 1)))
+        pl.when(m == 3)(lambda: self.scatter.slot(2, (0, 1, 2)))
+
+    def normed(self):
+        self.scatter.first(UP, 3)
+        self.scatter.slot(3)
+
+    def head_done(self, m, j):
+        if j == 0:
+            pl.when(m > 0)(lambda: self.scatter.first(ATT, m - 1))
+        if j == 2:
+            self.scatter.slot(m + 4)
+
+    def att_ready(self, m):
+        self.scatter.begin(ATT, m)
+
+
 N_BACKWARD_INS = 20
+N_BACKWARD_SCRATCH = 24
 
 
 def backward_linked(*refs):
     ins = refs[:N_BACKWARD_INS]
     out_ref, rows_out, frames_ref = refs[N_BACKWARD_INS : N_BACKWARD_INS + 3]
     scratch = refs[N_BACKWARD_INS + 3 :]
-    grads, rows_ref, weight, weight_sem, acts, acts_sem, probs, probs_sem = scratch[:8]
-    gb1, gb1t, grad_one, parts, g2, state_sem = scratch[8:14]
-    core_in, first_in, second_in, z_in, rows_in, mate_in = scratch[14:20]
-    send, recv, z_send, z_recv, t_send, t_recv, m_send, m_recv = scratch[20:]
+    scratch, links = scratch[:N_BACKWARD_SCRATCH], scratch[N_BACKWARD_SCRATCH:]
+    grads, rows_ref, gb1, grad_one = scratch[0], scratch[1], scratch[8], scratch[10]
+    core_in, first_in, second_in, z_in, rows_in, mate_in = links[:6]
+    send, recv, z_send, z_recv, t_send, t_recv, m_send, m_recv = links[6:]
     at = Place()
     at.greet(True)
     scatter = Scatter(at, grads, core_in, first_in, second_in, z_in, out_ref, send, recv, z_send, z_recv)
     totals = Totals(at, rows_ref, rows_in, t_send, t_recv)
-    backward_compute(
-        *ins, grads, rows_ref, weight, weight_sem, acts, acts_sem, probs, probs_sem,
-        gb1, gb1t, grad_one, parts, g2, state_sem, NoScatter(),
-    )
+    backward_compute(*ins, *scratch, ScatterHooks(scatter))
     swap = remote(gb1, mate_in, m_send, m_recv, at.mate)
     swap.start()
     totals.start(0)
 
-    def each(step, kind):
-        def body(m, _):
-            step(kind, m)
-            return 0
-
-        lax.fori_loop(0, 4, body, 0)
-
-    for kind in range(3):
-        each(scatter.begin, kind)
-    for kind in range(3):
-        each(scatter.first, kind)
-    for kind in range(3):
-        each(scatter.second, kind)
-    for kind in range(3):
-        each(scatter.third, kind)
-        scatter.z_step(kind, 0)
-    for step in range(1, 4):
-        for kind in range(3):
-            scatter.z_step(kind, step)
-    for stage in range(5):
-        totals.finish(stage)
-        if stage < 4:
-            totals.start(stage + 1)
-    rows_out[...] = rows_ref[5]
+    scatter.first(ATT, 3)
+
+    def rest(n, _):
+        scatter.slot(n)
+        return 0
+
+    lax.fori_loop(8, 12, rest, 0)
+    totals.finish(0)
+    totals.start(1)
+    scatter.slot(12, (1, 2, 3))
+    totals.finish(1)
+    totals.start(2)
+    scatter.finish(DOWN)
+    scatter.finish(UP)
+    totals.finish(2)
+    totals.start(3)
+    scatter.slot(13, (2, 3))
+    totals.finish(3)
+    totals.start(4)
     swap.wait()
     finish_frames(grad_one, mate_in, ins[18], frames_ref)
+    scatter.slot(14, (3,))
+    totals.finish(4)
+    rows_out[...] = rows_ref[5]
+    scatter.finish(ATT)
     scatter.drain()
 
 
@@ -961,12 +1087,9 @@
     ins = refs[:N_BACKWARD_INS]
     grads_out, rows_out, mate_out, grad_one_out = refs[N_BACKWARD_INS : N_BACKWARD_INS + 4]
     scratch = refs[N_BACKWARD_INS + 4 :]
-    grads, rows_ref, weight, weight_sem, acts, acts_sem, probs, probs_sem = scratch[:8]
-    gb1, gb1t, grad_one, parts, g2, state_sem, keep_sem = scratch[8:]
-    backward_compute(
-        *ins, grads, rows_ref, weight, weight_sem, acts, acts_sem, probs, probs_sem,
-        gb1, gb1t, grad_one, parts, g2, state_sem, NoScatter(),
-    )
+    *scratch, keep_sem = scratch
+    grads, rows_ref, gb1, grad_one = scratch[0], scratch[1], scratch[8], scratch[10]
+    backward_compute(*ins, *scratch, NoScatter())
     keep = pltpu.make_async_copy(grads, grads_out, keep_sem)
     keep.start()
     rows_out[...] = rows_ref[0]
@@ -990,7 +1113,17 @@
         pltpu.VMEM((rows, 768), F32),
         pltpu.VMEM((8, 8, 768), F32),
         pltpu.VMEM((rows, 768), F32),
-        pltpu.SemaphoreType.DMA((2,)),
+        pltpu.SemaphoreType.DMA((6,)),
+        pltpu.VMEM((rows, 768), BF16),
+        pltpu.VMEM((768, rows), BF16),
+        pltpu.VMEM((768, rows), BF16),
+        pltpu.VMEM((2, 768, rows), BF16),
+        pltpu.VMEM((2, 3, 64, rows), F32),
+        pltpu.VMEM((2, 3, rows, 128), BF16),
+        pltpu.VMEM((2, 2, 128, LEN), BF16),
+        pltpu.VMEM((2, 2, LEN, 128), BF16),
+        pltpu.VMEM((2, rows, 256), BF16),
+        pltpu.SemaphoreType.DMA((2, 5)),
     ]
 
 
@@ -1000,7 +1133,7 @@
     ins = (
         blocks, probs, acted, slope, recip, headout, xt, qm, kt, v, att, n1t, n1, rs1, gb2, gb2t, g2, sums, masked, vec
     )
-    in_specs = [hbm() if i in (0, 1, 2, 3, 12, 16) else vmem() for i in range(20)]
+    in_specs = [vmem() if i in (4, 13, 17, 18, 19) else hbm() for i in range(20)]
     if linked:
         return pl.pallas_call(
             backward_linked,

time: 320 us -> 256 us (0.80)
  Pallas kernels: 283 us -> 221 us
    pallas_call x1, Pallas kernels: 160 us -> 118 us  [run_backward(): pl.pallas_call(backward_linked, name='backward', out_shape=[jax.ShapeDtyp...]
    pallas_call x1, Pallas kernels: 123 us -> 103 us  [run_forward(): pl.pallas_call(forward_linked, name='forward', out_shape=[jax.ShapeDtypeS...]
where the time goes in v2:
time: 256 us; the launch traced here: 253 us
  Pallas kernels  221 us (86%)
  local copies, waits for them, and re-layouts  21.6 us (8%)
  other arithmetic  9.14 us (4%)
    pallas_call x1, Pallas kernels, run_backward(): pl.pallas_call(backward_linked, name='backward', out_shape=[jax.ShapeDtyp...  118 us
    pallas_call x1, Pallas kernels, run_forward(): pl.pallas_call(forward_linked, name='forward', out_shape=[jax.ShapeDtypeS...  103 us

profile of v2, /device:TPU:16, one launch (start us, length us, event | category | flops | bytes accessed | tf_op | source)
XLA Modules:
  0.0 252.6 jit_solution(818000557730106740)
XLA Ops:
  0.7 0.8 slice.135
  1.5 0.7 slice.136
  2.3 0.7 slice.137
  3.0 0.7 slice.138
  3.8 0.7 slice.139
  4.5 0.7 slice.140
  5.2 0.9 copy.44
  6.2 0.1 concatenate.24
  6.3 1.8 pad_maximum_fusion.pack_ref
  8.1 0.7 copy.50
  8.7 0.7 slice.143
  9.4 0.1 slice.144
  9.5 0.7 slice.145
  10.2 0.1 slice.146
  10.3 0.7 slice_bitcast_fusion.10
  11.0 0.1 concatenate.25
  11.1 0.6 fusion.2.bias_ref
  11.7 0.7 fusion.8
  12.4 0.2 and_reduce_fusion
  12.6 1.7 broadcast_select_fusion.x_ref
  14.3 0.0 copy-done.9
  14.3 0.6 dynamic_slice.27
  14.9 0.7 broadcast_compare_fusion
  15.5 0.9 select_convert_fusion.refs_0_
  16.5 0.9 copy.45.refs_1_
  17.3 0.0 copy-done.4
  17.5 0.6 pad_convert_fusion.refs_3_.refs_19_
  18.1 102.9 %forward.1 = (bf16[3,4,2,2,2,96,768]{6,5,4,3,2,1,0:T(8,128)(2,1)}, bf16[12,1024,512]{2,1,0:T(8,128)(2,1)}, bf16[512,768]{1,0:T(8,128)(2,1)}, f32[12,8,512]{2,1,0...) custom-call(bf16[3,96,768]{2,1,0:T(8,128)(2,1)} %pad_maximum_fusion., ...), custom_call_target="tpu_custom_call" | custom-call | tf_op jit(solution)/shard_map/forward/pallas_call | solution.py:535
  121.0 1.1 reshape.99.refs_18_
  122.1 118.0 %backward.1 = (f32[3,96,768]{2,1,0:T(8,128)}, f32[16,768]{1,0:T(8,128)}, bf16[512,768]{1,0:T(8,128)(2,1)}) custom-call(bf16[3,4,2,2,2,96,768]{6,5,4,3,2,1,0:T(8,128)(2,1)} %get-tuple-element.41.refs_0_, bf16[12,1024,512]{2,1,0:T(8,128)(2,1)} %get-tuple-element.42.refs_1_, bf16[4,512,768]{2,1,0:T(8,128)(2,1)} %get-tuple-element.43.refs_2_, ...), custom_call_target="tpu_custom_call" | custom-call | tf_op jit(solution)/shard_map/backward/pallas_call | solution.py:1138
  240.2 2.1 slice_bitcast_fusion
  242.3 0.1 fusion.11
  242.4 0.6 pad_maximum_fusion.1
  243.0 0.6 pad_maximum_fusion.2
  243.7 0.6 pad_maximum_fusion.3
  244.3 0.7 copy.47
  245.1 0.8 dynamic-slice_bitcast_fusion
  245.8 0.8 dynamic-slice_bitcast_fusion.1
  246.6 0.1 reshape.94
  246.7 0.7 constant_dynamic-slice_fusion.4
  247.3 0.1 reshape.95
  247.4 0.7 constant_dynamic-slice_fusion.3
  248.1 0.8 dynamic-slice_reduce_fusion
  248.8 0.7 constant_dynamic-slice_fusion.2
  249.5 0.8 constant_dynamic-slice_fusion.1
  250.3 0.5 slice_bitcast_fusion.3
  250.8 0.9 copy.53
  251.7 0.9 copy.54
  (39 shorter events, 0.2 us)
Async XLA Ops:
  0.7 11.9 %copy-start = (bf16[512,768]{1,0:T(8,128)(2,1)S(1)}, bf16[512,768]{1,0:T(8,128)(2,1)}, u32[]{:S(2)}) copy-start(bf16[512,768]{1,0:T(8,128)(2,1)} %param.20) | copy-start | bytes 2359300
  0.7 13.6 %copy-start.9 = (s32[2]{0:T(128)S(1)}, s32[2]{0:T(128)}, u32[]{:S(2)}) copy-start(s32[2]{0:T(128)} %param.21) | copy-start | bytes 28
  0.7 16.6 %copy-start.3 = (bf16[768]{0:T(1024)(128)(2,1)S(1)}, bf16[768]{0:T(1024)(128)(2,1)}, u32[]{:S(2)}) copy-start(bf16[768]{0:T(1024)(128)(2,1)} %param.33) | copy-start | bytes 4612
  0.7 16.6 %copy-start.4 = (bf16[768]{0:T(1024)(128)(2,1)S(1)}, bf16[768]{0:T(1024)(128)(2,1)}, u32[]{:S(2)}) copy-start(bf16[768]{0:T(1024)(128)(2,1)} %param.34) | copy-start | bytes 4612
  0.7 16.6 %copy-start.5 = (bf16[768]{0:T(1024)(128)(2,1)S(1)}, bf16[768]{0:T(1024)(128)(2,1)}, u32[]{:S(2)}) copy-start(bf16[768]{0:T(1024)(128)(2,1)} %param.35) | copy-start | bytes 4612
  0.7 16.7 %copy-start.6 = (bf16[768]{0:T(1024)(128)(2,1)S(1)}, bf16[768]{0:T(1024)(128)(2,1)}, u32[]{:S(2)}) copy-start(bf16[768]{0:T(1024)(128)(2,1)} %param.36) | copy-start | bytes 4612
  0.7 16.7 %copy-start.7 = (bf16[768]{0:T(1024)(128)(2,1)S(1)}, bf16[768]{0:T(1024)(128)(2,1)}, u32[]{:S(2)}) copy-start(bf16[768]{0:T(1024)(128)(2,1)} %param.37) | copy-start | bytes 4612
  0.7 16.7 %copy-start.8 = (bf16[768]{0:T(1024)(128)(2,1)S(1)}, bf16[768]{0:T(1024)(128)(2,1)}, u32[]{:S(2)}) copy-start(bf16[768]{0:T(1024)(128)(2,1)} %param.38) | copy-start | bytes 4612
  240.2 10.6 %copy-start.1 = (bf16[512,768]{1,0:T(8,128)(2,1)S(1)}, bf16[512,768]{1,0:T(8,128)(2,1)}, u32[]{:S(2)}) copy-start(bf16[512,768]{1,0:T(8,128)(2,1)} %get-tuple-element.162) | copy-start | bytes 2359300
  242.3 9.4 %copy-start.2 = (bf16[512,768]{1,0:T(8,128)(2,1)S(1)}, bf16[512,768]{1,0:T(8,128)(2,1)}, u32[]{:S(2)}) copy-start(bf16[512,768]{1,0:T(8,128)(2,1)} %get-tuple-element.163) | copy-start | bytes 2359300

commit v3 on v2

v3 whole, which is shorter than its diff:
```python
import functools
import math

import jax
import jax.numpy as jnp
from jax import lax
from jax.experimental import pallas as pl
from jax.experimental.pallas import tpu as pltpu
from jax.sharding import PartitionSpec as P

HEAD_DIM = 64
SPAN = 10
LEN = 1024
EPSILON = 1e-05
NEGATIVE = -1e30
SCALE = 1.0 / math.sqrt(HEAD_DIM)

F32 = jnp.float32
BF16 = jnp.bfloat16
MESH = pl.DeviceIdType.MESH
VMEM_LIMIT = 63 * 1024 * 1024

ATT, UP, DOWN = 0, 1, 2
PROJ = 640


def dot(left, right, contract=(1, 0)):
    return lax.dot_general(
        left, right, (((contract[0],), (contract[1],)), ((), ())), preferred_element_type=F32
    )


def hbm():
    return pl.BlockSpec(memory_space=pl.ANY)


def vmem():
    return pl.BlockSpec(memory_space=pltpu.VMEM)


class Place:
    def __init__(self):
        self.dp = lax.axis_index("dp")
        self.z = lax.axis_index("mp")
        self.c = lax.rem(self.dp, 2)
        self.x = lax.rem(self.dp // 2, 2)
        self.y = self.dp // 4
        self.core = (self.dp + 1 - 2 * self.c, self.z)
        self.across_x = (self.dp + 2 - 4 * self.x, self.z)
        self.across_y = (self.dp + 4 - 8 * self.y, self.z)
        self.right = (self.dp, self.z + 1)
        self.left = (self.dp, self.z - 1)
        self.mate = (self.dp, self.z + 1 - 2 * lax.rem(self.z, 2))
        self.far = (self.dp, lax.rem(self.z + 2, 4))

    def greet(self, far):
        barrier = pltpu.get_barrier_semaphore()

        def signal(device):
            pl.semaphore_signal(barrier, inc=1, device_id=device, device_id_type=MESH)

        signal(self.core)
        signal(self.across_x)
        signal(self.across_y)
        if far:
            signal(self.far)
        pl.when(self.z < 3)(lambda: signal(self.right))
        pl.when(self.z > 0)(lambda: signal(self.left))
        ends = jnp.where((self.z == 0) | (self.z == 3), 1, 2)
        pl.semaphore_wait(barrier, (4 if far else 3) + ends)


def remote(src, dst, send, recv, device):
    return pltpu.make_async_remote_copy(
        src_ref=src, dst_ref=dst, send_sem=send, recv_sem=recv, device_id=device, device_id_type=MESH
    )


class Gather:
    def __init__(self, at, blocks, biases, z_send, z_recv, p_send, p_recv):
        self.at, self.blocks, self.biases = at, blocks, biases
        self.z_send, self.z_recv, self.p_send, self.p_recv = z_send, z_recv, p_send, p_recv

    def z_copy(self, kind, m, direction, step):
        at = self.at
        if kind == 3:
            ref = self.biases.at[m]
        else:
            ref = self.blocks.at[kind, m, at.y, at.x, at.c]
        device = at.right if direction == 0 else at.left
        return remote(ref, ref, self.z_send.at[kind, direction, step], self.z_recv.at[kind, m], device)

    def z_step(self, kind, step):
        z = self.at.z
        if step == 0:
            pl.when(z < 3)(lambda: self.z_copy(kind, z, 0, 0).start())
            pl.when(z > 0)(lambda: self.z_copy(kind, z, 1, 0).start())
            return

        @pl.when(z >= step)
        def _():
            self.z_copy(kind, z - step, 0, 0).wait_recv()
            if step < 3:
                pl.when(z < 3)(lambda: self.z_copy(kind, z - step, 0, step).start())
            self.first(kind, z - step)

        @pl.when(z + step <= 3)
        def _():
            self.z_copy(kind, z + step, 1, 0).wait_recv()
            if step < 3:
                pl.when(z > 0)(lambda: self.z_copy(kind, z + step, 1, step).start())
            self.first(kind, z + step)

    def plane_copy(self, kind, m, which):
        at, block = self.at, self.blocks.at[kind, m]
        x, y, c = at.x, at.y, at.c
        low, high = pl.ds(0, 48), pl.ds(48, 48)
        ref, device = {
            0: lambda: (block.at[y, x, c, low], at.across_x),
            1: lambda: (block.at[y, x, c, high], at.across_y),
            2: lambda: (block.at[y, :, c, low], at.across_y),
            3: lambda: (block.at[:, x, c, high], at.across_x),
            4: lambda: (block.at[:, :, c], at.core),
        }[which]()
        return remote(ref, ref, self.p_send.at[kind, m, which], self.p_recv.at[kind, m, which], device)

    def at_step(self, step, act):
        z = self.at.z
        if step == 0:
            act(z)
            return
        pl.when(z >= step)(lambda: act(z - step))
        pl.when(z + step <= 3)(lambda: act(z + step))

    def first(self, kind, m):
        if kind < 3:
            self.plane_copy(kind, m, 0).start()
            self.plane_copy(kind, m, 1).start()

    def second(self, kind, step):
        def act(m):
            self.plane_copy(kind, m, 0).wait_recv()
            self.plane_copy(kind, m, 2).start()
            self.plane_copy(kind, m, 1).wait_recv()
            self.plane_copy(kind, m, 3).start()

        self.at_step(step, act)

    def third(self, kind, step):
        def act(m):
            self.plane_copy(kind, m, 2).wait_recv()
            self.plane_copy(kind, m, 3).wait_recv()
            self.plane_copy(kind, m, 4).start()

        self.at_step(step, act)

    def last(self, kind):
        for m in range(4):
            self.plane_copy(kind, m, 4).wait_recv()

    def drain(self):
        z = self.at.z
        for kind in range(4):
            for step in range(3):
                pl.when((z < 3) & (z >= step))(
                    lambda k=kind, s=step: self.z_copy(k, z - s, 0, s).wait_send()
                )
                pl.when((z > 0) & (z + step <= 3))(
                    lambda k=kind, s=step: self.z_copy(k, z + s, 1, s).wait_send()
                )
        for kind in range(3):
            for m in range(4):
                for which in range(5):
                    self.plane_copy(kind, m, which).wait_send()


def block_of(blocks, kind, m, low=0, width=768):
    return blocks[kind, m, :, :, :, :, pl.ds(low, width)].reshape(768, width)


def lane_mask(rows, lower):
    lanes = lax.broadcasted_iota(jnp.int32, (rows, 128), 1)
    return (lanes < 64) if lower else (lanes >= 64)


def forward_compute(
    blocks,
    biases,
    xs,
    keybias_ref,
    valid_ref,
    cot_ref,
    vec_ref,
    probs_hbm,
    out_ref,
    outs_hbm,
    outs_ref,
    outs_sem,
    k_ref,
    vt_ref,
    att_t,
    probs,
    probs_sem,
    total,
    low,
    stats,
    hooks,
):
    rows = xs.shape[1]
    (recip_ref, headout_ref, xt_ref, qm_ref, kt_ref, v_ref, att_ref, acted_ref, slope_ref, n1t_ref, n1_ref, rs1_ref,
     gb2_ref, gb2t_ref, g2_ref, sums_ref) = outs_ref
    keeps = [
        pltpu.make_async_copy(ref, to, outs_sem.at[i]) for i, (ref, to) in enumerate(zip(outs_ref, outs_hbm, strict=True))
    ]

    def keep(*which):
        for i in which:
            keeps[i].start()

    xt_ref[0] = xs[0].T
    ones_lane = jnp.where(lax.broadcasted_iota(jnp.int32, (rows, 128), 1) == 0, 1.0, 0.0).astype(BF16)

    def probs_copy(head, side, slot):
        return pltpu.make_async_copy(
            probs.at[slot], probs_hbm.at[head, pl.ds(side * rows, rows)], probs_sem.at[slot]
        )

    own_rows, other_rows = pl.ds(0, rows), pl.ds(rows, rows)

    def project(m, _):
        bias = biases[m, 0:1, :].astype(F32)[:, :PROJ]
        own = dot(xs[0], block_of(blocks, ATT, m, 0, PROJ)) + bias
        k_ref[2 * m, own_rows] = own[:, 128:256].astype(BF16)
        v_ref[2 * m, own_rows] = own[:, 256:384].astype(BF16)
        k_ref[2 * m + 1, own_rows] = own[:, 384:512].astype(BF16)
        v_ref[2 * m + 1, own_rows] = own[:, 512:640].astype(BF16)
        lower, upper = lane_mask(rows, True), lane_mask(rows, False)
        pair = own[:, 0:128].astype(BF16).astype(F32) * SCALE
        single = pltpu.roll(own[:, 384:512].astype(BF16).astype(F32) * SCALE, 64, 1)
        qm_ref[3 * m] = jnp.where(lower, pair, 0.0).astype(BF16)
        qm_ref[3 * m + 1] = jnp.where(upper, pair, 0.0).astype(BF16)
        qm_ref[3 * m + 2] = jnp.where(upper, single, 0.0).astype(BF16)
        for tile in range(2):
            kt_ref[2 * m + tile, :, own_rows] = k_ref[2 * m + tile, own_rows].T
            vt_ref[2 * m + tile, :, own_rows] = v_ref[2 * m + tile, own_rows].T
        hooks.in_project(m)
        return 0

    def project_other(m, _):
        bias = biases[m, 0:1, :].astype(F32)[:, 128:PROJ]
        other = dot(xs[1], block_of(blocks, ATT, m, 128, 512)) + bias
        k_ref[2 * m, other_rows] = other[:, 0:128].astype(BF16)
        v_ref[2 * m, other_rows] = other[:, 128:256].astype(BF16)
        k_ref[2 * m + 1, other_rows] = other[:, 256:384].astype(BF16)
        v_ref[2 * m + 1, other_rows] = other[:, 384:512].astype(BF16)
        for tile in range(2):
            kt_ref[2 * m + tile, :, other_rows] = k_ref[2 * m + tile, other_rows].T
            vt_ref[2 * m + tile, :, other_rows] = v_ref[2 * m + tile, other_rows].T
        return 0

    def attend_half(m, j, side):
        tile, head = 2 * m + j // 2, 3 * m + j
        half = own_rows if side == 0 else other_rows
        keys = jnp.concatenate([k_ref[tile, half], keybias_ref[half, :]], axis=1)
        queries = jnp.concatenate([qm_ref[head], ones_lane], axis=1)
        scores = dot(keys, queries, (1, 1))
        top = jnp.max(scores, axis=0, keepdims=True)
        weights = jnp.exp(scores - top)
        total_weight = jnp.sum(weights, axis=0, keepdims=True)
        weights = weights.astype(BF16)
        if side == 0:
            pl.when(m > 0)(lambda: probs_copy(head, side, j).wait())
        else:
            probs_copy(head, side, j).wait()
        probs[j] = weights
        probs_copy(head, side, j).start()
        lane = 64 * (j % 2)
        head_out = dot(vt_ref[tile, lane : lane + 64, half], weights)
        headout_ref[head, side] = head_out
        return top, total_weight, head_out

    def attend_own(m, _):
        for j in range(3):
            top, total_weight, _ = attend_half(m, j, 0)
            stats[3 * m + j, 0:1, :] = top
            stats[3 * m + j, 1:2, :] = total_weight
            hooks.in_own(m, j)
        return 0

    def attend(m, _):
        att_t[0:64, :] = jnp.zeros((64, rows), BF16)
        for j in range(3):
            head = 3 * m + j
            top, total_weight, head_out = attend_half(m, j, 1)
            top_own = stats[head, 0:1, :]
            top_all = jnp.maximum(top, top_own)
            factor, factor_own = jnp.exp(top - top_all), jnp.exp(top_own - top_all)
            recip = 1.0 / (factor_own * stats[head, 1:2, :] + factor * total_weight)
            factor, factor_own = factor * recip, factor_own * recip
            recip_ref[head] = jnp.concatenate(
                [factor_own, factor, jnp.zeros((6, rows), F32)], axis=0
            )
            place = (128, 192, 64)[j]
            att_t[place : place + 64, :] = (headout_ref[head, 0] * factor_own + head_out * factor).astype(BF16)
            hooks.in_attend(m, j)
        att_ref[m] = att_t[...].T
        part = dot(att_ref[m], block_of(blocks, ATT, m, 512, 256), (1, 1))

        @pl.when(m == 0)
        def _():
            total[...] = part

        @pl.when(m > 0)
        def _():
            total[...] += part

        return 0

    hooks.before_project()
    lax.fori_loop(0, 4, project, 0)
    lax.fori_loop(0, 4, attend_own, 0)
    hooks.before_other()
    xt_ref[1] = xs[1].T
    lax.fori_loop(0, 4, project_other, 0)
    keep(2, 3, 4, 5)
    lax.fori_loop(0, 4, attend, 0)
    keep(0, 1, 6)
    for j in range(3):
        probs_copy(9 + j, 1, j).wait()

    chunk = 64

    def norm_one(i, _):
        r = pl.ds(pl.multiple_of(i * chunk, chunk), chunk)
        resid = xs[0, r, :].astype(F32) + total[r, :] + vec_ref[0:1, :]
        centered = resid - jnp.mean(resid, axis=1, keepdims=True)
        rstd = lax.rsqrt(jnp.mean(centered * centered, axis=1, keepdims=True) + EPSILON)
        unit = centered * rstd
        n1_ref[r, :] = unit
        rs1_ref[r, :] = rstd
        low[r, :] = (unit * vec_ref[2:3, :] + vec_ref[3:4, :]).astype(BF16)
        return 0

    lax.fori_loop(0, rows // chunk, norm_one, 0)
    n1t_ref[...] = low[...].T
    keep(9, 10, 11)
    hooks.before_up()

    def feed(m, _):
        pre = dot(low[...], block_of(blocks, UP, m)) + biases[m, 1:2, :].astype(F32)
        phi = 0.5 * (1.0 + lax.erf(pre * (1.0 / math.sqrt(2.0))))
        acted_ref[m] = (pre * phi).astype(BF16)
        slope_ref[m] = (phi + pre * jnp.exp(-0.5 * pre * pre) * (1.0 / math.sqrt(2.0 * math.pi))).astype(BF16)
        hooks.in_feed(m)
        return 0

    lax.fori_loop(0, 4, feed, 0)
    keep(7, 8)
    hooks.before_down()

    def down(m, _):
        part = dot(acted_ref[m], block_of(blocks, DOWN, m), (1, 1))

        @pl.when(m == 0)
        def _():
            total[...] = part

        @pl.when(m > 0)
        def _():
            total[...] += part

        return 0

    lax.fori_loop(0, 4, down, 0)

    def norm_two(i, sums):
        r = pl.ds(pl.multiple_of(i * chunk, chunk), chunk)
        normed = n1_ref[r, :] * vec_ref[2:3, :] + vec_ref[3:4, :]
        resid = normed + total[r, :] + vec_ref[1:2, :]
        centered = resid - jnp.mean(resid, axis=1, keepdims=True)
        rstd = lax.rsqrt(jnp.mean(centered * centered, axis=1, keepdims=True) + EPSILON)
        unit = centered * rstd
        valid = valid_ref[r, :]
        out_ref[r, :] = (valid * (unit * vec_ref[4:5, :] + vec_ref[5:6, :])).astype(BF16)
        grad = valid * cot_ref[r, :].astype(F32)
        scaled = grad * vec_ref[4:5, :]
        grad_in = (
            scaled
            - jnp.mean(scaled, axis=1, keepdims=True)
            - unit * jnp.mean(scaled * unit, axis=1, keepdims=True)
        ) * rstd
        g2_ref[r, :] = grad_in
        gb2_ref[r, :] = grad_in.astype(BF16)
        return (
            sums[0] + jnp.sum(grad_in, axis=0, keepdims=True),
            sums[1] + jnp.sum(grad * unit, axis=0, keepdims=True),
            sums[2] + jnp.sum(grad, axis=0, keepdims=True),
        )

    zero = jnp.zeros((1, 768), F32)
    sums = lax.fori_loop(0, rows // chunk, norm_two, (zero, zero, zero))
    sums_ref[...] = jnp.concatenate([*sums, jnp.zeros((5, 768), F32)], axis=0)
    keep(12, 14, 15)
    gb2t_ref[...] = gb2_ref[...].T
    keep(13)
    for copy in keeps:
        copy.wait()


class NoHooks:
    def before_project(self):
        pass

    def in_project(self, m):
        pass

    def before_other(self):
        pass

    def in_own(self, m, j):
        pass

    def in_attend(self, m, j):
        pass

    def before_up(self):
        pass

    def in_feed(self, m):
        pass

    def before_down(self):
        pass


class GatherHooks:
    IN_PROJECT = {
        1: (("second", UP, 0),),
        3: (("second", DOWN, 0),),
    }
    IN_OWN = {
        (0, 2): (("second", UP, 1),),
        (1, 2): (("z_step", UP, 2), ("third", UP, 0)),
        (3, 2): (("third", UP, 1),),
    }
    BEFORE_OTHER = (("third", DOWN, 0),)
    IN_ATTEND = {
        (0, 0): (("z_step", DOWN, 1),),
        (0, 2): (("second", UP, 2),),
        (1, 1): (("z_step", UP, 3),),
        (1, 2): (("second", DOWN, 1),),
        (2, 1): (("z_step", DOWN, 2), ("third", UP, 2)),
        (3, 0): (("second", UP, 3),),
    }
    BEFORE_UP = (("z_step", DOWN, 3), ("third", UP, 3), ("second", DOWN, 2))
    IN_FEED = {
        1: (("third", DOWN, 1),),
        2: (("second", DOWN, 3),),
    }

    def __init__(self, gather, swap, blocks_out, keep_sem):
        self.gather, self.swap = gather, swap
        self.keep = [
            pltpu.make_async_copy(gather.blocks.at[kind], blocks_out.at[kind], keep_sem.at[kind]) for kind in range(3)
        ]

    def run(self, events):
        for name, kind, step in events:
            getattr(self.gather, name)(kind, step)

    def before_project(self):
        self.gather.last(ATT)
        self.keep[ATT].start()

    def in_project(self, m):
        self.on(self.IN_PROJECT, m)

    def before_other(self):
        self.run(self.BEFORE_OTHER)
        self.swap.wait()

    def on(self, table, m, j=None):
        for key, events in table.items():
            index, head = (key, None) if j is None else key
            if head == j:
                pl.when(m == index)(functools.partial(self.run, events))

    def in_own(self, m, j):
        self.on(self.IN_OWN, m, j)

    def in_attend(self, m, j):
        self.on(self.IN_ATTEND, m, j)

    def before_up(self):
        self.run(self.BEFORE_UP)
        self.gather.last(UP)
        self.keep[UP].start()

    def in_feed(self, m):
        self.on(self.IN_FEED, m)

    def before_down(self):
        self.run((("third", DOWN, 2), ("third", DOWN, 3)))
        self.gather.last(DOWN)
        self.keep[DOWN].start()

    def finish(self):
        for copy in self.keep:
            copy.wait()
        self.gather.drain()


N_KEPT = 16


def pack_weights(query, key, value, out_t, up, down_t):
    pair, single = 2 * HEAD_DIM, 3 * HEAD_DIM
    att = jnp.concatenate(
        [
            query[:, :pair], key[:, :pair], value[:, :pair],
            query[:, pair:single], key[:, pair:single],
            value[:, pair:single], out_t[:, pair:single], out_t[:, :pair],
        ],
        axis=1,
    )
    return att, up, down_t


def pack_biases(query_bias, value_bias, up_bias):
    def row(i, bias):
        return bias[i : i + 1, :]

    blank = jnp.zeros((1, HEAD_DIM), BF16)
    pieces = [
        row(0, query_bias), row(1, query_bias), blank, blank, row(0, value_bias), row(1, value_bias),
        row(2, query_bias), blank, row(2, value_bias), blank, blank, blank,
    ]
    ups = jnp.concatenate([row(i, up_bias) for i in range(6)], axis=1)
    return jnp.concatenate([jnp.concatenate(pieces, axis=1), ups, jnp.zeros((14, 768), BF16)], axis=0)


def fill_vectors(vec, vecs):
    for i, ref in enumerate(vecs):
        vec[i : i + 1, :] = ref[...].astype(F32).reshape(1, 768)


def transposed(block):
    wide = jnp.concatenate([block, jnp.zeros((block.shape[0], 128 - block.shape[1]), block.dtype)], axis=1)
    return wide.T[: block.shape[1]]


def forward_linked(*refs):
    (lengths, starts, frames, cot, query, key, value, out_w, up, down, query_bias, value_bias, up_bias) = refs[:13]
    vecs, refs = refs[13:20], refs[20:]
    blocks_hbm, probs_hbm, out_ref, masked_ref, *outs = refs[: 4 + N_KEPT]
    blocks, biases, xs, keybias, valid, vec, *scratch = refs[4 + N_KEPT :]
    scratch, links = scratch[:N_FORWARD_SCRATCH], scratch[N_FORWARD_SCRATCH:]
    z_send, z_recv, p_send, p_recv, x_send, x_recv, keep_sem = links
    at = Place()
    at.greet(False)
    gather = Gather(at, blocks, biases, z_send, z_recv, p_send, p_recv)
    packs = pack_weights(
        query[...], key[...], value[...], transposed(out_w[...]), up[...], down[...]
    )
    for kind in range(3):
        blocks[kind, at.z, at.y, at.x, at.c] = packs[kind]
        if kind == 0:
            gather.z_step(ATT, 0)
            gather.first(ATT, at.z)
    biases[at.z] = pack_biases(query_bias[...], value_bias[...], up_bias[...])
    gather.z_step(3, 0)
    fill_vectors(vec, vecs)
    rows = frames.shape[0]
    clip, half = at.z // 2, lax.rem(at.z, 2)
    length = lengths[clip]
    start = starts[pl.ds(clip, 1), :]
    for side in range(2):
        first = rows * (half if side == 0 else 1 - half)
        slots = first + lax.broadcasted_iota(jnp.int32, (rows, start.shape[1]), 0)
        covered = jnp.where((slots >= start) & (slots < start + SPAN), 1.0, 0.0)
        masked_ref[side] = jnp.max(covered, axis=1, keepdims=True)
        slots = first + lax.broadcasted_iota(jnp.int32, (rows, 128), 0)
        lanes = lax.broadcasted_iota(jnp.int32, (rows, 128), 1)
        here = pl.ds(side * rows, rows)
        keybias[here, :] = jnp.where((slots >= length) & (lanes == 0), NEGATIVE, 0.0).astype(BF16)
        if side == 0:
            valid[...] = jnp.where(slots[:, 0:1] < length, 1.0, 0.0)
    xs[0] = jnp.where(masked_ref[0] > 0, vec[6:7, :], frames[...].astype(F32)).astype(BF16)
    swap = remote(xs.at[0], xs.at[1], x_send, x_recv, at.mate)
    gather.z_step(ATT, 1)
    gather.z_step(3, 1)
    gather.second(ATT, 0)
    gather.z_step(ATT, 2)
    gather.z_step(3, 2)
    gather.z_step(UP, 0)
    gather.second(ATT, 1)
    gather.third(ATT, 0)
    gather.z_step(ATT, 3)
    gather.z_step(3, 3)
    gather.second(ATT, 2)
    gather.third(ATT, 1)
    gather.second(ATT, 3)
    gather.first(UP, at.z)
    gather.z_step(UP, 1)
    swap.start()
    gather.z_step(DOWN, 0)
    gather.first(DOWN, at.z)
    gather.third(ATT, 2)
    gather.third(ATT, 3)
    hooks = GatherHooks(gather, swap, blocks_hbm, keep_sem)
    forward_compute(blocks, biases, xs, keybias, valid, cot, vec, probs_hbm, out_ref, outs, *scratch, hooks)
    hooks.finish()


def forward_alone(blocks_in, biases, xs, keybias, valid, cot, *refs):
    vecs, (probs_hbm, out_ref, *outs), scratch = refs[:7], refs[7 : 9 + N_KEPT], refs[9 + N_KEPT :]
    blocks, vec, *scratch, keep_sem = scratch
    fill_vectors(vec, vecs)
    load = pltpu.make_async_copy(blocks_in, blocks, keep_sem)
    load.start()
    load.wait()
    forward_compute(
        blocks, biases, xs, keybias, valid, cot, vec, probs_hbm, out_ref, outs, *scratch, NoHooks()
    )


BLOCKS = (3, 4, 2, 2, 2, 96, 768)


def forward_outs(rows):
    def of(shape, dtype):
        return jax.ShapeDtypeStruct(shape, dtype)

    return [
        of((12, 8, rows), F32),
        of((12, 2, 64, rows), F32),
        of((2, 768, rows), BF16),
        of((12, rows, 128), BF16),
        of((8, 128, LEN), BF16),
        of((8, LEN, 128), BF16),
        of((4, rows, 256), BF16),
        of((4, rows, 768), BF16),
        of((4, rows, 768), BF16),
        of((768, rows), BF16),
        of((rows, 768), F32),
        of((rows, 1), F32),
        of((rows, 768), BF16),
        of((768, rows), BF16),
        of((rows, 768), F32),
        of((8, 768), F32),
    ]


N_FORWARD_SCRATCH = 10


def forward_scratch(rows):
    return [
        [pltpu.VMEM(out.shape, out.dtype) for out in forward_outs(rows)],
        pltpu.SemaphoreType.DMA((N_KEPT,)),
        pltpu.VMEM((8, LEN, 128), BF16),
        pltpu.VMEM((8, 128, LEN), BF16),
        pltpu.VMEM((256, rows), BF16),
        pltpu.VMEM((3, rows, rows), BF16),
        pltpu.SemaphoreType.DMA((3,)),
        pltpu.VMEM((rows, 768), F32),
        pltpu.VMEM((rows, 768), BF16),
        pltpu.VMEM((12, 8, rows), F32),
    ]


def run_forward_linked(rows, *ins):
    outs = forward_outs(rows)
    probs = jax.ShapeDtypeStruct((12, LEN, rows), BF16)
    frames = jax.ShapeDtypeStruct((rows, 768), BF16)
    masked = jax.ShapeDtypeStruct((2, rows, 1), F32)
    blocks, probs, frames, masked, *kept = pl.pallas_call(
        forward_linked,
        name="forward",
        out_shape=[jax.ShapeDtypeStruct(BLOCKS, BF16), probs, frames, masked, *outs],
        in_specs=[pl.BlockSpec(memory_space=pltpu.SMEM)] + [vmem()] * 19,
        out_specs=[hbm(), hbm(), vmem(), vmem()] + [hbm()] * N_KEPT,
        scratch_shapes=[
            pltpu.VMEM(BLOCKS, BF16),
            pltpu.VMEM((4, 16, 768), BF16),
            pltpu.VMEM((2, rows, 768), BF16),
            pltpu.VMEM((LEN, 128), BF16),
            pltpu.VMEM((rows, 1), F32),
            pltpu.VMEM((8, 768), F32),
            *forward_scratch(rows),
            pltpu.SemaphoreType.DMA((4, 2, 3)),
            pltpu.SemaphoreType.DMA((4, 4)),
            pltpu.SemaphoreType.DMA((3, 4, 5)),
            pltpu.SemaphoreType.DMA((3, 4, 5)),
            pltpu.SemaphoreType.DMA,
            pltpu.SemaphoreType.DMA,
            pltpu.SemaphoreType.DMA((3,)),
        ],
        compiler_params=pltpu.CompilerParams(
            collective_id=0, has_side_effects=True, vmem_limit_bytes=VMEM_LIMIT
        ),
    )(*ins)
    return blocks, probs, frames, masked, kept


def run_forward_alone(rows, *ins):
    probs = jax.ShapeDtypeStruct((12, LEN, rows), BF16)
    frames = jax.ShapeDtypeStruct((rows, 768), BF16)
    probs, frames, *kept = pl.pallas_call(
        forward_alone,
        name="forward",
        out_shape=[probs, frames, *forward_outs(rows)],
        in_specs=[hbm()] + [vmem()] * 12,
        out_specs=[hbm(), vmem()] + [hbm()] * N_KEPT,
        scratch_shapes=[pltpu.VMEM(BLOCKS, BF16), pltpu.VMEM((8, 768), F32), *forward_scratch(rows), pltpu.SemaphoreType.DMA],
        compiler_params=pltpu.CompilerParams(vmem_limit_bytes=VMEM_LIMIT),
    )(*ins)
    return probs, frames, kept


def chunk_at(n):
    return (2 - n % 2, n // 2) if n < 8 else (0, n - 8)


class Scatter:
    def __init__(self, at, grads, core_in, first_in, second_in, z_in, out, send, recv, z_send, z_recv):
        self.at, self.grads, self.out = at, grads, out
        self.core_in, self.first_in, self.second_in, self.z_in = core_in, first_in, second_in, z_in
        self.send, self.recv, self.z_send, self.z_recv = send, recv, z_send, z_recv

    def copy(self, kind, m, which):
        at, grads = self.at, self.grads.at[kind, m]
        x, y, c = at.x, at.y, at.c
        low, high = pl.ds(0, 48), pl.ds(48, 48)
        src, dst, device = {
            0: lambda: (grads.at[:, :, 1 - c], self.core_in.at[kind, m], at.core),
            1: lambda: (grads.at[:, 1 - x, c, low], self.first_in.at[kind, m, 0], at.across_x),
            2: lambda: (grads.at[1 - y, :, c, high], self.first_in.at[kind, m, 1], at.across_y),
            3: lambda: (grads.at[1 - y, x, c, low], self.second_in.at[kind, m, 0], at.across_y),
            4: lambda: (grads.at[y, 1 - x, c, high], self.second_in.at[kind, m, 1], at.across_x),
        }[which]()
        return remote(src, dst, self.send.at[kind, m, which], self.recv.at[kind, m, which], device)

    def add(self, ref, got):
        ref[...] = (ref[...].astype(F32) + got[...].astype(F32)).astype(BF16)

    def begin(self, kind, m):
        self.copy(kind, m, 0).start()

    def first(self, kind, m):
        at, grads = self.at, self.grads.at[kind, m]
        self.copy(kind, m, 0).wait_recv()
        for y in range(2):
            for x in range(2):
                self.add(grads.at[y, x, at.c], self.core_in.at[kind, m, y, x])
        self.copy(kind, m, 1).start()
        self.copy(kind, m, 2).start()

    def second(self, kind, m):
        at, grads = self.at, self.grads.at[kind, m]
        low, high = pl.ds(0, 48), pl.ds(48, 48)
        self.copy(kind, m, 1).wait_recv()
        for y in range(2):
            self.add(grads.at[y, at.x, at.c, low], self.first_in.at[kind, m, 0, y])
        self.copy(kind, m, 3).start()
        self.copy(kind, m, 2).wait_recv()
        for x in range(2):
            self.add(grads.at[at.y, x, at.c, high], self.first_in.at[kind, m, 1, x])
        self.copy(kind, m, 4).start()

    def third(self, kind, m):
        at = self.at
        grads = self.grads.at[kind, m, at.y, at.x, at.c]
        self.copy(kind, m, 3).wait_recv()
        self.add(grads.at[pl.ds(0, 48)], self.second_in.at[kind, m, 0])
        self.copy(kind, m, 4).wait_recv()
        self.add(grads.at[pl.ds(48, 48)], self.second_in.at[kind, m, 1])
        self.z_start(kind, m)

    def z_copy(self, kind, m, direction):
        at = self.at
        src = self.grads.at[kind, m, at.y, at.x, at.c]
        device = at.right if direction == 0 else at.left
        slot = m if direction == 0 else jnp.where(m == at.z - 1, 4, m)
        return remote(src, self.z_in.at[kind, slot], self.z_send.at[kind, m], self.z_recv.at[kind, slot], device)

    def z_landed(self, kind, m, slot, direction):
        at = self.at
        src = self.grads.at[kind, m, at.y, at.x, at.c]
        device = at.right if direction == 0 else at.left
        return remote(src, self.z_in.at[kind, slot], self.z_send.at[kind, m], self.z_recv.at[kind, slot], device)

    def relay(self, kind, m, direction):
        at = self.at
        self.z_landed(kind, m, m, direction).wait_recv()
        self.add(self.grads.at[kind, m, at.y, at.x, at.c], self.z_in.at[kind, m])
        self.z_copy(kind, m, direction).start()

    def z_start(self, kind, m):
        z = self.at.z
        if m > 0:
            pl.when(z == 0)(lambda: self.z_copy(kind, m, 0).start())
        if m < 3:
            pl.when(z == 3)(lambda: self.z_copy(kind, m, 1).start())

    def z_one(self, kind, m):
        z = self.at.z
        if m > 1:
            pl.when(z == 1)(lambda: self.relay(kind, m, 0))
        else:
            pl.when(z == 2)(lambda: self.relay(kind, m, 1))

    def z_two(self, kind, m):
        z = self.at.z
        if m == 3:
            pl.when(z == 2)(lambda: self.relay(kind, m, 0))
        if m == 0:
            pl.when(z == 1)(lambda: self.relay(kind, m, 1))

    def finish(self, kind):
        at, z = self.at, self.at.z
        self.out[kind] = self.grads[kind, z, at.y, at.x, at.c].astype(F32)

        @pl.when(z > 0)
        def _():
            self.z_landed(kind, z, z, 0).wait_recv()
            self.out[kind] += self.z_in[kind, z].astype(F32)

        @pl.when(z < 3)
        def _():
            self.z_landed(kind, z, 4, 1).wait_recv()
            self.out[kind] += self.z_in[kind, 4].astype(F32)

    def run(self, **steps):
        for name, places in steps.items():
            for n in places:
                getattr(self, name)(*chunk_at(n))

    def drain(self):
        z = self.at.z
        for kind in range(3):

            def of_index(m, _, kind=kind):
                for which in range(5):
                    self.copy(kind, m, which).wait_send()
                pl.when(m > z)(lambda: self.z_copy(kind, m, 0).wait_send())
                pl.when(m < z)(lambda: self.z_copy(kind, m, 1).wait_send())
                return 0

            lax.fori_loop(0, 4, of_index, 0)


class Totals:
    def __init__(self, at, rows, got, send, recv):
        self.rows, self.got, self.send, self.recv = rows, got, send, recv
        self.partners = (at.core, at.across_x, at.across_y, at.mate, at.far)

    def copy(self, stage):
        return remote(
            self.rows.at[stage], self.got.at[stage], self.send.at[stage], self.recv.at[stage], self.partners[stage]
        )

    def start(self, stage):
        self.copy(stage).start()

    def finish(self, stage):
        self.copy(stage).wait()
        self.rows[stage + 1] = self.rows[stage] + self.got[stage]


def backward_compute(
    blocks_hbm,
    probs_hbm,
    acted_hbm,
    slope_hbm,
    recip_ref,
    headout_hbm,
    xt_hbm,
    qm_hbm,
    kt_hbm,
    v_hbm,
    att_hbm,
    n1t_hbm,
    n1_hbm,
    rs1_ref,
    gb2_hbm,
    gb2t_hbm,
    g2_hbm,
    sums_ref,
    masked_ref,
    gain_ref,
    grads,
    rows_ref,
    weight,
    weight_sem,
    acts,
    acts_sem,
    probs,
    probs_sem,
    gb1,
    gb1t,
    grad_one,
    parts,
    g2_ref,
    state_sem,
    gb2_ref,
    gb2t_ref,
    n1t_ref,
    xt_ref,
    headout_ref,
    qm_ref,
    kt_ref,
    v_ref,
    att_ref,
    head_sem,
    own,
    sides,
    shifts,
    shares,
    hooks,
):
    rows = g2_ref.shape[0]
    g2_load = pltpu.make_async_copy(g2_hbm, g2_ref, state_sem.at[0])
    n1_load = pltpu.make_async_copy(n1_hbm, grad_one, state_sem.at[1])
    gb2_load = pltpu.make_async_copy(gb2_hbm, gb2_ref, state_sem.at[2])
    gb2t_load = pltpu.make_async_copy(gb2t_hbm, gb2t_ref, state_sem.at[3])
    n1t_load = pltpu.make_async_copy(n1t_hbm, n1t_ref, state_sem.at[4])
    xt_load = pltpu.make_async_copy(xt_hbm, xt_ref, state_sem.at[5])

    def head_loads(m, slot, side):
        three, two, half = pl.ds(3 * m, 3), pl.ds(2 * m, 2), pl.ds(side * rows, rows)
        pairs = [
            (qm_hbm.at[three], qm_ref.at[slot]),
            (kt_hbm.at[two, :, half], kt_ref.at[slot]),
            (v_hbm.at[two, half], v_ref.at[slot]),
            (headout_hbm.at[three], headout_ref.at[slot]) if side else (att_hbm.at[m], att_ref.at[slot]),
        ]
        return [
            pltpu.make_async_copy(src, dst, head_sem.at[slot, i if i < 3 else 4 - side])
            for i, (src, dst) in enumerate(pairs)
        ]

    def weight_load(kind, m, slot):
        return pltpu.make_async_copy(blocks_hbm.at[kind, m], weight.at[slot], weight_sem.at[slot])

    def act_loads(m, slot):
        return (
            pltpu.make_async_copy(acted_hbm.at[m], acts.at[slot, 0], acts_sem.at[slot, 0]),
            pltpu.make_async_copy(slope_hbm.at[m], acts.at[slot, 1], acts_sem.at[slot, 1]),
        )

    def probs_load(head, side, slot):
        return pltpu.make_async_copy(
            probs_hbm.at[head, pl.ds(side * rows, rows)], probs.at[slot], probs_sem.at[slot]
        )

    def feed_loads(m, slot):
        return (weight_load(DOWN, m, 2 * slot), weight_load(UP, m, 2 * slot + 1), *act_loads(m, slot))

    def begin(copies):
        for copy in copies:
            copy.start()

    def finish(copies):
        for copy in copies:
            copy.wait()

    def block(slot, low=0, width=768):
        return weight[slot, :, :, :, :, pl.ds(low, width)].reshape(768, width)

    def put(kind, m, value, low=0):
        width = value.shape[1]
        grads[kind, m, :, :, :, :, pl.ds(low, width)] = value.astype(BF16).reshape(2, 2, 2, 96, width)

    begin((gb2_load,))
    begin(feed_loads(0, 0))
    begin((gb2t_load, n1t_load, g2_load, n1_load, xt_load))
    begin(head_loads(0, 0, 1))
    for j in range(3):
        probs_load(j, 1, j).start()
    parts[...] = jnp.zeros_like(parts)
    finish((gb2_load, gb2t_load, n1t_load, g2_load))

    def feed(m, _):
        slot = lax.rem(m, 2)
        pl.when(m < 3)(lambda: begin(feed_loads(m + 1, 1 - slot)))
        finish(feed_loads(m, slot))
        grad_acted = dot(gb2_ref[...], block(2 * slot))
        grad_pre = (grad_acted * acts[slot, 1].astype(F32)).astype(BF16)
        acts[slot, 1] = grad_pre
        hooks.after("grad_pre", m)
        parts[m, 0:1, :] = jnp.sum(grad_pre.astype(F32), axis=0, keepdims=True)
        put(DOWN, m, dot(gb2t_ref[...], acts[slot, 0]))
        hooks.ready(DOWN, m)
        hooks.after("down", m)
        put(UP, m, dot(n1t_ref[...], acts[slot, 1]))
        hooks.ready(UP, m)
        g2_ref[...] += dot(acts[slot, 1], block(2 * slot + 1), (1, 1))
        hooks.after("feed", m)
        return 0

    lax.fori_loop(0, 4, feed, 0)
    for m in range(4):
        weight_load(ATT, m, m).start()

    chunk = 64

    def norm_back(i, sums):
        r = pl.ds(pl.multiple_of(i * chunk, chunk), chunk)
        grad = g2_ref[r, :]
        unit = grad_one[r, :]
        scaled = grad * gain
        grad_in = (
            scaled
            - jnp.mean(scaled, axis=1, keepdims=True)
            - unit * jnp.mean(scaled * unit, axis=1, keepdims=True)
        ) * rs1_ref[r, :]
        grad_one[r, :] = grad_in
        gb1[r, :] = grad_in.astype(BF16)
        return (
            sums[0] + jnp.sum(grad_in, axis=0, keepdims=True),
            sums[1] + jnp.sum(grad * unit, axis=0, keepdims=True),
            sums[2] + jnp.sum(grad, axis=0, keepdims=True),
        )

    zero = jnp.zeros((1, 768), F32)
    finish((n1_load, xt_load))
    gain = gain_ref[...].astype(F32).reshape(1, 768)
    sums = lax.fori_loop(0, rows // chunk, norm_back, (zero, zero, zero))
    rows_ref[0, 0:1, :] = sums[0]
    rows_ref[0, 1:2, :] = sums_ref[0:1, :]
    rows_ref[0, 2:3, :] = sums[1]
    rows_ref[0, 3:4, :] = sums[2]
    rows_ref[0, 4:5, :] = sums_ref[1:2, :]
    rows_ref[0, 5:6, :] = sums_ref[2:3, :]
    gb1t[...] = gb1[...].T
    hooks.after("norm")
    g2_ref[...] = jnp.zeros_like(g2_ref)

    def wide(m, j, side):
        zeros = jnp.zeros((64, rows), BF16)
        return jnp.concatenate([zeros, side] if j == 1 else [side, zeros], axis=0)

    def half_back(slot, m, j, side, shift, next_load):
        t = j // 2
        side = wide(m, j, side)
        probs_load(0, 0, j).wait()
        weights = probs[j]
        grad_weights = dot(v_ref[slot, t], side)
        grad_scores = (weights.astype(F32) * (grad_weights - shift)).astype(BF16)
        grad_v = dot(weights, side.T)
        next_load()
        grad_k = dot(grad_scores, qm_ref[slot, j])
        lane = 0 if j == 0 else 64
        grad_q = dot(kt_ref[slot, t, lane : lane + 64, :], grad_scores)
        return grad_k, grad_v, grad_q

    def join(parts):
        return [parts[0] + parts[1], parts[2]]

    def back_other(m, _):
        slot = lax.rem(m, 2)
        pl.when(m < 3)(lambda: begin(head_loads(m + 1, 1 - slot, 1)))
        pl.when(m == 3)(lambda: begin(head_loads(0, 0, 0)))
        weight_load(ATT, m, m).wait()
        finish(head_loads(m, slot, 1))
        grad_att_t = dot(gb1[...], block(m, 512, 256)).T
        grads_k, grads_v = [], []
        for j in range(3):
            head = 3 * m + j
            place = (128, 192, 64)[j]
            grad_att = grad_att_t[place : place + 64, :]
            own = (grad_att * recip_ref[head, 0:1, :]).astype(BF16)
            other = (grad_att * recip_ref[head, 1:2, :]).astype(BF16)
            row_sum = jnp.sum(
                own.astype(F32) * headout_ref[slot, j, 0] + other.astype(F32) * headout_ref[slot, j, 1],
                axis=0,
                keepdims=True,
            )
            sides[head] = own
            shifts[head, 0:1, :] = row_sum * recip_ref[head, 0:1, :]

            def next_load(j=j, head=head):
                pl.when(m < 3)(lambda: probs_load(head + 3, 1, j).start())
                pl.when(m == 3)(lambda: probs_load(j, 0, j).start())

            grad_k, grad_v, grad_q = half_back(
                slot, m, j, other, row_sum * recip_ref[head, 1:2, :], next_load
            )
            grads_k.append(grad_k)
            grads_v.append(grad_v)
            shares[head] = grad_q
            hooks.after(f"other{j}", m)
        grads_k, grads_v = join(grads_k), join(grads_v)
        tile = acts.at[m // 2, lax.rem(m, 2)]
        tile[:, 128:256] = grads_k[0].astype(BF16)
        tile[:, 256:384] = grads_v[0].astype(BF16)
        tile[:, 384:512] = grads_k[1].astype(BF16)
        tile[:, 512:640] = grads_v[1].astype(BF16)
        parts[4 + m, 0:1, 128:640] = jnp.sum(tile[:, 128:640].astype(F32), axis=0, keepdims=True)
        g2_ref[...] += dot(tile[:, 128:640], block(m, 128, 512), (1, 1))
        return 0

    lax.fori_loop(0, 4, back_other, 0)

    def fill_other(i, total):
        r = pl.ds(pl.multiple_of(i * chunk, chunk), chunk)
        other = g2_ref[r, :]
        gb1[r, :] = other.astype(BF16)
        return total + jnp.sum(other * masked_ref[1, r, :], axis=0, keepdims=True)

    fill = lax.fori_loop(0, rows // chunk, fill_other, zero)
    hooks.after("mate")

    def back_own(m, _):
        slot = lax.rem(m, 2)
        pl.when(m < 3)(lambda: begin(head_loads(m + 1, 1 - slot, 0)))
        finish(head_loads(m, slot, 0))
        grads_k, grads_v, grads_q = [], [], []
        for j in range(3):
            head = 3 * m + j

            def next_load(j=j, head=head):
                pl.when(m < 3)(lambda: probs_load(head + 3, 0, j).start())

            grad_k, grad_v, grad_q = half_back(slot, m, j, sides[head], shifts[head, 0:1, :], next_load)
            grads_k.append(grad_k)
            grads_v.append(grad_v)
            grads_q.append((grad_q + shares[head]) * SCALE)
            hooks.after(f"own{j}", m)
        grads_k, grads_v = join(grads_k), join(grads_v)
        single = jnp.concatenate([grads_q[2], jnp.zeros((64, rows), F32)], axis=0).T
        own[:, 0:128] = jnp.concatenate(grads_q[:2], axis=0).T.astype(BF16)
        own[:, 128:256] = grads_k[0].astype(BF16)
        own[:, 256:384] = grads_v[0].astype(BF16)
        own[:, 384:512] = (grads_k[1] + single).astype(BF16)
        own[:, 512:640] = grads_v[1].astype(BF16)
        parts[4 + m, 0:1, 0:PROJ] += jnp.sum(own[...].astype(F32), axis=0, keepdims=True)
        other = acts[m // 2, lax.rem(m, 2), :, 128:640]
        grad_proj = dot(xt_ref[0], own[...])
        grad_other = dot(xt_ref[1], other)
        grad_out_w = dot(gb1t[...], att_ref[slot])
        put(ATT, m, grad_proj[:, :128], 0)
        put(ATT, m, grad_proj[:, 128:512] + grad_other[:, :384], 128)
        put(ATT, m, grad_proj[:, 512:] + grad_other[:, 384:] + grad_out_w[:, :128], 512)
        put(ATT, m, grad_out_w[:, 128:], 640)
        hooks.ready(ATT, m)
        grad_one[...] += dot(own[...], block(m, 0, PROJ), (1, 1))
        hooks.after("own", m)
        return 0

    lax.fori_loop(0, 4, back_own, 0)

    def fill_own(i, total):
        r = pl.ds(pl.multiple_of(i * chunk, chunk), chunk)
        return total + jnp.sum(grad_one[r, :] * masked_ref[0, r, :], axis=0, keepdims=True)

    rows_ref[0, 6:7, :] = lax.fori_loop(0, rows // chunk, fill_own, fill)
    rows_ref[0, 7:8, :] = zero
    for row in range(8):
        rows_ref[0, 8 + row : 9 + row, :] = parts[row, 0:1, :]


def finish_frames(grad_one, got, masked_ref, frames_ref):
    chunk = 64

    def body(i, _):
        r = pl.ds(pl.multiple_of(i * chunk, chunk), chunk)
        total = grad_one[r, :] + got[r, :].astype(F32)
        frames_ref[r, :] = jnp.where(masked_ref[0, r, :] > 0, 0.0, total).astype(BF16)
        return 0

    lax.fori_loop(0, grad_one.shape[0] // chunk, body, 0)


class NoScatter:
    def after(self, point, m=0):
        pass

    def ready(self, kind, m):
        pass


class ScatterHooks:
    PLAN = {
        ("feed", 0): dict(first=(0,)),
        ("grad_pre", 1): dict(first=(1,)),
        ("feed", 1): dict(second=(0,), first=(2,)),
        ("down", 2): dict(second=(1,), first=(3,)),
        ("feed", 3): dict(second=(2,), first=(4,), third=(0,)),
        ("norm", 0): dict(second=(3,), first=(5,), third=(1,)),
        ("other1", 1): dict(second=(4,), first=(6,), third=(2,), z_one=(0,)),
        ("other1", 2): dict(second=(5,), first=(7,), third=(3,), z_one=(1,)),
        ("other2", 3): dict(second=(6,), third=(4,), z_one=(2,), z_two=(0,)),
        ("mate", 0): dict(swap=(0,)),
        ("own0", 0): dict(swap=(1,)),
        ("own", 0): dict(second=(7,), third=(5,), z_one=(3,), z_two=(1,), swap=(2,)),
        ("own0", 1): dict(first=(8,)),
        ("own1", 1): dict(swap=(3,)),
        ("own", 1): dict(second=(8,), third=(6, 7), z_one=(4,), z_two=(2,)),
        ("own0", 2): dict(first=(9,)),
        ("own", 2): dict(second=(9,), third=(8,), z_one=(5,), z_two=(3,)),
        ("own0", 3): dict(first=(10,)),
        ("own", 3): dict(second=(10,), third=(9,), z_one=(6, 7), z_two=(4, 5)),
    }

    def __init__(self, scatter, swaps):
        self.scatter, self.swaps = scatter, swaps

    def ready(self, kind, m):
        self.scatter.begin(kind, m)

    def run(self, swap=(), **steps):
        self.scatter.run(**steps)
        for piece in swap:
            self.swaps[piece].start()

    def after(self, point, m=0):
        for (name, index), steps in self.PLAN.items():
            if name == point:
                if isinstance(m, int):
                    self.run(**steps)
                else:
                    pl.when(m == index)(functools.partial(self.run, **steps))


N_BACKWARD_INS = 20
N_BACKWARD_SCRATCH = 28


def backward_linked(*refs):
    ins = refs[:N_BACKWARD_INS]
    out_ref, rows_out, frames_ref = refs[N_BACKWARD_INS : N_BACKWARD_INS + 3]
    scratch = refs[N_BACKWARD_INS + 3 :]
    scratch, links = scratch[:N_BACKWARD_SCRATCH], scratch[N_BACKWARD_SCRATCH:]
    grads, rows_ref, gb1, grad_one = scratch[0], scratch[1], scratch[8], scratch[10]
    core_in, first_in, second_in, z_in, rows_in, mate_in = links[:6]
    send, recv, z_send, z_recv, t_send, t_recv, m_send, m_recv = links[6:]
    at = Place()
    at.greet(True)
    scatter = Scatter(at, grads, core_in, first_in, second_in, z_in, out_ref, send, recv, z_send, z_recv)
    totals = Totals(at, rows_ref, rows_in, t_send, t_recv)
    piece = gb1.shape[0] // 4
    swaps = [
        remote(
            gb1.at[pl.ds(i * piece, piece)], mate_in.at[pl.ds(i * piece, piece)], m_send.at[i], m_recv.at[i], at.mate
        )
        for i in range(4)
    ]
    backward_compute(*ins, *scratch, ScatterHooks(scatter, swaps))
    totals.start(0)
    scatter.run(first=(11,))
    totals.finish(0)
    totals.start(1)
    scatter.run(third=(10,), z_one=(8,), z_two=(6,))
    scatter.run(second=(11,))
    totals.finish(1)
    totals.start(2)
    scatter.run(z_one=(9,), z_two=(7,))
    scatter.run(third=(11,))
    totals.finish(2)
    totals.start(3)
    scatter.finish(DOWN)
    scatter.finish(UP)
    scatter.run(z_one=(10,), z_two=(8,))
    totals.finish(3)
    totals.start(4)
    scatter.run(z_one=(11,), z_two=(9, 10))
    for swap in swaps:
        swap.wait()
    finish_frames(grad_one, mate_in, ins[18], frames_ref)
    totals.finish(4)
    rows_out[...] = rows_ref[5]
    scatter.run(z_two=(11,))
    scatter.finish(ATT)
    scatter.drain()


def backward_alone(*refs):
    ins = refs[:N_BACKWARD_INS]
    grads_out, rows_out, mate_out, grad_one_out = refs[N_BACKWARD_INS : N_BACKWARD_INS + 4]
    scratch = refs[N_BACKWARD_INS + 4 :]
    *scratch, keep_sem = scratch
    grads, rows_ref, gb1, grad_one = scratch[0], scratch[1], scratch[8], scratch[10]
    backward_compute(*ins, *scratch, NoScatter())
    keep = pltpu.make_async_copy(grads, grads_out, keep_sem)
    keep.start()
    rows_out[...] = rows_ref[0]
    mate_out[...] = gb1[...]
    grad_one_out[...] = grad_one[...]
    keep.wait()


def backward_scratch(rows):
    return [
        pltpu.VMEM(BLOCKS, BF16),
        pltpu.VMEM((6, 16, 768), F32),
        pltpu.VMEM((4, *BLOCKS[2:]), BF16),
        pltpu.SemaphoreType.DMA((4,)),
        pltpu.VMEM((2, 2, rows, 768), BF16),
        pltpu.SemaphoreType.DMA((2, 2)),
        pltpu.VMEM((3, rows, rows), BF16),
        pltpu.SemaphoreType.DMA((3,)),
        pltpu.VMEM((rows, 768), BF16),
        pltpu.VMEM((768, rows), BF16),
        pltpu.VMEM((rows, 768), F32),
        pltpu.VMEM((8, 8, 768), F32),
        pltpu.VMEM((rows, 768), F32),
        pltpu.SemaphoreType.DMA((6,)),
        pltpu.VMEM((rows, 768), BF16),
        pltpu.VMEM((768, rows), BF16),
        pltpu.VMEM((768, rows), BF16),
        pltpu.VMEM((2, 768, rows), BF16),
        pltpu.VMEM((2, 3, 2, 64, rows), F32),
        pltpu.VMEM((2, 3, rows, 128), BF16),
        pltpu.VMEM((2, 2, 128, rows), BF16),
        pltpu.VMEM((2, 2, rows, 128), BF16),
        pltpu.VMEM((2, rows, 256), BF16),
        pltpu.SemaphoreType.DMA((2, 5)),
        pltpu.VMEM((rows, PROJ), BF16),
        pltpu.VMEM((12, 64, rows), BF16),
        pltpu.VMEM((12, 8, rows), F32),
        pltpu.VMEM((12, 64, rows), F32),
    ]


def run_backward(linked, blocks, probs, kept, masked, gain):
    recip, headout, xt, qm, kt, v, att, acted, slope, n1t, n1, rs1, gb2, gb2t, g2, sums = kept
    rows = gb2.shape[0]
    ins = (
        blocks, probs, acted, slope, recip, headout, xt, qm, kt, v, att, n1t, n1, rs1, gb2, gb2t, g2, sums, masked, gain
    )
    in_specs = [vmem() if i in (4, 13, 17, 18, 19) else hbm() for i in range(20)]
    if linked:
        return pl.pallas_call(
            backward_linked,
            name="backward",
            out_shape=[
                jax.ShapeDtypeStruct((3, 96, 768), F32),
                jax.ShapeDtypeStruct((16, 768), F32),
                jax.ShapeDtypeStruct((rows, 768), BF16),
            ],
            in_specs=in_specs,
            out_specs=[vmem()] * 3,
            scratch_shapes=[
                *backward_scratch(rows),
                pltpu.VMEM((3, 4, 2, 2, 96, 768), BF16),
                pltpu.VMEM((3, 4, 2, 2, 48, 768), BF16),
                pltpu.VMEM((3, 4, 2, 48, 768), BF16),
                pltpu.VMEM((3, 5, 96, 768), BF16),
                pltpu.VMEM((5, 16, 768), F32),
                pltpu.VMEM((rows, 768), BF16),
                pltpu.SemaphoreType.DMA((3, 4, 5)),
                pltpu.SemaphoreType.DMA((3, 4, 5)),
                pltpu.SemaphoreType.DMA((3, 4)),
                pltpu.SemaphoreType.DMA((3, 5)),
                pltpu.SemaphoreType.DMA((5,)),
                pltpu.SemaphoreType.DMA((5,)),
                pltpu.SemaphoreType.DMA((4,)),
                pltpu.SemaphoreType.DMA((4,)),
            ],
            compiler_params=pltpu.CompilerParams(
                collective_id=1, has_side_effects=True, vmem_limit_bytes=VMEM_LIMIT
            ),
        )(*ins)
    return pl.pallas_call(
        backward_alone,
        name="backward",
        out_shape=[
            jax.ShapeDtypeStruct(BLOCKS, BF16),
            jax.ShapeDtypeStruct((16, 768), F32),
            jax.ShapeDtypeStruct((rows, 768), BF16),
            jax.ShapeDtypeStruct((rows, 768), F32),
        ],
        in_specs=in_specs,
        out_specs=[hbm()] + [vmem()] * 3,
        scratch_shapes=[*backward_scratch(rows), pltpu.SemaphoreType.DMA],
        compiler_params=pltpu.CompilerParams(vmem_limit_bytes=VMEM_LIMIT),
    )(*ins)


def finish_kernel(parts, grads, totals, out_in, frames_in, out, frames, *outs):
    n_dp, n_mp = parts
    query, key, value, out_w, up, down, query_bias, value_bias, up_bias, *vectors = outs
    out[...] = out_in[...]
    frames[...] = frames_in[...]
    att = grads[0]
    query[...] = jnp.concatenate([att[:, 0:128], att[:, 384:448]], axis=1)
    key[...] = jnp.concatenate([att[:, 128:256], att[:, 448:512]], axis=1)
    value[...] = jnp.concatenate([att[:, 256:384], att[:, 512:576]], axis=1)
    out_w[...] = jnp.concatenate([att[:, 640:768], att[:, 576:640]], axis=1).T
    up[...] = grads[1]
    down[...] = grads[2]
    dp, z = lax.axis_index("dp"), lax.axis_index("mp")
    rows = totals[...]
    row_at = lax.broadcasted_iota(jnp.int32, rows.shape, 0)

    def shifted(block, by):
        return pltpu.roll(block, lax.rem(768 - by, 768), 1)

    def row_of(index):
        return jnp.broadcast_to(jnp.sum(jnp.where(row_at == index, rows, 0.0), axis=0, keepdims=True), (8, 768))

    part = 768 // (n_dp * n_mp)
    mine = shifted(rows[0:8], (dp * n_mp + z) * part)
    for i, ref in enumerate(vectors):
        ref[...] = mine[i : i + 1, :part]
    step = HEAD_DIM // n_dp
    heads = shifted(row_of(12 + z), dp * step)
    for head, (q_lane, v_lane) in enumerate(((0, 256), (64, 320), (384, 512))):
        query_bias[head : head + 1, :] = heads[0:1, q_lane : q_lane + step]
        value_bias[head : head + 1, :] = heads[0:1, v_lane : v_lane + step]
    ups = shifted(row_of(8 + z), dp * 2 * step)
    for i in range(6):
        up_bias[i : i + 1, :] = ups[0:1, 128 * i : 128 * i + 2 * step]


def run_finish(n_dp, n_mp, grads, totals, out, frames):
    def of(shape, dtype=F32):
        return jax.ShapeDtypeStruct(shape, dtype)

    d, step, part = grads.shape[1], HEAD_DIM // n_dp, 768 // (n_dp * n_mp)
    *outs, = pl.pallas_call(
        functools.partial(finish_kernel, (n_dp, n_mp)),
        name="finish",
        out_shape=[
            of(out.shape, BF16), of(frames.shape, BF16), of((d, 192)), of((d, 192)), of((d, 192)), of((192, d)),
            of((d, 768)), of((d, 768)), of((3, step)), of((3, step)), of((6, 2 * step)), *[of((1, part))] * 7,
        ],
        in_specs=[vmem()] * 4,
        out_specs=[vmem()] * 18,
        compiler_params=pltpu.CompilerParams(vmem_limit_bytes=VMEM_LIMIT),
    )(grads, totals, out, frames)
    return (*outs[:7], outs[7].T, *outs[8:11], *(row.reshape(part) for row in outs[11:]))


def shards(
    linked,
    frames,
    lengths,
    span_starts,
    cotangent,
    query_weight,
    key_weight,
    value_weight,
    out_weight,
    up_weight,
    down_weight,
    query_bias,
    value_bias,
    up_bias,
    out_bias,
    down_bias,
    first_gain,
    first_shift,
    second_gain,
    second_shift,
    mask_vector,
):
    rows = frames.shape[0]
    n_dp = 768 // query_weight.shape[0]
    n_mp = 768 // query_weight.shape[1]
    vecs = (out_bias, down_bias, first_gain, first_shift, second_gain, second_shift, mask_vector)
    if linked:
        blocks, probs, out, masked, kept = run_forward_linked(
            rows, lengths, span_starts, frames, cotangent, query_weight, key_weight, value_weight, out_weight,
            up_weight, down_weight.T, query_bias, value_bias, up_bias, *vecs,
        )
        grads, totals, grad_frames = run_backward(True, blocks, probs, kept, masked, first_gain)
        return run_finish(n_dp, n_mp, grads, totals, out, grad_frames)
    z = lax.axis_index("mp")
    half = z % 2
    length = lax.dynamic_index_in_dim(lengths, z // 2, keepdims=False)
    starts = lax.dynamic_index_in_dim(span_starts, z // 2, keepdims=False)
    slots = (jnp.arange(LEN, dtype=jnp.int32) + half * rows) % LEN
    valid = slots < length
    masked = jnp.any((slots[:, None] >= starts[None, :]) & (slots[:, None] < starts[None, :] + SPAN), axis=1)
    keybias = jnp.where(
        (jnp.arange(128) == 0)[None, :] & ~valid[:, None], jnp.float32(NEGATIVE), 0.0
    ).astype(BF16)
    valid_rows = valid[:rows].astype(F32)[:, None]
    masked_rows = masked.astype(F32).reshape(2, rows, 1)
    x = jnp.where(masked[:rows, None], mask_vector[None, :], frames)
    pack = jnp.stack(pack_weights(query_weight, key_weight, value_weight, out_weight.T, up_weight, down_weight.T))
    bias = pack_biases(query_bias, value_bias, up_bias)
    mates = [(0, 1), (1, 0), (2, 3), (3, 2)]
    blocks = lax.all_gather(lax.all_gather(pack, "dp", axis=1, tiled=True), "mp", axis=1).reshape(BLOCKS)
    biases = lax.all_gather(bias, "mp", axis=0)
    both = jnp.stack([x, lax.ppermute(x, "mp", mates)])
    probs, out, kept = run_forward_alone(rows, blocks, biases, both, keybias, valid_rows, cotangent, *vecs)
    grads, totals, mate, grad_one = run_backward(False, blocks, probs, kept, masked_rows, first_gain)
    grads = grads.reshape(3, 4, 768, 768).astype(F32)
    grads = lax.psum_scatter(grads, "mp", scatter_dimension=1, tiled=False)
    grads = lax.psum_scatter(grads, "dp", scatter_dimension=1, tiled=True)
    totals = lax.psum(totals, ("dp", "mp"))
    grad_frames = grad_one + lax.ppermute(mate, "mp", mates).astype(F32)
    grad_frames = jnp.where(masked[:rows, None], 0.0, grad_frames).astype(BF16)
    return run_finish(n_dp, n_mp, grads, totals, out, grad_frames)


def solution(mesh):
    linked = mesh.shape["dp"] == 8 and mesh.shape["mp"] == 4
    split = P(("dp", "mp"))
    return jax.shard_map(
        functools.partial(shards, linked),
        mesh=mesh,
        in_specs=(
            P(("dp", "mp"), None),
            P("dp"),
            P("dp", None),
            P(("dp", "mp"), None),
            P("dp", "mp"),
            P("dp", "mp"),
            P("dp", "mp"),
            P("mp", "dp"),
            P("dp", "mp"),
            P("mp", "dp"),
            P("mp", None),
            P("mp", None),
            P("mp", None),
            *([P()] * 7),
        ),
        out_specs=(
            P(("dp", "mp"), None),
            P(("dp", "mp"), None),
            P("dp", "mp"),
            P("dp", "mp"),
            P("dp", "mp"),
            P("mp", "dp"),
            P("dp", "mp"),
            P("mp", "dp"),
            P("mp", "dp"),
            P("mp", "dp"),
            P("mp", "dp"),
            *([split] * 7),
        ),
        check_vma=False,
    )
```

time: 256 us -> 192 us (0.75); the launches traced: 253 us -> 191 us
  Pallas kernels: 221 us -> 190 us
  local copies, waits for them, and re-layouts: 21.6 us -> 0 us
  other arithmetic: 9.14 us -> 0 us
    pallas_call x1 -> x2, Pallas kernels: 103 us -> 87.3 us  [the longest x1 83.9 us: run_forward_linked(): pl.pallas_call(forward_linked, name='forward', out_shape=[jax.ShapeDtypeS...]
    pallas_call x1, Pallas kernels: 118 us -> 103 us  [run_backward(): pl.pallas_call(backward_linked, name='backward', out_shape=[jax.ShapeDtyp...]
    slice x19 -> x0, local copies, waits for them, and re-layouts: 8.36 us -> none  [the longest x1 0.8 us: shards(): query_weight[:, :pair]]
    unnamed x25 -> x0, local copies, waits for them, and re-layouts: 4.11 us -> none
    dynamic_slice x6 -> x0, local copies, waits for them, and re-layouts: 4.07 us -> none  [the longest x1 0.77 us: shards(): row_parts = lax.dynamic_slice(totals, (0, (dp * 4 + z) * part), (7, part))]
where the time goes in v3:
time: 192 us; the launch traced here: 191 us
  Pallas kernels  190 us (99%)
    pallas_call x1, Pallas kernels, run_backward(): pl.pallas_call(backward_linked, name='backward', out_shape=[jax.ShapeDtyp...  103 us
    pallas_call x1, Pallas kernels, run_forward_linked(): pl.pallas_call(forward_linked, name='forward', out_shape=[jax.ShapeDtypeS...  83.9 us

profile of v3, /device:TPU:16, one launch (start us, length us, event | category | flops | bytes accessed | tf_op | source)
XLA Modules:
  0.0 191.2 jit_solution(847874437714084009)
XLA Ops:
  0.7 83.9 %forward.1 = (bf16[3,4,2,2,2,96,768]{6,5,4,3,2,1,0:T(8,128)(2,1)}, bf16[12,1024,512]{2,1,0:T(8,128)(2,1)}, bf16[512,768]{1,0:T(8,128)(2,1)}, f32[2,512,1]{2,1,0:...) custom-call(s32[2]{0:T(128)} %refs_0_.1, ...), custom_call_target="tpu_custom_call" | custom-call | tf_op jit(solution)/shard_map/forward/pallas_call | solution.py:677
  84.6 103.1 %backward.1 = (f32[3,96,768]{2,1,0:T(8,128)}, f32[16,768]{1,0:T(8,128)}, bf16[512,768]{1,0:T(8,128)(2,1)}) custom-call(bf16[3,4,2,2,2,96,768]{6,5,4,3,2,1,0:T(8,128)(2,1)} %get-tuple-element.59.refs_0_, bf16[12,1024,512]{2,1,0:T(8,128)(2,1)} %get-tuple-element.60.refs_1_, bf16[4,512,768]{2,1,0:T(8,128)(2,1)} %get-tuple-element.61.refs_2_, ...), custom_call_target="tpu_custom_call" | custom-call | tf_op jit(solution)/shard_map/backward/pallas_call | solution.py:1335
  187.7 3.3 %finish.1 = (bf16[512,768]{1,0:T(8,128)(2,1)}, bf16[512,768]{1,0:T(8,128)(2,1)}, f32[96,192]{1,0:T(8,128)}, f32[96,192]{1,0:T(8,128)}, f32[96,192]{1,0:T(8,128)}...) custom-call(f32[3,96,768]{2,1,0:T(8,128)} %get-tuple-element.78.grad, ...), custom_call_target="tpu_custom_call" | custom-call | tf_op jit(solution)/shard_map/finish/pallas_call | solution.py:1423

commit v4 on v3

--- a/solution.py
+++ b/solution.py
@@ -53,7 +53,7 @@
         self.mate = (self.dp, self.z + 1 - 2 * lax.rem(self.z, 2))
         self.far = (self.dp, lax.rem(self.z + 2, 4))
 
-    def greet(self, far):
+    def hello(self, far):
         barrier = pltpu.get_barrier_semaphore()
 
         def signal(device):
@@ -66,8 +66,10 @@
             signal(self.far)
         pl.when(self.z < 3)(lambda: signal(self.right))
         pl.when(self.z > 0)(lambda: signal(self.left))
+
+    def meet(self, far):
         ends = jnp.where((self.z == 0) | (self.z == 3), 1, 2)
-        pl.semaphore_wait(barrier, (4 if far else 3) + ends)
+        pl.semaphore_wait(pltpu.get_barrier_semaphore(), (4 if far else 3) + ends)
 
 
 def remote(src, dst, send, recv, device):
@@ -93,23 +95,30 @@
     def z_step(self, kind, step):
         z = self.at.z
         if step == 0:
+            pl.when((z > 0) & (z < 2))(lambda: self.z_copy(kind, z, 1, 0).start())
             pl.when(z < 3)(lambda: self.z_copy(kind, z, 0, 0).start())
-            pl.when(z > 0)(lambda: self.z_copy(kind, z, 1, 0).start())
+            pl.when(z >= 2)(lambda: self.z_copy(kind, z, 1, 0).start())
             return
 
-        @pl.when(z >= step)
-        def _():
-            self.z_copy(kind, z - step, 0, 0).wait_recv()
-            if step < 3:
-                pl.when(z < 3)(lambda: self.z_copy(kind, z - step, 0, step).start())
-            self.first(kind, z - step)
-
-        @pl.when(z + step <= 3)
-        def _():
-            self.z_copy(kind, z + step, 1, 0).wait_recv()
-            if step < 3:
-                pl.when(z > 0)(lambda: self.z_copy(kind, z + step, 1, step).start())
-            self.first(kind, z + step)
+        def from_left():
+            @pl.when(z >= step)
+            def _():
+                self.z_copy(kind, z - step, 0, 0).wait_recv()
+                if step < 3:
+                    pl.when(z < 3)(lambda: self.z_copy(kind, z - step, 0, step).start())
+                self.first(kind, z - step)
+
+        def from_right():
+            @pl.when(z + step <= 3)
+            def _():
+                self.z_copy(kind, z + step, 1, 0).wait_recv()
+                if step < 3:
+                    pl.when(z > 0)(lambda: self.z_copy(kind, z + step, 1, step).start())
+                self.first(kind, z + step)
+
+        pl.when(z < 2)(from_right)
+        from_left()
+        pl.when(z >= 2)(from_right)
 
     def plane_copy(self, kind, m, which):
         at, block = self.at, self.blocks.at[kind, m]
@@ -131,6 +140,13 @@
             return
         pl.when(z >= step)(lambda: act(z - step))
         pl.when(z + step <= 3)(lambda: act(z + step))
+
+    def order(self, step):
+        z = self.at.z
+        from_low = jnp.where(z == 1, jnp.where(step < 2, 1 - step, step), step)
+        mirrored = 3 - z
+        from_high = jnp.where(mirrored == 1, jnp.where(step < 2, 1 - step, step), step)
+        return jnp.where(z < 2, from_low, 3 - from_high)
 
     def first(self, kind, m):
         if kind < 3:
@@ -192,18 +208,19 @@
     cot_ref,
     vec_ref,
     probs_hbm,
-    out_ref,
+    out_hbm,
     outs_hbm,
     outs_ref,
     outs_sem,
     k_ref,
     vt_ref,
-    att_t,
     probs,
     probs_sem,
     total,
     low,
     stats,
+    out_ref,
+    out_sem,
     hooks,
 ):
     rows = xs.shape[1]
@@ -243,7 +260,7 @@
         for tile in range(2):
             kt_ref[2 * m + tile, :, own_rows] = k_ref[2 * m + tile, own_rows].T
             vt_ref[2 * m + tile, :, own_rows] = v_ref[2 * m + tile, own_rows].T
-        hooks.in_project(m)
+        hooks.after("project", m)
         return 0
 
     def project_other(m, _):
@@ -258,73 +275,75 @@
             vt_ref[2 * m + tile, :, other_rows] = v_ref[2 * m + tile, other_rows].T
         return 0
 
-    def attend_half(m, j, side):
-        tile, head = 2 * m + j // 2, 3 * m + j
+    def attend_half(m, side):
         half = own_rows if side == 0 else other_rows
-        keys = jnp.concatenate([k_ref[tile, half], keybias_ref[half, :]], axis=1)
-        queries = jnp.concatenate([qm_ref[head], ones_lane], axis=1)
-        scores = dot(keys, queries, (1, 1))
-        top = jnp.max(scores, axis=0, keepdims=True)
-        weights = jnp.exp(scores - top)
-        total_weight = jnp.sum(weights, axis=0, keepdims=True)
-        weights = weights.astype(BF16)
+
+        def free():
+            for j in range(3):
+                probs_copy(3 * m + j, side, j).wait()
+
         if side == 0:
-            pl.when(m > 0)(lambda: probs_copy(head, side, j).wait())
+            pl.when(m > 0)(free)
         else:
-            probs_copy(head, side, j).wait()
-        probs[j] = weights
-        probs_copy(head, side, j).start()
-        lane = 64 * (j % 2)
-        head_out = dot(vt_ref[tile, lane : lane + 64, half], weights)
-        headout_ref[head, side] = head_out
-        return top, total_weight, head_out
+            free()
+        scores, tops, sums, outs = [], [], [], []
+        for j in range(3):
+            keys = jnp.concatenate([k_ref[2 * m + j // 2, half], keybias_ref[half, :]], axis=1)
+            queries = jnp.concatenate([qm_ref[3 * m + j], ones_lane], axis=1)
+            scores.append(dot(keys, queries, (1, 1)))
+        for j in range(3):
+            top = jnp.max(scores[j], axis=0, keepdims=True)
+            weights = jnp.exp(scores[j] - top)
+            tops.append(top)
+            sums.append(jnp.sum(weights, axis=0, keepdims=True))
+            probs[j] = weights.astype(BF16)
+            lane = 64 * (j % 2)
+            outs.append(dot(vt_ref[2 * m + j // 2, lane : lane + 64, half], probs[j]))
+            headout_ref[3 * m + j, side] = outs[j]
+        return tops, sums, outs
+
+    def send_probs(m, side):
+        for j in range(3):
+            probs_copy(3 * m + j, side, j).start()
 
     def attend_own(m, _):
+        tops, sums, _ = attend_half(m, 0)
         for j in range(3):
-            top, total_weight, _ = attend_half(m, j, 0)
-            stats[3 * m + j, 0:1, :] = top
-            stats[3 * m + j, 1:2, :] = total_weight
-            hooks.in_own(m, j)
+            stats[3 * m + j, 0:1, :] = tops[j]
+            stats[3 * m + j, 1:2, :] = sums[j]
+        send_probs(m, 0)
+        hooks.after("own", m)
         return 0
 
     def attend(m, _):
-        att_t[0:64, :] = jnp.zeros((64, rows), BF16)
+        tops, sums, outs = attend_half(m, 1)
+        pieces = [jnp.zeros((64, rows), BF16), None, None, None]
         for j in range(3):
             head = 3 * m + j
-            top, total_weight, head_out = attend_half(m, j, 1)
             top_own = stats[head, 0:1, :]
-            top_all = jnp.maximum(top, top_own)
-            factor, factor_own = jnp.exp(top - top_all), jnp.exp(top_own - top_all)
-            recip = 1.0 / (factor_own * stats[head, 1:2, :] + factor * total_weight)
+            top_all = jnp.maximum(tops[j], top_own)
+            factor, factor_own = jnp.exp(tops[j] - top_all), jnp.exp(top_own - top_all)
+            recip = 1.0 / (factor_own * stats[head, 1:2, :] + factor * sums[j])
             factor, factor_own = factor * recip, factor_own * recip
-            recip_ref[head] = jnp.concatenate(
-                [factor_own, factor, jnp.zeros((6, rows), F32)], axis=0
-            )
-            place = (128, 192, 64)[j]
-            att_t[place : place + 64, :] = (headout_ref[head, 0] * factor_own + head_out * factor).astype(BF16)
-            hooks.in_attend(m, j)
-        att_ref[m] = att_t[...].T
-        part = dot(att_ref[m], block_of(blocks, ATT, m, 512, 256), (1, 1))
-
-        @pl.when(m == 0)
-        def _():
-            total[...] = part
-
-        @pl.when(m > 0)
-        def _():
-            total[...] += part
-
+            recip_ref[head] = jnp.concatenate([factor_own, factor, jnp.zeros((6, rows), F32)], axis=0)
+            pieces[(2, 3, 1)[j]] = (headout_ref[head, 0] * factor_own + outs[j] * factor).astype(BF16)
+        att_ref[m] = jnp.concatenate(pieces, axis=0).T
+        send_probs(m, 1)
+        hooks.after("other", m)
         return 0
 
-    hooks.before_project()
+    hooks.before("project")
     lax.fori_loop(0, 4, project, 0)
     lax.fori_loop(0, 4, attend_own, 0)
-    hooks.before_other()
+    hooks.before("other")
     xt_ref[1] = xs[1].T
     lax.fori_loop(0, 4, project_other, 0)
     keep(2, 3, 4, 5)
+    hooks.after("swapped")
     lax.fori_loop(0, 4, attend, 0)
     keep(0, 1, 6)
+    branch = [dot(att_ref[m], block_of(blocks, ATT, m, 512, 256), (1, 1)) for m in range(4)]
+    total[...] = (branch[0] + branch[1]) + (branch[2] + branch[3])
     for j in range(3):
         probs_copy(9 + j, 1, j).wait()
 
@@ -344,34 +363,38 @@
     lax.fori_loop(0, rows // chunk, norm_one, 0)
     n1t_ref[...] = low[...].T
     keep(9, 10, 11)
-    hooks.before_up()
+    hooks.after("norm")
+    hooks.before("feed")
 
     def feed(m, _):
         pre = dot(low[...], block_of(blocks, UP, m)) + biases[m, 1:2, :].astype(F32)
         phi = 0.5 * (1.0 + lax.erf(pre * (1.0 / math.sqrt(2.0))))
         acted_ref[m] = (pre * phi).astype(BF16)
         slope_ref[m] = (phi + pre * jnp.exp(-0.5 * pre * pre) * (1.0 / math.sqrt(2.0 * math.pi))).astype(BF16)
-        hooks.in_feed(m)
+        hooks.after("feed", m)
         return 0
 
     lax.fori_loop(0, 4, feed, 0)
     keep(7, 8)
-    hooks.before_down()
-
-    def down(m, _):
+    hooks.before("down")
+
+    def down(step, _):
+        m = hooks.order(step)
+        hooks.landed(DOWN, m)
         part = dot(acted_ref[m], block_of(blocks, DOWN, m), (1, 1))
 
-        @pl.when(m == 0)
+        @pl.when(step == 0)
         def _():
             total[...] = part
 
-        @pl.when(m > 0)
+        @pl.when(step > 0)
         def _():
             total[...] += part
 
         return 0
 
     lax.fori_loop(0, 4, down, 0)
+    hooks.all_landed()
 
     def norm_two(i, sums):
         r = pl.ds(pl.multiple_of(i * chunk, chunk), chunk)
@@ -391,6 +414,8 @@
         ) * rstd
         g2_ref[r, :] = grad_in
         gb2_ref[r, :] = grad_in.astype(BF16)
+        for i, (ref, to) in enumerate(((out_ref, out_hbm), (g2_ref, outs_hbm[14]), (gb2_ref, outs_hbm[12]))):
+            pltpu.make_async_copy(ref.at[r], to.at[r], out_sem.at[i]).start()
         return (
             sums[0] + jnp.sum(grad_in, axis=0, keepdims=True),
             sums[1] + jnp.sum(grad * unit, axis=0, keepdims=True),
@@ -400,108 +425,107 @@
     zero = jnp.zeros((1, 768), F32)
     sums = lax.fori_loop(0, rows // chunk, norm_two, (zero, zero, zero))
     sums_ref[...] = jnp.concatenate([*sums, jnp.zeros((5, 768), F32)], axis=0)
-    keep(12, 14, 15)
+    keep(15)
     gb2t_ref[...] = gb2_ref[...].T
     keep(13)
-    for copy in keeps:
-        copy.wait()
+    hooks.finish()
+    for i, copy in enumerate(keeps):
+        if i not in (12, 14):
+            copy.wait()
+    for i, (ref, to) in enumerate(((out_ref, out_hbm), (g2_ref, outs_hbm[14]), (gb2_ref, outs_hbm[12]))):
+        pltpu.make_async_copy(ref, to, out_sem.at[i]).wait()
 
 
 class NoHooks:
-    def before_project(self):
+    def after(self, point, m=0):
         pass
 
-    def in_project(self, m):
+    def before(self, point):
         pass
 
-    def before_other(self):
+    def order(self, step):
+        return step
+
+    def landed(self, kind, m):
         pass
 
-    def in_own(self, m, j):
+    def all_landed(self):
         pass
 
-    def in_attend(self, m, j):
+    def finish(self):
         pass
 
-    def before_up(self):
-        pass
-
-    def in_feed(self, m):
-        pass
-
-    def before_down(self):
-        pass
-
 
 class GatherHooks:
-    IN_PROJECT = {
-        1: (("second", UP, 0),),
-        3: (("second", DOWN, 0),),
+    MIDDLE = {
+        ("project", 1): (("z_step", DOWN, 1),),
+        ("project", 3): (("second", UP, 0), ("second", UP, 1)),
+        ("own", 0): (("second", UP, 2),),
+        ("own", 1): (("z_step", DOWN, 2), ("second", DOWN, 0), ("third", UP, 0)),
+        ("own", 3): (("second", DOWN, 1),),
+        ("swapped", 0): (("third", UP, 1),),
+        ("other", 0): (("second", DOWN, 2), ("third", UP, 2)),
+        ("other", 1): (("third", DOWN, 0),),
+        ("other", 3): (("third", DOWN, 1),),
+        ("feed", 0): (("third", DOWN, 2),),
     }
-    IN_OWN = {
-        (0, 2): (("second", UP, 1),),
-        (1, 2): (("z_step", UP, 2), ("third", UP, 0)),
-        (3, 2): (("third", UP, 1),),
-    }
-    BEFORE_OTHER = (("third", DOWN, 0),)
-    IN_ATTEND = {
-        (0, 0): (("z_step", DOWN, 1),),
-        (0, 2): (("second", UP, 2),),
-        (1, 1): (("z_step", UP, 3),),
-        (1, 2): (("second", DOWN, 1),),
-        (2, 1): (("z_step", DOWN, 2), ("third", UP, 2)),
-        (3, 0): (("second", UP, 3),),
-    }
-    BEFORE_UP = (("z_step", DOWN, 3), ("third", UP, 3), ("second", DOWN, 2))
-    IN_FEED = {
-        1: (("third", DOWN, 1),),
-        2: (("second", DOWN, 3),),
+    END = {
+        ("project", 1): (("second", UP, 0),),
+        ("project", 3): (("second", UP, 1),),
+        ("own", 0): (("second", DOWN, 0),),
+        ("own", 1): (("third", UP, 0),),
+        ("own", 2): (("third", UP, 1),),
+        ("own", 3): (("z_step", UP, 2),),
+        ("swapped", 0): (("z_step", UP, 3), ("third", DOWN, 0)),
+        ("other", 0): (("second", UP, 2), ("z_step", DOWN, 1)),
+        ("other", 1): (("second", UP, 3), ("z_step", DOWN, 2)),
+        ("other", 2): (("second", DOWN, 1), ("third", UP, 2)),
+        ("other", 3): (("z_step", DOWN, 3), ("second", DOWN, 2)),
+        ("norm", 0): (("third", UP, 3),),
+        ("feed", 0): (("second", DOWN, 3),),
+        ("feed", 1): (("third", DOWN, 1),),
+        ("feed", 3): (("third", DOWN, 2),),
+        ("down", 0): (("third", DOWN, 3),),
     }
 
     def __init__(self, gather, swap, blocks_out, keep_sem):
         self.gather, self.swap = gather, swap
+        z = gather.at.z
+        self.at_end = (z == 0) | (z == 3)
         self.keep = [
             pltpu.make_async_copy(gather.blocks.at[kind], blocks_out.at[kind], keep_sem.at[kind]) for kind in range(3)
         ]
 
-    def run(self, events):
-        for name, kind, step in events:
-            getattr(self.gather, name)(kind, step)
-
-    def before_project(self):
-        self.gather.last(ATT)
-        self.keep[ATT].start()
-
-    def in_project(self, m):
-        self.on(self.IN_PROJECT, m)
-
-    def before_other(self):
-        self.run(self.BEFORE_OTHER)
-        self.swap.wait()
-
-    def on(self, table, m, j=None):
-        for key, events in table.items():
-            index, head = (key, None) if j is None else key
-            if head == j:
-                pl.when(m == index)(functools.partial(self.run, events))
-
-    def in_own(self, m, j):
-        self.on(self.IN_OWN, m, j)
-
-    def in_attend(self, m, j):
-        self.on(self.IN_ATTEND, m, j)
-
-    def before_up(self):
-        self.run(self.BEFORE_UP)
-        self.gather.last(UP)
-        self.keep[UP].start()
-
-    def in_feed(self, m):
-        self.on(self.IN_FEED, m)
-
-    def before_down(self):
-        self.run((("third", DOWN, 2), ("third", DOWN, 3)))
-        self.gather.last(DOWN)
+    def after(self, point, m=0):
+        for table, here in ((self.MIDDLE, ~self.at_end), (self.END, self.at_end)):
+            for (name, index), events in table.items():
+                if name == point:
+
+                    def act(events=events):
+                        for step, *which in events:
+                            getattr(self.gather, step)(*which)
+
+                    pl.when(here if isinstance(m, int) else here & (m == index))(act)
+
+    def before(self, point):
+        if point == "project":
+            self.gather.last(ATT)
+            self.keep[ATT].start()
+        if point == "other":
+            self.swap.wait()
+        if point == "feed":
+            self.gather.last(UP)
+            self.keep[UP].start()
+        if point == "down":
+            self.after("down")
+
+    def order(self, step):
+        return self.gather.order(step)
+
+    def landed(self, kind, m):
+        self.gather.plane_copy(kind, m, 4).wait_recv()
+
+    def all_landed(self):
         self.keep[DOWN].start()
 
     def finish(self):
@@ -552,12 +576,13 @@
 def forward_linked(*refs):
     (lengths, starts, frames, cot, query, key, value, out_w, up, down, query_bias, value_bias, up_bias) = refs[:13]
     vecs, refs = refs[13:20], refs[20:]
-    blocks_hbm, probs_hbm, out_ref, masked_ref, *outs = refs[: 4 + N_KEPT]
-    blocks, biases, xs, keybias, valid, vec, *scratch = refs[4 + N_KEPT :]
+    blocks_hbm, probs_hbm, out_hbm, masked_hbm, *outs = refs[: 4 + N_KEPT]
+    blocks, biases, xs, keybias, valid, vec, masked_ref, masked_sem, *scratch = refs[4 + N_KEPT :]
     scratch, links = scratch[:N_FORWARD_SCRATCH], scratch[N_FORWARD_SCRATCH:]
     z_send, z_recv, p_send, p_recv, x_send, x_recv, keep_sem = links
     at = Place()
-    at.greet(False)
+    at.hello(False)
+    at.meet(False)
     gather = Gather(at, blocks, biases, z_send, z_recv, p_send, p_recv)
     packs = pack_weights(
         query[...], key[...], value[...], transposed(out_w[...]), up[...], down[...]
@@ -569,6 +594,13 @@
             gather.first(ATT, at.z)
     biases[at.z] = pack_biases(query_bias[...], value_bias[...], up_bias[...])
     gather.z_step(3, 0)
+    at_end = (at.z == 0) | (at.z == 3)
+
+    @pl.when(at_end)
+    def _():
+        gather.z_step(UP, 0)
+        gather.z_step(DOWN, 0)
+
     fill_vectors(vec, vecs)
     rows = frames.shape[0]
     clip, half = at.z // 2, lax.rem(at.z, 2)
@@ -585,42 +617,54 @@
         keybias[here, :] = jnp.where((slots >= length) & (lanes == 0), NEGATIVE, 0.0).astype(BF16)
         if side == 0:
             valid[...] = jnp.where(slots[:, 0:1] < length, 1.0, 0.0)
+    masked_copy = pltpu.make_async_copy(masked_ref, masked_hbm, masked_sem)
+    masked_copy.start()
     xs[0] = jnp.where(masked_ref[0] > 0, vec[6:7, :], frames[...].astype(F32)).astype(BF16)
     swap = remote(xs.at[0], xs.at[1], x_send, x_recv, at.mate)
+    pl.when(at_end)(swap.start)
     gather.z_step(ATT, 1)
     gather.z_step(3, 1)
     gather.second(ATT, 0)
     gather.z_step(ATT, 2)
     gather.z_step(3, 2)
-    gather.z_step(UP, 0)
+
+    @pl.when(~at_end)
+    def _():
+        gather.z_step(UP, 0)
+        swap.start()
+
     gather.second(ATT, 1)
     gather.third(ATT, 0)
     gather.z_step(ATT, 3)
     gather.z_step(3, 3)
     gather.second(ATT, 2)
+    gather.z_step(UP, 1)
     gather.third(ATT, 1)
     gather.second(ATT, 3)
     gather.first(UP, at.z)
-    gather.z_step(UP, 1)
-    swap.start()
-    gather.z_step(DOWN, 0)
+    gather.third(ATT, 2)
+
+    @pl.when(~at_end)
+    def _():
+        gather.z_step(UP, 2)
+        gather.z_step(DOWN, 0)
+
     gather.first(DOWN, at.z)
-    gather.third(ATT, 2)
     gather.third(ATT, 3)
     hooks = GatherHooks(gather, swap, blocks_hbm, keep_sem)
-    forward_compute(blocks, biases, xs, keybias, valid, cot, vec, probs_hbm, out_ref, outs, *scratch, hooks)
-    hooks.finish()
+    forward_compute(blocks, biases, xs, keybias, valid, cot, vec, probs_hbm, out_hbm, outs, *scratch, hooks)
+    masked_copy.wait()
 
 
 def forward_alone(blocks_in, biases, xs, keybias, valid, cot, *refs):
-    vecs, (probs_hbm, out_ref, *outs), scratch = refs[:7], refs[7 : 9 + N_KEPT], refs[9 + N_KEPT :]
+    vecs, (probs_hbm, out_hbm, *outs), scratch = refs[:7], refs[7 : 9 + N_KEPT], refs[9 + N_KEPT :]
     blocks, vec, *scratch, keep_sem = scratch
     fill_vectors(vec, vecs)
     load = pltpu.make_async_copy(blocks_in, blocks, keep_sem)
     load.start()
     load.wait()
     forward_compute(
-        blocks, biases, xs, keybias, valid, cot, vec, probs_hbm, out_ref, outs, *scratch, NoHooks()
+        blocks, biases, xs, keybias, valid, cot, vec, probs_hbm, out_hbm, outs, *scratch, NoHooks()
     )
 
 
@@ -651,7 +695,7 @@
     ]
 
 
-N_FORWARD_SCRATCH = 10
+N_FORWARD_SCRATCH = 11
 
 
 def forward_scratch(rows):
@@ -660,12 +704,13 @@
         pltpu.SemaphoreType.DMA((N_KEPT,)),
         pltpu.VMEM((8, LEN, 128), BF16),
         pltpu.VMEM((8, 128, LEN), BF16),
-        pltpu.VMEM((256, rows), BF16),
         pltpu.VMEM((3, rows, rows), BF16),
         pltpu.SemaphoreType.DMA((3,)),
         pltpu.VMEM((rows, 768), F32),
         pltpu.VMEM((rows, 768), BF16),
         pltpu.VMEM((12, 8, rows), F32),
+        pltpu.VMEM((rows, 768), BF16),
+        pltpu.SemaphoreType.DMA((3,)),
     ]
 
 
@@ -679,7 +724,7 @@
         name="forward",
         out_shape=[jax.ShapeDtypeStruct(BLOCKS, BF16), probs, frames, masked, *outs],
         in_specs=[pl.BlockSpec(memory_space=pltpu.SMEM)] + [vmem()] * 19,
-        out_specs=[hbm(), hbm(), vmem(), vmem()] + [hbm()] * N_KEPT,
+        out_specs=[hbm()] * (4 + N_KEPT),
         scratch_shapes=[
             pltpu.VMEM(BLOCKS, BF16),
             pltpu.VMEM((4, 16, 768), BF16),
@@ -687,6 +732,8 @@
             pltpu.VMEM((LEN, 128), BF16),
             pltpu.VMEM((rows, 1), F32),
             pltpu.VMEM((8, 768), F32),
+            pltpu.VMEM((2, rows, 1), F32),
+            pltpu.SemaphoreType.DMA,
             *forward_scratch(rows),
             pltpu.SemaphoreType.DMA((4, 2, 3)),
             pltpu.SemaphoreType.DMA((4, 4)),
@@ -711,15 +758,22 @@
         name="forward",
         out_shape=[probs, frames, *forward_outs(rows)],
         in_specs=[hbm()] + [vmem()] * 12,
-        out_specs=[hbm(), vmem()] + [hbm()] * N_KEPT,
+        out_specs=[hbm()] * (2 + N_KEPT),
         scratch_shapes=[pltpu.VMEM(BLOCKS, BF16), pltpu.VMEM((8, 768), F32), *forward_scratch(rows), pltpu.SemaphoreType.DMA],
         compiler_params=pltpu.CompilerParams(vmem_limit_bytes=VMEM_LIMIT),
     )(*ins)
     return probs, frames, kept
 
 
+ATT_ORDER = (0, 3, 1, 2)
+
+
+def att_order(place):
+    return jnp.where(place == 0, 0, jnp.where(place == 1, 3, place - 1))
+
+
 def chunk_at(n):
-    return (2 - n % 2, n // 2) if n < 8 else (0, n - 8)
+    return (DOWN, n) if n < 4 else (UP, n - 4) if n < 8 else (ATT, ATT_ORDER[n - 8])
 
 
 class Scatter:
@@ -873,7 +927,7 @@
     probs_hbm,
     acted_hbm,
     slope_hbm,
-    recip_ref,
+    recip_hbm,
     headout_hbm,
     xt_hbm,
     qm_hbm,
@@ -882,12 +936,12 @@
     att_hbm,
     n1t_hbm,
     n1_hbm,
-    rs1_ref,
+    rs1_hbm,
     gb2_hbm,
     gb2t_hbm,
     g2_hbm,
-    sums_ref,
-    masked_ref,
+    sums_hbm,
+    masked_hbm,
     gain_ref,
     grads,
     rows_ref,
@@ -917,6 +971,11 @@
     sides,
     shifts,
     shares,
+    recip_ref,
+    rs1_ref,
+    sums_ref,
+    masked_ref,
+    small_sem,
     hooks,
 ):
     rows = g2_ref.shape[0]
@@ -926,6 +985,13 @@
     gb2t_load = pltpu.make_async_copy(gb2t_hbm, gb2t_ref, state_sem.at[3])
     n1t_load = pltpu.make_async_copy(n1t_hbm, n1t_ref, state_sem.at[4])
     xt_load = pltpu.make_async_copy(xt_hbm, xt_ref, state_sem.at[5])
+
+    small_loads = [
+        pltpu.make_async_copy(src, dst, small_sem.at[i])
+        for i, (src, dst) in enumerate(
+            ((recip_hbm, recip_ref), (rs1_hbm, rs1_ref), (sums_hbm, sums_ref), (masked_hbm, masked_ref))
+        )
+    ]
 
     def head_loads(m, slot, side):
         three, two, half = pl.ds(3 * m, 3), pl.ds(2 * m, 2), pl.ds(side * rows, rows)
@@ -949,13 +1015,15 @@
             pltpu.make_async_copy(slope_hbm.at[m], acts.at[slot, 1], acts_sem.at[slot, 1]),
         )
 
-    def probs_load(head, side, slot):
-        return pltpu.make_async_copy(
-            probs_hbm.at[head, pl.ds(side * rows, rows)], probs.at[slot], probs_sem.at[slot]
-        )
+    def probs_loads(m, slot, side):
+        half = pl.ds(side * rows, rows)
+        return [
+            pltpu.make_async_copy(probs_hbm.at[3 * m + j, half], probs.at[slot, j], probs_sem.at[slot, j])
+            for j in range(3)
+        ]
 
     def feed_loads(m, slot):
-        return (weight_load(DOWN, m, 2 * slot), weight_load(UP, m, 2 * slot + 1), *act_loads(m, slot))
+        return (weight_load(DOWN, m, 2 * slot), weight_load(UP, m, 2 * slot + 1), act_loads(m, slot)[1])
 
     def begin(copies):
         for copy in copies:
@@ -972,14 +1040,30 @@
         width = value.shape[1]
         grads[kind, m, :, :, :, :, pl.ds(low, width)] = value.astype(BF16).reshape(2, 2, 2, 96, width)
 
-    begin((gb2_load,))
-    begin(feed_loads(0, 0))
-    begin((gb2t_load, n1t_load, g2_load, n1_load, xt_load))
-    begin(head_loads(0, 0, 1))
-    for j in range(3):
-        probs_load(j, 1, j).start()
+    begin((gb2t_load, act_loads(0, 0)[0], act_loads(1, 1)[0]))
     parts[...] = jnp.zeros_like(parts)
-    finish((gb2_load, gb2t_load, n1t_load, g2_load))
+    hooks.after("start")
+    finish((gb2t_load,))
+
+    def feed_down(m, _):
+        slot = lax.rem(m, 2)
+        finish(act_loads(m, slot)[:1])
+        put(DOWN, m, dot(gb2t_ref[...], acts[slot, 0]))
+        hooks.ready(DOWN, m)
+        pl.when(m < 2)(lambda: begin(act_loads(m + 2, slot)[:1]))
+
+        @pl.when(m == 0)
+        def _():
+            begin((gb2_load, *feed_loads(0, 0)))
+            begin((n1t_load, g2_load, n1_load, *small_loads, xt_load))
+            begin(head_loads(0, 0, 1))
+            begin(probs_loads(0, 0, 1))
+
+        hooks.after("down", m)
+        return 0
+
+    lax.fori_loop(0, 4, feed_down, 0)
+    finish((gb2_load, n1t_load, g2_load))
 
     def feed(m, _):
         slot = lax.rem(m, 2)
@@ -987,15 +1071,10 @@
         finish(feed_loads(m, slot))
         grad_acted = dot(gb2_ref[...], block(2 * slot))
         grad_pre = (grad_acted * acts[slot, 1].astype(F32)).astype(BF16)
-        acts[slot, 1] = grad_pre
-        hooks.after("grad_pre", m)
         parts[m, 0:1, :] = jnp.sum(grad_pre.astype(F32), axis=0, keepdims=True)
-        put(DOWN, m, dot(gb2t_ref[...], acts[slot, 0]))
-        hooks.ready(DOWN, m)
-        hooks.after("down", m)
-        put(UP, m, dot(n1t_ref[...], acts[slot, 1]))
+        put(UP, m, dot(n1t_ref[...], grad_pre))
+        g2_ref[...] += dot(grad_pre, block(2 * slot + 1), (1, 1))
         hooks.ready(UP, m)
-        g2_ref[...] += dot(acts[slot, 1], block(2 * slot + 1), (1, 1))
         hooks.after("feed", m)
         return 0
 
@@ -1025,6 +1104,7 @@
 
     zero = jnp.zeros((1, 768), F32)
     finish((n1_load, xt_load))
+    finish(small_loads)
     gain = gain_ref[...].astype(F32).reshape(1, 768)
     sums = lax.fori_loop(0, rows // chunk, norm_back, (zero, zero, zero))
     rows_ref[0, 0:1, :] = sums[0]
@@ -1037,61 +1117,50 @@
     hooks.after("norm")
     g2_ref[...] = jnp.zeros_like(g2_ref)
 
-    def wide(m, j, side):
+    def wide(j, side):
         zeros = jnp.zeros((64, rows), BF16)
         return jnp.concatenate([zeros, side] if j == 1 else [side, zeros], axis=0)
 
-    def half_back(slot, m, j, side, shift, next_load):
-        t = j // 2
-        side = wide(m, j, side)
-        probs_load(0, 0, j).wait()
-        weights = probs[j]
-        grad_weights = dot(v_ref[slot, t], side)
-        grad_scores = (weights.astype(F32) * (grad_weights - shift)).astype(BF16)
-        grad_v = dot(weights, side.T)
-        next_load()
-        grad_k = dot(grad_scores, qm_ref[slot, j])
-        lane = 0 if j == 0 else 64
-        grad_q = dot(kt_ref[slot, t, lane : lane + 64, :], grad_scores)
-        return grad_k, grad_v, grad_q
-
-    def join(parts):
-        return [parts[0] + parts[1], parts[2]]
+    def half_back(slot, sides_here, shifts_here):
+        grads_k, grads_v, grads_q = [], [], []
+        wides = [wide(j, sides_here[j]) for j in range(3)]
+        grad_weights = [dot(v_ref[slot, j // 2], wides[j]) for j in range(3)]
+        for j in range(3):
+            weights = probs[slot, j]
+            grad_scores = (weights.astype(F32) * (grad_weights[j] - shifts_here[j])).astype(BF16)
+            grads_v.append(dot(weights, wides[j].T))
+            grads_k.append(dot(grad_scores, qm_ref[slot, j]))
+            lane = 0 if j == 0 else 64
+            grads_q.append(dot(kt_ref[slot, j // 2, lane : lane + 64, :], grad_scores))
+        return [grads_k[0] + grads_k[1], grads_k[2]], [grads_v[0] + grads_v[1], grads_v[2]], grads_q
 
     def back_other(m, _):
         slot = lax.rem(m, 2)
-        pl.when(m < 3)(lambda: begin(head_loads(m + 1, 1 - slot, 1)))
-        pl.when(m == 3)(lambda: begin(head_loads(0, 0, 0)))
+        pl.when(m < 3)(lambda: begin([*head_loads(m + 1, 1 - slot, 1), *probs_loads(m + 1, 1 - slot, 1)]))
+        pl.when(m == 3)(lambda: begin([*head_loads(0, 0, 0), *probs_loads(0, 0, 0)]))
         weight_load(ATT, m, m).wait()
         finish(head_loads(m, slot, 1))
+        finish(probs_loads(m, slot, 1))
         grad_att_t = dot(gb1[...], block(m, 512, 256)).T
-        grads_k, grads_v = [], []
+        others, shifts_here = [], []
         for j in range(3):
             head = 3 * m + j
             place = (128, 192, 64)[j]
             grad_att = grad_att_t[place : place + 64, :]
-            own = (grad_att * recip_ref[head, 0:1, :]).astype(BF16)
-            other = (grad_att * recip_ref[head, 1:2, :]).astype(BF16)
+            factor_own, factor = recip_ref[head, 0:1, :], recip_ref[head, 1:2, :]
+            own_side = (grad_att * factor_own).astype(BF16)
+            others.append((grad_att * factor).astype(BF16))
             row_sum = jnp.sum(
-                own.astype(F32) * headout_ref[slot, j, 0] + other.astype(F32) * headout_ref[slot, j, 1],
+                own_side.astype(F32) * headout_ref[slot, j, 0] + others[j].astype(F32) * headout_ref[slot, j, 1],
                 axis=0,
                 keepdims=True,
             )
-            sides[head] = own
-            shifts[head, 0:1, :] = row_sum * recip_ref[head, 0:1, :]
-
-            def next_load(j=j, head=head):
-                pl.when(m < 3)(lambda: probs_load(head + 3, 1, j).start())
-                pl.when(m == 3)(lambda: probs_load(j, 0, j).start())
-
-            grad_k, grad_v, grad_q = half_back(
-                slot, m, j, other, row_sum * recip_ref[head, 1:2, :], next_load
-            )
-            grads_k.append(grad_k)
-            grads_v.append(grad_v)
-            shares[head] = grad_q
-            hooks.after(f"other{j}", m)
-        grads_k, grads_v = join(grads_k), join(grads_v)
+            sides[head] = own_side
+            shifts[head, 0:1, :] = row_sum * factor_own
+            shifts_here.append(row_sum * factor)
+        grads_k, grads_v, grads_q = half_back(slot, others, shifts_here)
+        for j in range(3):
+            shares[3 * m + j] = grads_q[j]
         tile = acts.at[m // 2, lax.rem(m, 2)]
         tile[:, 128:256] = grads_k[0].astype(BF16)
         tile[:, 256:384] = grads_v[0].astype(BF16)
@@ -1099,6 +1168,7 @@
         tile[:, 512:640] = grads_v[1].astype(BF16)
         parts[4 + m, 0:1, 128:640] = jnp.sum(tile[:, 128:640].astype(F32), axis=0, keepdims=True)
         g2_ref[...] += dot(tile[:, 128:640], block(m, 128, 512), (1, 1))
+        hooks.after("other", m)
         return 0
 
     lax.fori_loop(0, 4, back_other, 0)
@@ -1112,23 +1182,21 @@
     fill = lax.fori_loop(0, rows // chunk, fill_other, zero)
     hooks.after("mate")
 
-    def back_own(m, _):
-        slot = lax.rem(m, 2)
-        pl.when(m < 3)(lambda: begin(head_loads(m + 1, 1 - slot, 0)))
+    def back_own(place, _):
+        slot = lax.rem(place, 2)
+        m = att_order(place)
+
+        @pl.when(place < 3)
+        def _():
+            after = att_order(place + 1)
+            begin([*head_loads(after, 1 - slot, 0), *probs_loads(after, 1 - slot, 0)])
+
         finish(head_loads(m, slot, 0))
-        grads_k, grads_v, grads_q = [], [], []
-        for j in range(3):
-            head = 3 * m + j
-
-            def next_load(j=j, head=head):
-                pl.when(m < 3)(lambda: probs_load(head + 3, 0, j).start())
-
-            grad_k, grad_v, grad_q = half_back(slot, m, j, sides[head], shifts[head, 0:1, :], next_load)
-            grads_k.append(grad_k)
-            grads_v.append(grad_v)
-            grads_q.append((grad_q + shares[head]) * SCALE)
-            hooks.after(f"own{j}", m)
-        grads_k, grads_v = join(grads_k), join(grads_v)
+        finish(probs_loads(m, slot, 0))
+        grads_k, grads_v, grads_q = half_back(
+            slot, [sides[3 * m + j] for j in range(3)], [shifts[3 * m + j, 0:1, :] for j in range(3)]
+        )
+        grads_q = [(grads_q[j] + shares[3 * m + j]) * SCALE for j in range(3)]
         single = jnp.concatenate([grads_q[2], jnp.zeros((64, rows), F32)], axis=0).T
         own[:, 0:128] = jnp.concatenate(grads_q[:2], axis=0).T.astype(BF16)
         own[:, 128:256] = grads_k[0].astype(BF16)
@@ -1136,6 +1204,7 @@
         own[:, 384:512] = (grads_k[1] + single).astype(BF16)
         own[:, 512:640] = grads_v[1].astype(BF16)
         parts[4 + m, 0:1, 0:PROJ] += jnp.sum(own[...].astype(F32), axis=0, keepdims=True)
+        hooks.after("middle", place)
         other = acts[m // 2, lax.rem(m, 2), :, 128:640]
         grad_proj = dot(xt_ref[0], own[...])
         grad_other = dot(xt_ref[1], other)
@@ -1144,9 +1213,9 @@
         put(ATT, m, grad_proj[:, 128:512] + grad_other[:, :384], 128)
         put(ATT, m, grad_proj[:, 512:] + grad_other[:, 384:] + grad_out_w[:, :128], 512)
         put(ATT, m, grad_out_w[:, 128:], 640)
+        grad_one[...] += dot(own[...], block(m, 0, PROJ), (1, 1))
         hooks.ready(ATT, m)
-        grad_one[...] += dot(own[...], block(m, 0, PROJ), (1, 1))
-        hooks.after("own", m)
+        hooks.after("own", place)
         return 0
 
     lax.fori_loop(0, 4, back_own, 0)
@@ -1183,29 +1252,28 @@
 
 class ScatterHooks:
     PLAN = {
-        ("feed", 0): dict(first=(0,)),
-        ("grad_pre", 1): dict(first=(1,)),
-        ("feed", 1): dict(second=(0,), first=(2,)),
-        ("down", 2): dict(second=(1,), first=(3,)),
-        ("feed", 3): dict(second=(2,), first=(4,), third=(0,)),
-        ("norm", 0): dict(second=(3,), first=(5,), third=(1,)),
-        ("other1", 1): dict(second=(4,), first=(6,), third=(2,), z_one=(0,)),
-        ("other1", 2): dict(second=(5,), first=(7,), third=(3,), z_one=(1,)),
-        ("other2", 3): dict(second=(6,), third=(4,), z_one=(2,), z_two=(0,)),
+        ("down", 2): dict(first=(0,)),
+        ("down", 3): dict(first=(1,)),
+        ("feed", 0): dict(first=(2,)),
+        ("feed", 1): dict(second=(0, 1), first=(3,)),
+        ("feed", 3): dict(second=(2,), first=(4, 5), third=(0,)),
+        ("norm", 0): dict(third=(1,)),
+        ("other", 0): dict(second=(3,), first=(6,)),
+        ("other", 1): dict(third=(2,), z_one=(0,)),
+        ("other", 2): dict(second=(4,), first=(7,), z_one=(1,)),
+        ("other", 3): dict(second=(5,), third=(3,), z_one=(2,), z_two=(0,)),
         ("mate", 0): dict(swap=(0,)),
-        ("own0", 0): dict(swap=(1,)),
-        ("own", 0): dict(second=(7,), third=(5,), z_one=(3,), z_two=(1,), swap=(2,)),
-        ("own0", 1): dict(first=(8,)),
-        ("own1", 1): dict(swap=(3,)),
-        ("own", 1): dict(second=(8,), third=(6, 7), z_one=(4,), z_two=(2,)),
-        ("own0", 2): dict(first=(9,)),
-        ("own", 2): dict(second=(9,), third=(8,), z_one=(5,), z_two=(3,)),
-        ("own0", 3): dict(first=(10,)),
-        ("own", 3): dict(second=(10,), third=(9,), z_one=(6, 7), z_two=(4, 5)),
+        ("own", 0): dict(second=(6,), third=(4,), z_one=(3,)),
+        ("middle", 1): dict(first=(8,), second=(7,), swap=(1,)),
+        ("own", 1): dict(third=(5,), z_one=(4,), z_two=(3,)),
+        ("middle", 2): dict(first=(9,), third=(6,), swap=(2,)),
+        ("own", 2): dict(z_one=(5,)),
+        ("middle", 3): dict(second=(8,), first=(10,), third=(7,), swap=(3,)),
+        ("own", 3): dict(z_one=(6,), z_two=(4,)),
     }
 
-    def __init__(self, scatter, swaps):
-        self.scatter, self.swaps = scatter, swaps
+    def __init__(self, at, scatter, swaps):
+        self.at, self.scatter, self.swaps = at, scatter, swaps
 
     def ready(self, kind, m):
         self.scatter.begin(kind, m)
@@ -1216,6 +1284,8 @@
             self.swaps[piece].start()
 
     def after(self, point, m=0):
+        if point == "start":
+            self.at.meet(True)
         for (name, index), steps in self.PLAN.items():
             if name == point:
                 if isinstance(m, int):
@@ -1225,7 +1295,7 @@
 
 
 N_BACKWARD_INS = 20
-N_BACKWARD_SCRATCH = 28
+N_BACKWARD_SCRATCH = 33
 
 
 def backward_linked(*refs):
@@ -1237,7 +1307,7 @@
     core_in, first_in, second_in, z_in, rows_in, mate_in = links[:6]
     send, recv, z_send, z_recv, t_send, t_recv, m_send, m_recv = links[6:]
     at = Place()
-    at.greet(True)
+    at.hello(True)
     scatter = Scatter(at, grads, core_in, first_in, second_in, z_in, out_ref, send, recv, z_send, z_recv)
     totals = Totals(at, rows_ref, rows_in, t_send, t_recv)
     piece = gb1.shape[0] // 4
@@ -1247,33 +1317,34 @@
         )
         for i in range(4)
     ]
-    backward_compute(*ins, *scratch, ScatterHooks(scatter, swaps))
+    backward_compute(*ins, *scratch, ScatterHooks(at, scatter, swaps))
     totals.start(0)
-    scatter.run(first=(11,))
+    scatter.run(second=(9,), first=(11,))
     totals.finish(0)
+    scatter.run(third=(8,), z_one=(7,))
+    scatter.run(second=(10,))
+    scatter.run(third=(9,), z_one=(8,), z_two=(7,))
+    scatter.run(second=(11,))
     totals.start(1)
-    scatter.run(third=(10,), z_one=(8,), z_two=(6,))
-    scatter.run(second=(11,))
+    scatter.run(third=(10,))
+    scatter.run(z_one=(9,), z_two=(8,))
+    scatter.run(third=(11,))
     totals.finish(1)
     totals.start(2)
-    scatter.run(z_one=(9,), z_two=(7,))
-    scatter.run(third=(11,))
+    scatter.finish(DOWN)
+    scatter.finish(UP)
     totals.finish(2)
     totals.start(3)
-    scatter.finish(DOWN)
-    scatter.finish(UP)
-    scatter.run(z_one=(10,), z_two=(8,))
+    scatter.run(z_one=(10, 11), z_two=(9,))
     totals.finish(3)
     totals.start(4)
-    scatter.run(z_one=(11,), z_two=(9, 10))
     for swap in swaps:
         swap.wait()
-    finish_frames(grad_one, mate_in, ins[18], frames_ref)
+    finish_frames(grad_one, mate_in, scratch[31], frames_ref)
     totals.finish(4)
     rows_out[...] = rows_ref[5]
-    scatter.run(z_two=(11,))
+    scatter.drain()
     scatter.finish(ATT)
-    scatter.drain()
 
 
 def backward_alone(*refs):
@@ -1299,8 +1370,8 @@
         pltpu.SemaphoreType.DMA((4,)),
         pltpu.VMEM((2, 2, rows, 768), BF16),
         pltpu.SemaphoreType.DMA((2, 2)),
-        pltpu.VMEM((3, rows, rows), BF16),
-        pltpu.SemaphoreType.DMA((3,)),
+        pltpu.VMEM((2, 3, rows, rows), BF16),
+        pltpu.SemaphoreType.DMA((2, 3)),
         pltpu.VMEM((rows, 768), BF16),
         pltpu.VMEM((768, rows), BF16),
         pltpu.VMEM((rows, 768), F32),
@@ -1321,6 +1392,11 @@
         pltpu.VMEM((12, 64, rows), BF16),
         pltpu.VMEM((12, 8, rows), F32),
         pltpu.VMEM((12, 64, rows), F32),
+        pltpu.VMEM((12, 8, rows), F32),
+        pltpu.VMEM((rows, 1), F32),
+        pltpu.VMEM((8, 768), F32),
+        pltpu.VMEM((2, rows, 1), F32),
+        pltpu.SemaphoreType.DMA((4,)),
     ]
 
 
@@ -1330,7 +1406,7 @@
     ins = (
         blocks, probs, acted, slope, recip, headout, xt, qm, kt, v, att, n1t, n1, rs1, gb2, gb2t, g2, sums, masked, gain
     )
-    in_specs = [vmem() if i in (4, 13, 17, 18, 19) else hbm() for i in range(20)]
+    in_specs = [vmem() if i == 19 else hbm() for i in range(20)]
     if linked:
         return pl.pallas_call(
             backward_linked,

time: 192 us -> 171 us (0.89)
  Pallas kernels: 190 us -> 169 us
    pallas_call x1, Pallas kernels: 103 us -> 85.4 us  [run_backward(): pl.pallas_call(backward_linked, name='backward', out_shape=[jax.ShapeDtyp...]
    pallas_call x1, Pallas kernels: 83.9 us -> 80.2 us  [run_forward_linked(): pl.pallas_call(forward_linked, name='forward', out_shape=[jax.ShapeDtypeS...]
where the time goes in v4:
time: 171 us; the launch traced here: 170 us
  Pallas kernels  169 us (99%)
    pallas_call x1, Pallas kernels, run_backward(): pl.pallas_call(backward_linked, name='backward', out_shape=[jax.ShapeDtyp...  85.4 us
    pallas_call x1, Pallas kernels, run_forward_linked(): pl.pallas_call(forward_linked, name='forward', out_shape=[jax.ShapeDtypeS...  80.2 us

profile of v4, /device:TPU:16, one launch (start us, length us, event | category | flops | bytes accessed | tf_op | source)
XLA Modules:
  0.0 169.8 jit_solution(14604262076493725525)
XLA Ops:
  0.7 80.2 %forward.1 = (bf16[3,4,2,2,2,96,768]{6,5,4,3,2,1,0:T(8,128)(2,1)}, bf16[12,1024,512]{2,1,0:T(8,128)(2,1)}, bf16[512,768]{1,0:T(8,128)(2,1)}, f32[2,512,1]{2,1,0:...) custom-call(s32[2]{0:T(128)} %refs_0_.1, ...), custom_call_target="tpu_custom_call" | custom-call | tf_op jit(solution)/shard_map/forward/pallas_call | solution.py:722
  80.9 85.4 %backward.1 = (f32[3,96,768]{2,1,0:T(8,128)}, f32[16,768]{1,0:T(8,128)}, bf16[512,768]{1,0:T(8,128)(2,1)}) custom-call(bf16[3,4,2,2,2,96,768]{6,5,4,3,2,1,0:T(8,128)(2,1)} %get-tuple-element.59.refs_0_, bf16[12,1024,512]{2,1,0:T(8,128)(2,1)} %get-tuple-element.60.refs_1_, bf16[4,512,768]{2,1,0:T(8,128)(2,1)} %get-tuple-element.61.refs_2_, ...), custom_call_target="tpu_custom_call" | custom-call | tf_op jit(solution)/shard_map/backward/pallas_call | solution.py:1411
  166.3 3.3 %finish.1 = (bf16[512,768]{1,0:T(8,128)(2,1)}, bf16[512,768]{1,0:T(8,128)(2,1)}, f32[96,192]{1,0:T(8,128)}, f32[96,192]{1,0:T(8,128)}, f32[96,192]{1,0:T(8,128)}...) custom-call(f32[3,96,768]{2,1,0:T(8,128)} %get-tuple-element.78.grad, ...), custom_call_target="tpu_custom_call" | custom-call | tf_op jit(solution)/shard_map/finish/pallas_call | solution.py:1499

commit v5 on v4

--- a/solution.py
+++ b/solution.py
@@ -360,7 +360,7 @@
         low[r, :] = (unit * vec_ref[2:3, :] + vec_ref[3:4, :]).astype(BF16)
         return 0
 
-    lax.fori_loop(0, rows // chunk, norm_one, 0)
+    lax.fori_loop(0, rows // chunk, norm_one, 0, unroll=2)
     n1t_ref[...] = low[...].T
     keep(9, 10, 11)
     hooks.after("norm")
@@ -378,22 +378,15 @@
     keep(7, 8)
     hooks.before("down")
 
-    def down(step, _):
-        m = hooks.order(step)
-        hooks.landed(DOWN, m)
-        part = dot(acted_ref[m], block_of(blocks, DOWN, m), (1, 1))
-
-        @pl.when(step == 0)
-        def _():
-            total[...] = part
-
-        @pl.when(step > 0)
-        def _():
-            total[...] += part
-
-        return 0
-
-    lax.fori_loop(0, 4, down, 0)
+    def down(steps):
+        places = [hooks.order(step) for step in steps]
+        for m in places:
+            hooks.landed(DOWN, m)
+        shares = [dot(acted_ref[m], block_of(blocks, DOWN, m), (1, 1)) for m in places]
+        return functools.reduce(jnp.add, shares)
+
+    total[...] = down((0, 1, 2))
+    total[...] += down((3,))
     hooks.all_landed()
 
     def norm_two(i, sums):
@@ -423,7 +416,7 @@
         )
 
     zero = jnp.zeros((1, 768), F32)
-    sums = lax.fori_loop(0, rows // chunk, norm_two, (zero, zero, zero))
+    sums = lax.fori_loop(0, rows // chunk, norm_two, (zero, zero, zero), unroll=2)
     sums_ref[...] = jnp.concatenate([*sums, jnp.zeros((5, 768), F32)], axis=0)
     keep(15)
     gb2t_ref[...] = gb2_ref[...].T
@@ -591,7 +584,7 @@
         blocks[kind, at.z, at.y, at.x, at.c] = packs[kind]
         if kind == 0:
             gather.z_step(ATT, 0)
-            gather.first(ATT, at.z)
+        gather.first(kind, at.z)
     biases[at.z] = pack_biases(query_bias[...], value_bias[...], up_bias[...])
     gather.z_step(3, 0)
     at_end = (at.z == 0) | (at.z == 3)
@@ -641,7 +634,6 @@
     gather.z_step(UP, 1)
     gather.third(ATT, 1)
     gather.second(ATT, 3)
-    gather.first(UP, at.z)
     gather.third(ATT, 2)
 
     @pl.when(~at_end)
@@ -649,7 +641,6 @@
         gather.z_step(UP, 2)
         gather.z_step(DOWN, 0)
 
-    gather.first(DOWN, at.z)
     gather.third(ATT, 3)
     hooks = GatherHooks(gather, swap, blocks_hbm, keep_sem)
     forward_compute(blocks, biases, xs, keybias, valid, cot, vec, probs_hbm, out_hbm, outs, *scratch, hooks)
@@ -766,32 +757,47 @@
 
 
 ATT_ORDER = (0, 3, 1, 2)
+DOWN_ORDER = (3, 0, 2, 1)
+DEEP = 32
 
 
 def att_order(place):
     return jnp.where(place == 0, 0, jnp.where(place == 1, 3, place - 1))
 
 
+def down_order(place):
+    return jnp.where(place == 0, 3, jnp.where(place == 1, 0, 4 - place))
+
+
+def row_parts(kind):
+    base = DEEP if kind == DOWN else 0
+    half = (96 - base) // 2
+    return pl.ds(base, half), pl.ds(base + half, half), pl.ds(base, 2 * half)
+
+
 def chunk_at(n):
-    return (DOWN, n) if n < 4 else (UP, n - 4) if n < 8 else (ATT, ATT_ORDER[n - 8])
+    return (DOWN, DOWN_ORDER[n]) if n < 4 else (UP, n - 4) if n < 8 else (ATT, ATT_ORDER[n - 8])
 
 
 class Scatter:
-    def __init__(self, at, grads, core_in, first_in, second_in, z_in, out, send, recv, z_send, z_recv):
+    def __init__(self, at, grads, out, buffers, semaphores):
         self.at, self.grads, self.out = at, grads, out
-        self.core_in, self.first_in, self.second_in, self.z_in = core_in, first_in, second_in, z_in
-        self.send, self.recv, self.z_send, self.z_recv = send, recv, z_send, z_recv
+        self.core_in, self.first_in, self.second_in, self.z_in, self.deep_in, self.plane_in = buffers
+        self.send, self.recv, self.z_send, self.z_recv, *deep = semaphores
+        self.deep_send, self.deep_recv, self.plane_send, self.plane_recv = deep
 
     def copy(self, kind, m, which):
         at, grads = self.at, self.grads.at[kind, m]
         x, y, c = at.x, at.y, at.c
-        low, high = pl.ds(0, 48), pl.ds(48, 48)
+        low, high, _ = row_parts(kind)
+        first, second = self.first_in.at[kind, m], self.second_in.at[kind, m]
+        part = pl.ds(0, low.size)
         src, dst, device = {
             0: lambda: (grads.at[:, :, 1 - c], self.core_in.at[kind, m], at.core),
-            1: lambda: (grads.at[:, 1 - x, c, low], self.first_in.at[kind, m, 0], at.across_x),
-            2: lambda: (grads.at[1 - y, :, c, high], self.first_in.at[kind, m, 1], at.across_y),
-            3: lambda: (grads.at[1 - y, x, c, low], self.second_in.at[kind, m, 0], at.across_y),
-            4: lambda: (grads.at[y, 1 - x, c, high], self.second_in.at[kind, m, 1], at.across_x),
+            1: lambda: (grads.at[:, 1 - x, c, low], first.at[0, :, part], at.across_x),
+            2: lambda: (grads.at[1 - y, :, c, high], first.at[1, :, part], at.across_y),
+            3: lambda: (grads.at[1 - y, x, c, low], second.at[0, part], at.across_y),
+            4: lambda: (grads.at[y, 1 - x, c, high], second.at[1, part], at.across_x),
         }[which]()
         return remote(src, dst, self.send.at[kind, m, which], self.recv.at[kind, m, which], device)
 
@@ -809,53 +815,130 @@
                 self.add(grads.at[y, x, at.c], self.core_in.at[kind, m, y, x])
         self.copy(kind, m, 1).start()
         self.copy(kind, m, 2).start()
+        if kind == DOWN:
+            self.ends(m, lambda direction: self.deep_copy(m, direction).start())
 
     def second(self, kind, m):
         at, grads = self.at, self.grads.at[kind, m]
-        low, high = pl.ds(0, 48), pl.ds(48, 48)
+        low, high, _ = row_parts(kind)
+        part = pl.ds(0, low.size)
         self.copy(kind, m, 1).wait_recv()
         for y in range(2):
-            self.add(grads.at[y, at.x, at.c, low], self.first_in.at[kind, m, 0, y])
+            self.add(grads.at[y, at.x, at.c, low], self.first_in.at[kind, m, 0, y, part])
         self.copy(kind, m, 3).start()
         self.copy(kind, m, 2).wait_recv()
         for x in range(2):
-            self.add(grads.at[at.y, x, at.c, high], self.first_in.at[kind, m, 1, x])
+            self.add(grads.at[at.y, x, at.c, high], self.first_in.at[kind, m, 1, x, part])
         self.copy(kind, m, 4).start()
 
     def third(self, kind, m):
         at = self.at
         grads = self.grads.at[kind, m, at.y, at.x, at.c]
+        low, high, _ = row_parts(kind)
+        part = pl.ds(0, low.size)
         self.copy(kind, m, 3).wait_recv()
-        self.add(grads.at[pl.ds(0, 48)], self.second_in.at[kind, m, 0])
+        self.add(grads.at[low], self.second_in.at[kind, m, 0, part])
         self.copy(kind, m, 4).wait_recv()
-        self.add(grads.at[pl.ds(48, 48)], self.second_in.at[kind, m, 1])
+        self.add(grads.at[high], self.second_in.at[kind, m, 1, part])
         self.z_start(kind, m)
 
-    def z_copy(self, kind, m, direction):
-        at = self.at
-        src = self.grads.at[kind, m, at.y, at.x, at.c]
-        device = at.right if direction == 0 else at.left
-        slot = m if direction == 0 else jnp.where(m == at.z - 1, 4, m)
-        return remote(src, self.z_in.at[kind, slot], self.z_send.at[kind, m], self.z_recv.at[kind, slot], device)
-
-    def z_landed(self, kind, m, slot, direction):
-        at = self.at
-        src = self.grads.at[kind, m, at.y, at.x, at.c]
-        device = at.right if direction == 0 else at.left
-        return remote(src, self.z_in.at[kind, slot], self.z_send.at[kind, m], self.z_recv.at[kind, slot], device)
-
-    def relay(self, kind, m, direction):
-        at = self.at
-        self.z_landed(kind, m, m, direction).wait_recv()
-        self.add(self.grads.at[kind, m, at.y, at.x, at.c], self.z_in.at[kind, m])
-        self.z_copy(kind, m, direction).start()
-
-    def z_start(self, kind, m):
+    def ends(self, m, act):
         z = self.at.z
         if m > 0:
-            pl.when(z == 0)(lambda: self.z_copy(kind, m, 0).start())
+            pl.when(z == 0)(lambda: act(0))
         if m < 3:
-            pl.when(z == 3)(lambda: self.z_copy(kind, m, 1).start())
+            pl.when(z == 3)(lambda: act(1))
+
+    def deep_copy(self, m, direction, slot=None):
+        at = self.at
+        device = at.right if direction == 0 else at.left
+        if slot is None:
+            slot = m if direction == 0 else jnp.where(m == at.z - 1, 4, m)
+        src = self.grads.at[DOWN, m, :, :, at.c, pl.ds(0, DEEP)]
+        return remote(src, self.deep_in.at[slot], self.deep_send.at[m], self.deep_recv.at[slot], device)
+
+    def deep_add(self, m, slot, direction):
+        self.deep_copy(m, direction, slot).wait_recv()
+        for y in range(2):
+            for x in range(2):
+                self.add(self.grads.at[DOWN, m, y, x, self.at.c, pl.ds(0, DEEP)], self.deep_in.at[slot, y, x])
+
+    def deep_relay(self, m, direction):
+        self.deep_add(m, m, direction)
+        self.deep_copy(m, direction).start()
+
+    def deep_one(self, kind, m):
+        z = self.at.z
+        if m > 1:
+            pl.when(z == 1)(lambda: self.deep_relay(m, 0))
+        else:
+            pl.when(z == 2)(lambda: self.deep_relay(m, 1))
+
+    def deep_two(self, kind, m):
+        z = self.at.z
+        if m == 3:
+            pl.when(z == 2)(lambda: self.deep_relay(m, 0))
+        if m == 0:
+            pl.when(z == 1)(lambda: self.deep_relay(m, 1))
+
+    def deep_plane(self, which):
+        at, grads = self.at, self.grads.at[DOWN, self.at.z]
+        x, y, c = at.x, at.y, at.c
+        half = DEEP // 2
+        low, high = pl.ds(0, half), pl.ds(half, half)
+        src, dst, device = {
+            0: lambda: (grads.at[:, 1 - x, c, low], self.plane_in.at[0], at.across_x),
+            1: lambda: (grads.at[1 - y, :, c, high], self.plane_in.at[1], at.across_y),
+            2: lambda: (grads.at[1 - y, x, c, low], self.plane_in.at[2, 0], at.across_y),
+            3: lambda: (grads.at[y, 1 - x, c, high], self.plane_in.at[2, 1], at.across_x),
+        }[which]()
+        return remote(src, dst, self.plane_send.at[which], self.plane_recv.at[which], device)
+
+    def deep_first(self):
+        z = self.at.z
+        pl.when(z > 0)(lambda: self.deep_add(z, z, 0))
+        pl.when(z < 3)(lambda: self.deep_add(z, 4, 1))
+        self.deep_plane(0).start()
+        self.deep_plane(1).start()
+
+    def deep_second(self):
+        at, half = self.at, DEEP // 2
+        grads = self.grads.at[DOWN, at.z]
+        self.deep_plane(0).wait_recv()
+        for y in range(2):
+            self.add(grads.at[y, at.x, at.c, pl.ds(0, half)], self.plane_in.at[0, y])
+        self.deep_plane(2).start()
+        self.deep_plane(1).wait_recv()
+        for x in range(2):
+            self.add(grads.at[at.y, x, at.c, pl.ds(half, half)], self.plane_in.at[1, x])
+        self.deep_plane(3).start()
+
+    def deep_third(self):
+        at, half = self.at, DEEP // 2
+        grads = self.grads.at[DOWN, at.z, at.y, at.x, at.c]
+        self.deep_plane(2).wait_recv()
+        self.add(grads.at[pl.ds(0, half)], self.plane_in.at[2, 0])
+        self.deep_plane(3).wait_recv()
+        self.add(grads.at[pl.ds(half, half)], self.plane_in.at[2, 1])
+
+    def z_copy(self, kind, m, direction, slot=None):
+        at = self.at
+        whole = row_parts(kind)[2]
+        device = at.right if direction == 0 else at.left
+        if slot is None:
+            slot = m if direction == 0 else jnp.where(m == at.z - 1, 4, m)
+        src = self.grads.at[kind, m, at.y, at.x, at.c, whole]
+        dst = self.z_in.at[kind, slot, whole]
+        return remote(src, dst, self.z_send.at[kind, m], self.z_recv.at[kind, slot], device)
+
+    def relay(self, kind, m, direction):
+        whole = row_parts(kind)[2]
+        self.z_copy(kind, m, direction, m).wait_recv()
+        self.add(self.grads.at[kind, m, self.at.y, self.at.x, self.at.c, whole], self.z_in.at[kind, m, whole])
+        self.z_copy(kind, m, direction).start()
+
+    def z_start(self, kind, m):
+        self.ends(m, lambda direction: self.z_copy(kind, m, direction).start())
 
     def z_one(self, kind, m):
         z = self.at.z
@@ -873,17 +956,18 @@
 
     def finish(self, kind):
         at, z = self.at, self.at.z
+        whole = row_parts(kind)[2]
         self.out[kind] = self.grads[kind, z, at.y, at.x, at.c].astype(F32)
 
         @pl.when(z > 0)
         def _():
-            self.z_landed(kind, z, z, 0).wait_recv()
-            self.out[kind] += self.z_in[kind, z].astype(F32)
+            self.z_copy(kind, z, 0, z).wait_recv()
+            self.out[kind, whole] += self.z_in[kind, z, whole].astype(F32)
 
         @pl.when(z < 3)
         def _():
-            self.z_landed(kind, z, 4, 1).wait_recv()
-            self.out[kind] += self.z_in[kind, 4].astype(F32)
+            self.z_copy(kind, z, 1, 4).wait_recv()
+            self.out[kind, whole] += self.z_in[kind, 4, whole].astype(F32)
 
     def run(self, **steps):
         for name, places in steps.items():
@@ -892,13 +976,21 @@
 
     def drain(self):
         z = self.at.z
+        for which in range(4):
+            self.deep_plane(which).wait_send()
         for kind in range(3):
 
             def of_index(m, _, kind=kind):
                 for which in range(5):
                     self.copy(kind, m, which).wait_send()
-                pl.when(m > z)(lambda: self.z_copy(kind, m, 0).wait_send())
-                pl.when(m < z)(lambda: self.z_copy(kind, m, 1).wait_send())
+
+                def along(direction):
+                    self.z_copy(kind, m, direction).wait_send()
+                    if kind == DOWN:
+                        self.deep_copy(m, direction).wait_send()
+
+                pl.when(m > z)(lambda: along(0))
+                pl.when(m < z)(lambda: along(1))
                 return 0
 
             lax.fori_loop(0, 4, of_index, 0)
@@ -907,7 +999,7 @@
 class Totals:
     def __init__(self, at, rows, got, send, recv):
         self.rows, self.got, self.send, self.recv = rows, got, send, recv
-        self.partners = (at.core, at.across_x, at.across_y, at.mate, at.far)
+        self.partners = (at.core, at.mate, at.far, at.across_x, at.across_y)
 
     def copy(self, stage):
         return remote(
@@ -1009,11 +1101,9 @@
     def weight_load(kind, m, slot):
         return pltpu.make_async_copy(blocks_hbm.at[kind, m], weight.at[slot], weight_sem.at[slot])
 
-    def act_loads(m, slot):
-        return (
-            pltpu.make_async_copy(acted_hbm.at[m], acts.at[slot, 0], acts_sem.at[slot, 0]),
-            pltpu.make_async_copy(slope_hbm.at[m], acts.at[slot, 1], acts_sem.at[slot, 1]),
-        )
+    def act_load(which, m):
+        pair, place = m // 2, lax.rem(m, 2)
+        return pltpu.make_async_copy(which.at[m], acts.at[pair, place], acts_sem.at[pair, place])
 
     def probs_loads(m, slot, side):
         half = pl.ds(side * rows, rows)
@@ -1023,7 +1113,7 @@
         ]
 
     def feed_loads(m, slot):
-        return (weight_load(DOWN, m, 2 * slot), weight_load(UP, m, 2 * slot + 1), act_loads(m, slot)[1])
+        return (weight_load(DOWN, m, 2 * slot), weight_load(UP, m, 2 * slot + 1))
 
     def begin(copies):
         for copy in copies:
@@ -1040,26 +1130,30 @@
         width = value.shape[1]
         grads[kind, m, :, :, :, :, pl.ds(low, width)] = value.astype(BF16).reshape(2, 2, 2, 96, width)
 
-    begin((gb2t_load, act_loads(0, 0)[0], act_loads(1, 1)[0]))
+    begin([gb2t_load, *(act_load(acted_hbm, m) for m in DOWN_ORDER)])
     parts[...] = jnp.zeros_like(parts)
     hooks.after("start")
     finish((gb2t_load,))
 
-    def feed_down(m, _):
-        slot = lax.rem(m, 2)
-        finish(act_loads(m, slot)[:1])
-        put(DOWN, m, dot(gb2t_ref[...], acts[slot, 0]))
+    def feed_down(place, _):
+        m = down_order(place)
+        act_load(acted_hbm, m).wait()
+        put(DOWN, m, dot(gb2t_ref[...], acts[m // 2, lax.rem(m, 2)]))
         hooks.ready(DOWN, m)
-        pl.when(m < 2)(lambda: begin(act_loads(m + 2, slot)[:1]))
-
-        @pl.when(m == 0)
+
+        @pl.when(place == 0)
         def _():
             begin((gb2_load, *feed_loads(0, 0)))
+
+        act_load(slope_hbm, m).start()
+
+        @pl.when(place == 1)
+        def _():
             begin((n1t_load, g2_load, n1_load, *small_loads, xt_load))
             begin(head_loads(0, 0, 1))
             begin(probs_loads(0, 0, 1))
 
-        hooks.after("down", m)
+        hooks.after("down", place)
         return 0
 
     lax.fori_loop(0, 4, feed_down, 0)
@@ -1069,8 +1163,9 @@
         slot = lax.rem(m, 2)
         pl.when(m < 3)(lambda: begin(feed_loads(m + 1, 1 - slot)))
         finish(feed_loads(m, slot))
+        act_load(slope_hbm, m).wait()
         grad_acted = dot(gb2_ref[...], block(2 * slot))
-        grad_pre = (grad_acted * acts[slot, 1].astype(F32)).astype(BF16)
+        grad_pre = (grad_acted * acts[m // 2, lax.rem(m, 2)].astype(F32)).astype(BF16)
         parts[m, 0:1, :] = jnp.sum(grad_pre.astype(F32), axis=0, keepdims=True)
         put(UP, m, dot(n1t_ref[...], grad_pre))
         g2_ref[...] += dot(grad_pre, block(2 * slot + 1), (1, 1))
@@ -1106,7 +1201,7 @@
     finish((n1_load, xt_load))
     finish(small_loads)
     gain = gain_ref[...].astype(F32).reshape(1, 768)
-    sums = lax.fori_loop(0, rows // chunk, norm_back, (zero, zero, zero))
+    sums = lax.fori_loop(0, rows // chunk, norm_back, (zero, zero, zero), unroll=2)
     rows_ref[0, 0:1, :] = sums[0]
     rows_ref[0, 1:2, :] = sums_ref[0:1, :]
     rows_ref[0, 2:3, :] = sums[1]
@@ -1254,21 +1349,23 @@
     PLAN = {
         ("down", 2): dict(first=(0,)),
         ("down", 3): dict(first=(1,)),
-        ("feed", 0): dict(first=(2,)),
-        ("feed", 1): dict(second=(0, 1), first=(3,)),
-        ("feed", 3): dict(second=(2,), first=(4, 5), third=(0,)),
-        ("norm", 0): dict(third=(1,)),
-        ("other", 0): dict(second=(3,), first=(6,)),
-        ("other", 1): dict(third=(2,), z_one=(0,)),
-        ("other", 2): dict(second=(4,), first=(7,), z_one=(1,)),
-        ("other", 3): dict(second=(5,), third=(3,), z_one=(2,), z_two=(0,)),
+        ("feed", 0): dict(first=(2, 3)),
+        ("feed", 1): dict(second=(0, 1), deep_one=(0,)),
+        ("feed", 2): dict(second=(2,), first=(4,), deep_one=(1,)),
+        ("feed", 3): dict(second=(3,), first=(5,), third=(0,), deep_one=(2,), deep_two=(0,)),
+        ("norm", 0): dict(third=(1,), deep_one=(3,), deep_two=(1,)),
+        ("other", 0): dict(second=(4,), first=(6,), third=(2,)),
+        ("other", 1): dict(deep=("deep_first",), third=(3,), z_one=(0,)),
+        ("other", 2): dict(first=(7,), z_one=(1,)),
+        ("other", 3): dict(second=(5,), third=(4,), z_one=(2,), z_two=(0,)),
         ("mate", 0): dict(swap=(0,)),
-        ("own", 0): dict(second=(6,), third=(4,), z_one=(3,)),
-        ("middle", 1): dict(first=(8,), second=(7,), swap=(1,)),
-        ("own", 1): dict(third=(5,), z_one=(4,), z_two=(3,)),
-        ("middle", 2): dict(first=(9,), third=(6,), swap=(2,)),
+        ("middle", 0): dict(deep=("deep_second",), swap=(1,)),
+        ("own", 0): dict(second=(6,), third=(5,), z_one=(3,), z_two=(1,)),
+        ("middle", 1): dict(first=(8,), deep=("deep_third",), swap=(2,)),
+        ("own", 1): dict(second=(7,), z_one=(4,)),
+        ("middle", 2): dict(first=(9,), third=(6,), swap=(3,)),
         ("own", 2): dict(z_one=(5,)),
-        ("middle", 3): dict(second=(8,), first=(10,), third=(7,), swap=(3,)),
+        ("middle", 3): dict(second=(8,), first=(10,), third=(7,)),
         ("own", 3): dict(z_one=(6,), z_two=(4,)),
     }
 
@@ -1278,8 +1375,10 @@
     def ready(self, kind, m):
         self.scatter.begin(kind, m)
 
-    def run(self, swap=(), **steps):
+    def run(self, swap=(), deep=(), **steps):
         self.scatter.run(**steps)
+        for name in deep:
+            getattr(self.scatter, name)()
         for piece in swap:
             self.swaps[piece].start()
 
@@ -1304,11 +1403,10 @@
     scratch = refs[N_BACKWARD_INS + 3 :]
     scratch, links = scratch[:N_BACKWARD_SCRATCH], scratch[N_BACKWARD_SCRATCH:]
     grads, rows_ref, gb1, grad_one = scratch[0], scratch[1], scratch[8], scratch[10]
-    core_in, first_in, second_in, z_in, rows_in, mate_in = links[:6]
-    send, recv, z_send, z_recv, t_send, t_recv, m_send, m_recv = links[6:]
+    rows_in, mate_in, t_send, t_recv, m_send, m_recv = links[14:]
     at = Place()
     at.hello(True)
-    scatter = Scatter(at, grads, core_in, first_in, second_in, z_in, out_ref, send, recv, z_send, z_recv)
+    scatter = Scatter(at, grads, out_ref, links[:6], links[6:14])
     totals = Totals(at, rows_ref, rows_in, t_send, t_recv)
     piece = gb1.shape[0] // 4
     swaps = [
@@ -1321,26 +1419,28 @@
     totals.start(0)
     scatter.run(second=(9,), first=(11,))
     totals.finish(0)
+    totals.start(1)
     scatter.run(third=(8,), z_one=(7,))
     scatter.run(second=(10,))
-    scatter.run(third=(9,), z_one=(8,), z_two=(7,))
-    scatter.run(second=(11,))
-    totals.start(1)
-    scatter.run(third=(10,))
-    scatter.run(z_one=(9,), z_two=(8,))
-    scatter.run(third=(11,))
+    scatter.run(third=(9,))
     totals.finish(1)
     totals.start(2)
+    scatter.run(second=(11,))
+    scatter.run(z_one=(8,), z_two=(7,))
+    scatter.run(third=(10,))
+    totals.finish(2)
+    totals.start(3)
+    scatter.run(third=(11,))
+    scatter.run(z_one=(9,), z_two=(8,))
     scatter.finish(DOWN)
     scatter.finish(UP)
-    totals.finish(2)
-    totals.start(3)
-    scatter.run(z_one=(10, 11), z_two=(9,))
     totals.finish(3)
     totals.start(4)
+    scatter.run(z_one=(10,))
     for swap in swaps:
         swap.wait()
     finish_frames(grad_one, mate_in, scratch[31], frames_ref)
+    scatter.run(z_one=(11,), z_two=(9,))
     totals.finish(4)
     rows_out[...] = rows_ref[5]
     scatter.drain()
@@ -1424,12 +1524,18 @@
                 pltpu.VMEM((3, 4, 2, 2, 48, 768), BF16),
                 pltpu.VMEM((3, 4, 2, 48, 768), BF16),
                 pltpu.VMEM((3, 5, 96, 768), BF16),
-                pltpu.VMEM((5, 16, 768), F32),
-                pltpu.VMEM((rows, 768), BF16),
+                pltpu.VMEM((5, 2, 2, DEEP, 768), BF16),
+                pltpu.VMEM((3, 2, DEEP // 2, 768), BF16),
                 pltpu.SemaphoreType.DMA((3, 4, 5)),
                 pltpu.SemaphoreType.DMA((3, 4, 5)),
                 pltpu.SemaphoreType.DMA((3, 4)),
                 pltpu.SemaphoreType.DMA((3, 5)),
+                pltpu.SemaphoreType.DMA((4,)),
+                pltpu.SemaphoreType.DMA((5,)),
+                pltpu.SemaphoreType.DMA((4,)),
+                pltpu.SemaphoreType.DMA((4,)),
+                pltpu.VMEM((5, 16, 768), F32),
+                pltpu.VMEM((rows, 768), BF16),
                 pltpu.SemaphoreType.DMA((5,)),
                 pltpu.SemaphoreType.DMA((5,)),
                 pltpu.SemaphoreType.DMA((4,)),

time: 171 us -> 163 us (0.953)
  Pallas kernels: 169 us -> 162 us
    pallas_call x1, Pallas kernels: 85.4 us -> 80.9 us  [run_backward(): pl.pallas_call(backward_linked, name='backward', out_shape=[jax.ShapeDtyp...]
    pallas_call x1, Pallas kernels: 80.2 us -> 77.9 us  [run_forward_linked(): pl.pallas_call(forward_linked, name='forward', out_shape=[jax.ShapeDtypeS...]
where the time goes in v5:
time: 163 us
  Pallas kernels  162 us (99%)
    pallas_call x1, Pallas kernels, run_backward(): pl.pallas_call(backward_linked, name='backward', out_shape=[jax.ShapeDtyp...  80.9 us
    pallas_call x1, Pallas kernels, run_forward_linked(): pl.pallas_call(forward_linked, name='forward', out_shape=[jax.ShapeDtypeS...  77.9 us
    pallas_call x1, Pallas kernels, run_finish(): pl.pallas_call(functools.partial(finish_kernel, (n_dp, n_mp)), name='fini...  3.34 us

profile of v5, /device:TPU:16, one launch (start us, length us, event | category | flops | bytes accessed | tf_op | source)
XLA Modules:
  0.0 163.1 jit_solution(17968191333899299408)
XLA Ops:
  0.7 77.9 %forward.1 = (bf16[3,4,2,2,2,96,768]{6,5,4,3,2,1,0:T(8,128)(2,1)}, bf16[12,1024,512]{2,1,0:T(8,128)(2,1)}, bf16[512,768]{1,0:T(8,128)(2,1)}, f32[2,512,1]{2,1,0:...) custom-call(s32[2]{0:T(128)} %refs_0_.1, ...), custom_call_target="tpu_custom_call" | custom-call | tf_op jit(solution)/shard_map/forward/pallas_call | solution.py:713
  78.6 80.9 %backward.1 = (f32[3,96,768]{2,1,0:T(8,128)}, f32[16,768]{1,0:T(8,128)}, bf16[512,768]{1,0:T(8,128)(2,1)}) custom-call(bf16[3,4,2,2,2,96,768]{6,5,4,3,2,1,0:T(8,128)(2,1)} %get-tuple-element.59.refs_0_, bf16[12,1024,512]{2,1,0:T(8,128)(2,1)} %get-tuple-element.60.refs_1_, bf16[4,512,768]{2,1,0:T(8,128)(2,1)} %get-tuple-element.61.refs_2_, ...), custom_call_target="tpu_custom_call" | custom-call | tf_op jit(solution)/shard_map/backward/pallas_call | solution.py:1511
  159.5 3.3 %finish.1 = (bf16[512,768]{1,0:T(8,128)(2,1)}, bf16[512,768]{1,0:T(8,128)(2,1)}, f32[96,192]{1,0:T(8,128)}, f32[96,192]{1,0:T(8,128)}, f32[96,192]{1,0:T(8,128)}...) custom-call(f32[3,96,768]{2,1,0:T(8,128)} %get-tuple-element.78.grad, ...), custom_call_target="tpu_custom_call" | custom-call | tf_op jit(solution)/shard_map/finish/pallas_call | solution.py:1605

commit v6 on v5

--- a/solution.py
+++ b/solution.py
@@ -83,37 +83,37 @@
         self.at, self.blocks, self.biases = at, blocks, biases
         self.z_send, self.z_recv, self.p_send, self.p_recv = z_send, z_recv, p_send, p_recv
 
-    def z_copy(self, kind, m, direction, step):
+    def z_copy(self, kind, m, direction):
         at = self.at
         if kind == 3:
             ref = self.biases.at[m]
         else:
             ref = self.blocks.at[kind, m, at.y, at.x, at.c]
         device = at.right if direction == 0 else at.left
-        return remote(ref, ref, self.z_send.at[kind, direction, step], self.z_recv.at[kind, m], device)
+        return remote(ref, ref, self.z_send.at[kind, direction], self.z_recv.at[kind, m], device)
 
     def z_step(self, kind, step):
         z = self.at.z
         if step == 0:
-            pl.when((z > 0) & (z < 2))(lambda: self.z_copy(kind, z, 1, 0).start())
-            pl.when(z < 3)(lambda: self.z_copy(kind, z, 0, 0).start())
-            pl.when(z >= 2)(lambda: self.z_copy(kind, z, 1, 0).start())
+            pl.when((z > 0) & (z < 2))(lambda: self.z_copy(kind, z, 1).start())
+            pl.when(z < 3)(lambda: self.z_copy(kind, z, 0).start())
+            pl.when(z >= 2)(lambda: self.z_copy(kind, z, 1).start())
             return
 
         def from_left():
             @pl.when(z >= step)
             def _():
-                self.z_copy(kind, z - step, 0, 0).wait_recv()
+                self.z_copy(kind, z - step, 0).wait_recv()
                 if step < 3:
-                    pl.when(z < 3)(lambda: self.z_copy(kind, z - step, 0, step).start())
+                    pl.when(z < 3)(lambda: self.z_copy(kind, z - step, 0).start())
                 self.first(kind, z - step)
 
         def from_right():
             @pl.when(z + step <= 3)
             def _():
-                self.z_copy(kind, z + step, 1, 0).wait_recv()
+                self.z_copy(kind, z + step, 1).wait_recv()
                 if step < 3:
-                    pl.when(z > 0)(lambda: self.z_copy(kind, z + step, 1, step).start())
+                    pl.when(z > 0)(lambda: self.z_copy(kind, z + step, 1).start())
                 self.first(kind, z + step)
 
         pl.when(z < 2)(from_right)
@@ -121,17 +121,19 @@
         pl.when(z >= 2)(from_right)
 
     def plane_copy(self, kind, m, which):
-        at, block = self.at, self.blocks.at[kind, m]
+        recv = 0 if m is None else m
+        at, block = self.at, self.blocks.at[kind, slice(None) if m is None else m]
         x, y, c = at.x, at.y, at.c
         low, high = pl.ds(0, 48), pl.ds(48, 48)
+        every = (slice(None),) if m is None else ()
         ref, device = {
-            0: lambda: (block.at[y, x, c, low], at.across_x),
-            1: lambda: (block.at[y, x, c, high], at.across_y),
-            2: lambda: (block.at[y, :, c, low], at.across_y),
-            3: lambda: (block.at[:, x, c, high], at.across_x),
-            4: lambda: (block.at[:, :, c], at.core),
+            0: lambda: (block.at[(*every, y, x, c, low)], at.across_x),
+            1: lambda: (block.at[(*every, y, x, c, high)], at.across_y),
+            2: lambda: (block.at[(*every, y, slice(None), c, low)], at.across_y),
+            3: lambda: (block.at[(*every, slice(None), x, c, high)], at.across_x),
+            4: lambda: (block.at[(*every, slice(None), slice(None), c)], at.core),
         }[which]()
-        return remote(ref, ref, self.p_send.at[kind, m, which], self.p_recv.at[kind, m, which], device)
+        return remote(ref, ref, self.p_send.at[kind, which], self.p_recv.at[kind, recv, which], device)
 
     def at_step(self, step, act):
         z = self.at.z
@@ -177,17 +179,13 @@
     def drain(self):
         z = self.at.z
         for kind in range(4):
-            for step in range(3):
-                pl.when((z < 3) & (z >= step))(
-                    lambda k=kind, s=step: self.z_copy(k, z - s, 0, s).wait_send()
-                )
-                pl.when((z > 0) & (z + step <= 3))(
-                    lambda k=kind, s=step: self.z_copy(k, z + s, 1, s).wait_send()
-                )
+            for here in range(4):
+                for direction, count in ((0, here + 1), (1, 4 - here)):
+                    if (direction == 0 and here < 3) or (direction == 1 and here > 0):
+                        pl.when(z == here)(self.z_copy(kind, pl.ds(0, count), direction).wait_send)
         for kind in range(3):
-            for m in range(4):
-                for which in range(5):
-                    self.plane_copy(kind, m, which).wait_send()
+            for which in range(5):
+                self.plane_copy(kind, None, which).wait_send()
 
 
 def block_of(blocks, kind, m, low=0, width=768):
@@ -225,7 +223,7 @@
 ):
     rows = xs.shape[1]
     (recip_ref, headout_ref, xt_ref, qm_ref, kt_ref, v_ref, att_ref, acted_ref, slope_ref, n1t_ref, n1_ref, rs1_ref,
-     gb2_ref, gb2t_ref, g2_ref, sums_ref) = outs_ref
+     gb2_ref, g2_ref, sums_ref) = outs_ref
     keeps = [
         pltpu.make_async_copy(ref, to, outs_sem.at[i]) for i, (ref, to) in enumerate(zip(outs_ref, outs_hbm, strict=True))
     ]
@@ -376,7 +374,6 @@
 
     lax.fori_loop(0, 4, feed, 0)
     keep(7, 8)
-    hooks.before("down")
 
     def down(steps):
         places = [hooks.order(step) for step in steps]
@@ -385,6 +382,7 @@
         shares = [dot(acted_ref[m], block_of(blocks, DOWN, m), (1, 1)) for m in places]
         return functools.reduce(jnp.add, shares)
 
+    hooks.before("down")
     total[...] = down((0, 1, 2))
     total[...] += down((3,))
     hooks.all_landed()
@@ -407,7 +405,7 @@
         ) * rstd
         g2_ref[r, :] = grad_in
         gb2_ref[r, :] = grad_in.astype(BF16)
-        for i, (ref, to) in enumerate(((out_ref, out_hbm), (g2_ref, outs_hbm[14]), (gb2_ref, outs_hbm[12]))):
+        for i, (ref, to) in enumerate(((out_ref, out_hbm), (g2_ref, outs_hbm[13]), (gb2_ref, outs_hbm[12]))):
             pltpu.make_async_copy(ref.at[r], to.at[r], out_sem.at[i]).start()
         return (
             sums[0] + jnp.sum(grad_in, axis=0, keepdims=True),
@@ -418,14 +416,12 @@
     zero = jnp.zeros((1, 768), F32)
     sums = lax.fori_loop(0, rows // chunk, norm_two, (zero, zero, zero), unroll=2)
     sums_ref[...] = jnp.concatenate([*sums, jnp.zeros((5, 768), F32)], axis=0)
-    keep(15)
-    gb2t_ref[...] = gb2_ref[...].T
-    keep(13)
+    keep(14)
     hooks.finish()
     for i, copy in enumerate(keeps):
-        if i not in (12, 14):
+        if i not in (12, 13):
             copy.wait()
-    for i, (ref, to) in enumerate(((out_ref, out_hbm), (g2_ref, outs_hbm[14]), (gb2_ref, outs_hbm[12]))):
+    for i, (ref, to) in enumerate(((out_ref, out_hbm), (g2_ref, outs_hbm[13]), (gb2_ref, outs_hbm[12]))):
         pltpu.make_async_copy(ref, to, out_sem.at[i]).wait()
 
 
@@ -458,21 +454,20 @@
         ("own", 3): (("second", DOWN, 1),),
         ("swapped", 0): (("third", UP, 1),),
         ("other", 0): (("second", DOWN, 2), ("third", UP, 2)),
-        ("other", 1): (("third", DOWN, 0),),
-        ("other", 3): (("third", DOWN, 1),),
-        ("feed", 0): (("third", DOWN, 2),),
+        ("other", 2): (("third", DOWN, 0),),
+        ("norm", 0): (("third", DOWN, 1),),
+        ("feed", 1): (("third", DOWN, 2),),
     }
     END = {
         ("project", 1): (("second", UP, 0),),
-        ("project", 3): (("second", UP, 1),),
+        ("project", 3): (("second", UP, 1), ("z_step", UP, 2)),
         ("own", 0): (("second", DOWN, 0),),
         ("own", 1): (("third", UP, 0),),
-        ("own", 2): (("third", UP, 1),),
-        ("own", 3): (("z_step", UP, 2),),
+        ("own", 2): (("second", UP, 2), ("third", UP, 1)),
         ("swapped", 0): (("z_step", UP, 3), ("third", DOWN, 0)),
-        ("other", 0): (("second", UP, 2), ("z_step", DOWN, 1)),
+        ("other", 0): (("z_step", DOWN, 1), ("third", UP, 2)),
         ("other", 1): (("second", UP, 3), ("z_step", DOWN, 2)),
-        ("other", 2): (("second", DOWN, 1), ("third", UP, 2)),
+        ("other", 2): (("second", DOWN, 1),),
         ("other", 3): (("z_step", DOWN, 3), ("second", DOWN, 2)),
         ("norm", 0): (("third", UP, 3),),
         ("feed", 0): (("second", DOWN, 3),),
@@ -527,7 +522,7 @@
         self.gather.drain()
 
 
-N_KEPT = 16
+N_KEPT = 15
 
 
 def pack_weights(query, key, value, out_t, up, down_t):
@@ -624,7 +619,6 @@
     @pl.when(~at_end)
     def _():
         gather.z_step(UP, 0)
-        swap.start()
 
     gather.second(ATT, 1)
     gather.third(ATT, 0)
@@ -632,6 +626,7 @@
     gather.z_step(3, 3)
     gather.second(ATT, 2)
     gather.z_step(UP, 1)
+    pl.when(~at_end)(swap.start)
     gather.third(ATT, 1)
     gather.second(ATT, 3)
     gather.third(ATT, 2)
@@ -680,7 +675,6 @@
         of((rows, 768), F32),
         of((rows, 1), F32),
         of((rows, 768), BF16),
-        of((768, rows), BF16),
         of((rows, 768), F32),
         of((8, 768), F32),
     ]
@@ -726,9 +720,9 @@
             pltpu.VMEM((2, rows, 1), F32),
             pltpu.SemaphoreType.DMA,
             *forward_scratch(rows),
-            pltpu.SemaphoreType.DMA((4, 2, 3)),
+            pltpu.SemaphoreType.DMA((4, 2)),
             pltpu.SemaphoreType.DMA((4, 4)),
-            pltpu.SemaphoreType.DMA((3, 4, 5)),
+            pltpu.SemaphoreType.DMA((3, 5)),
             pltpu.SemaphoreType.DMA((3, 4, 5)),
             pltpu.SemaphoreType.DMA,
             pltpu.SemaphoreType.DMA,
@@ -779,6 +773,9 @@
     return (DOWN, DOWN_ORDER[n]) if n < 4 else (UP, n - 4) if n < 8 else (ATT, ATT_ORDER[n - 8])
 
 
+ALL = pl.ds(0, 3)
+
+
 class Scatter:
     def __init__(self, at, grads, out, buffers, semaphores):
         self.at, self.grads, self.out = at, grads, out
@@ -787,19 +784,21 @@
         self.deep_send, self.deep_recv, self.plane_send, self.plane_recv = deep
 
     def copy(self, kind, m, which):
-        at, grads = self.at, self.grads.at[kind, m]
+        every, index = ((slice(None),), slice(None)) if m is None else ((), m)
+        recv = 0 if m is None else m
+        at, grads = self.at, self.grads.at[kind, index]
         x, y, c = at.x, at.y, at.c
         low, high, _ = row_parts(kind)
-        first, second = self.first_in.at[kind, m], self.second_in.at[kind, m]
-        part = pl.ds(0, low.size)
+        core, first, second = self.core_in.at[kind, index], self.first_in.at[kind, index], self.second_in.at[kind, index]
+        part, whole = pl.ds(0, low.size), slice(None)
         src, dst, device = {
-            0: lambda: (grads.at[:, :, 1 - c], self.core_in.at[kind, m], at.core),
-            1: lambda: (grads.at[:, 1 - x, c, low], first.at[0, :, part], at.across_x),
-            2: lambda: (grads.at[1 - y, :, c, high], first.at[1, :, part], at.across_y),
-            3: lambda: (grads.at[1 - y, x, c, low], second.at[0, part], at.across_y),
-            4: lambda: (grads.at[y, 1 - x, c, high], second.at[1, part], at.across_x),
+            0: lambda: (grads.at[(*every, whole, whole, 1 - c)], core, at.core),
+            1: lambda: (grads.at[(*every, whole, 1 - x, c, low)], first.at[(*every, 0, whole, part)], at.across_x),
+            2: lambda: (grads.at[(*every, 1 - y, whole, c, high)], first.at[(*every, 1, whole, part)], at.across_y),
+            3: lambda: (grads.at[(*every, 1 - y, x, c, low)], second.at[(*every, 0, part)], at.across_y),
+            4: lambda: (grads.at[(*every, y, 1 - x, c, high)], second.at[(*every, 1, part)], at.across_x),
         }[which]()
-        return remote(src, dst, self.send.at[kind, m, which], self.recv.at[kind, m, which], device)
+        return remote(src, dst, self.send.at[kind, which], self.recv.at[kind, recv, which], device)
 
     def add(self, ref, got):
         ref[...] = (ref[...].astype(F32) + got[...].astype(F32)).astype(BF16)
@@ -851,11 +850,12 @@
 
     def deep_copy(self, m, direction, slot=None):
         at = self.at
-        device = at.right if direction == 0 else at.left
+        device = at.mate if slot is ALL else at.right if direction == 0 else at.left
         if slot is None:
             slot = m if direction == 0 else jnp.where(m == at.z - 1, 4, m)
+        recv = slot if slot is not ALL else 0
         src = self.grads.at[DOWN, m, :, :, at.c, pl.ds(0, DEEP)]
-        return remote(src, self.deep_in.at[slot], self.deep_send.at[m], self.deep_recv.at[slot], device)
+        return remote(src, self.deep_in.at[slot], self.deep_send, self.deep_recv.at[recv], device)
 
     def deep_add(self, m, slot, direction):
         self.deep_copy(m, direction, slot).wait_recv()
@@ -924,12 +924,13 @@
     def z_copy(self, kind, m, direction, slot=None):
         at = self.at
         whole = row_parts(kind)[2]
-        device = at.right if direction == 0 else at.left
+        device = at.mate if slot is ALL else at.right if direction == 0 else at.left
         if slot is None:
             slot = m if direction == 0 else jnp.where(m == at.z - 1, 4, m)
+        recv = slot if slot is not ALL else 0
         src = self.grads.at[kind, m, at.y, at.x, at.c, whole]
         dst = self.z_in.at[kind, slot, whole]
-        return remote(src, dst, self.z_send.at[kind, m], self.z_recv.at[kind, slot], device)
+        return remote(src, dst, self.z_send.at[kind], self.z_recv.at[kind, recv], device)
 
     def relay(self, kind, m, direction):
         whole = row_parts(kind)[2]
@@ -975,25 +976,13 @@
                 getattr(self, name)(*chunk_at(n))
 
     def drain(self):
-        z = self.at.z
         for which in range(4):
             self.deep_plane(which).wait_send()
+        self.deep_copy(ALL, 0, ALL).wait_send()
         for kind in range(3):
-
-            def of_index(m, _, kind=kind):
-                for which in range(5):
-                    self.copy(kind, m, which).wait_send()
-
-                def along(direction):
-                    self.z_copy(kind, m, direction).wait_send()
-                    if kind == DOWN:
-                        self.deep_copy(m, direction).wait_send()
-
-                pl.when(m > z)(lambda: along(0))
-                pl.when(m < z)(lambda: along(1))
-                return 0
-
-            lax.fori_loop(0, 4, of_index, 0)
+            for which in range(5):
+                self.copy(kind, None, which).wait_send()
+            self.z_copy(kind, ALL, 0, ALL).wait_send()
 
 
 class Totals:
@@ -1030,7 +1019,6 @@
     n1_hbm,
     rs1_hbm,
     gb2_hbm,
-    gb2t_hbm,
     g2_hbm,
     sums_hbm,
     masked_hbm,
@@ -1074,7 +1062,6 @@
     g2_load = pltpu.make_async_copy(g2_hbm, g2_ref, state_sem.at[0])
     n1_load = pltpu.make_async_copy(n1_hbm, grad_one, state_sem.at[1])
     gb2_load = pltpu.make_async_copy(gb2_hbm, gb2_ref, state_sem.at[2])
-    gb2t_load = pltpu.make_async_copy(gb2t_hbm, gb2t_ref, state_sem.at[3])
     n1t_load = pltpu.make_async_copy(n1t_hbm, n1t_ref, state_sem.at[4])
     xt_load = pltpu.make_async_copy(xt_hbm, xt_ref, state_sem.at[5])
 
@@ -1130,21 +1117,25 @@
         width = value.shape[1]
         grads[kind, m, :, :, :, :, pl.ds(low, width)] = value.astype(BF16).reshape(2, 2, 2, 96, width)
 
-    begin([gb2t_load, *(act_load(acted_hbm, m) for m in DOWN_ORDER)])
+    begin([gb2_load, *(act_load(acted_hbm, m) for m in DOWN_ORDER)])
     parts[...] = jnp.zeros_like(parts)
-    hooks.after("start")
-    finish((gb2t_load,))
-
-    def feed_down(place, _):
-        m = down_order(place)
+    finish((gb2_load,))
+    gb2t_ref[...] = gb2_ref[...].T
+
+    def feed_down(m):
         act_load(acted_hbm, m).wait()
         put(DOWN, m, dot(gb2t_ref[...], acts[m // 2, lax.rem(m, 2)]))
+
+    feed_down(DOWN_ORDER[0])
+    hooks.after("start")
+    hooks.ready(DOWN, DOWN_ORDER[0])
+    begin(feed_loads(0, 0))
+    act_load(slope_hbm, DOWN_ORDER[0]).start()
+
+    def feed_downs(place, _):
+        m = down_order(place)
+        feed_down(m)
         hooks.ready(DOWN, m)
-
-        @pl.when(place == 0)
-        def _():
-            begin((gb2_load, *feed_loads(0, 0)))
-
         act_load(slope_hbm, m).start()
 
         @pl.when(place == 1)
@@ -1156,8 +1147,8 @@
         hooks.after("down", place)
         return 0
 
-    lax.fori_loop(0, 4, feed_down, 0)
-    finish((gb2_load, n1t_load, g2_load))
+    lax.fori_loop(1, 4, feed_downs, 0)
+    finish((n1t_load, g2_load))
 
     def feed(m, _):
         slot = lax.rem(m, 2)
@@ -1393,7 +1384,7 @@
                     pl.when(m == index)(functools.partial(self.run, **steps))
 
 
-N_BACKWARD_INS = 20
+N_BACKWARD_INS = 19
 N_BACKWARD_SCRATCH = 33
 
 
@@ -1501,12 +1492,12 @@
 
 
 def run_backward(linked, blocks, probs, kept, masked, gain):
-    recip, headout, xt, qm, kt, v, att, acted, slope, n1t, n1, rs1, gb2, gb2t, g2, sums = kept
+    recip, headout, xt, qm, kt, v, att, acted, slope, n1t, n1, rs1, gb2, g2, sums = kept
     rows = gb2.shape[0]
     ins = (
-        blocks, probs, acted, slope, recip, headout, xt, qm, kt, v, att, n1t, n1, rs1, gb2, gb2t, g2, sums, masked, gain
+        blocks, probs, acted, slope, recip, headout, xt, qm, kt, v, att, n1t, n1, rs1, gb2, g2, sums, masked, gain
     )
-    in_specs = [vmem() if i == 19 else hbm() for i in range(20)]
+    in_specs = [vmem() if i == 18 else hbm() for i in range(19)]
     if linked:
         return pl.pallas_call(
             backward_linked,
@@ -1526,11 +1517,11 @@
                 pltpu.VMEM((3, 5, 96, 768), BF16),
                 pltpu.VMEM((5, 2, 2, DEEP, 768), BF16),
                 pltpu.VMEM((3, 2, DEEP // 2, 768), BF16),
+                pltpu.SemaphoreType.DMA((3, 5)),
                 pltpu.SemaphoreType.DMA((3, 4, 5)),
-                pltpu.SemaphoreType.DMA((3, 4, 5)),
-                pltpu.SemaphoreType.DMA((3, 4)),
+                pltpu.SemaphoreType.DMA((3,)),
                 pltpu.SemaphoreType.DMA((3, 5)),
-                pltpu.SemaphoreType.DMA((4,)),
+                pltpu.SemaphoreType.DMA,
                 pltpu.SemaphoreType.DMA((5,)),
                 pltpu.SemaphoreType.DMA((4,)),
                 pltpu.SemaphoreType.DMA((4,)),

time: 163 us -> 160 us (0.982)
  Pallas kernels: 162 us -> 159 us
    pallas_call x1, Pallas kernels: 77.9 us -> 74.6 us  [run_forward_linked(): pl.pallas_call(forward_linked, name='forward', out_shape=[jax.ShapeDtypeS...]
where the time goes in v6:
time: 160 us
  Pallas kernels  159 us (99%)
    pallas_call x1, Pallas kernels, run_backward(): pl.pallas_call(backward_linked, name='backward', out_shape=[jax.ShapeDtyp...  80.7 us
    pallas_call x1, Pallas kernels, run_forward_linked(): pl.pallas_call(forward_linked, name='forward', out_shape=[jax.ShapeDtypeS...  74.6 us
    pallas_call x1, Pallas kernels, run_finish(): pl.pallas_call(functools.partial(finish_kernel, (n_dp, n_mp)), name='fini...  3.34 us

profile of v6, /device:TPU:16, one launch (start us, length us, event | category | flops | bytes accessed | tf_op | source)
XLA Modules:
  0.0 159.5 jit_solution(4712551748938494606)
XLA Ops:
  0.7 74.6 %forward.1 = (bf16[3,4,2,2,2,96,768]{6,5,4,3,2,1,0:T(8,128)(2,1)}, bf16[12,1024,512]{2,1,0:T(8,128)(2,1)}, bf16[512,768]{1,0:T(8,128)(2,1)}, f32[2,512,1]{2,1,0:...) custom-call(s32[2]{0:T(128)} %refs_0_.1, ...), custom_call_target="tpu_custom_call" | custom-call | tf_op jit(solution)/shard_map/forward/pallas_call | solution.py:707
  75.3 80.7 %backward.1 = (f32[3,96,768]{2,1,0:T(8,128)}, f32[16,768]{1,0:T(8,128)}, bf16[512,768]{1,0:T(8,128)(2,1)}) custom-call(bf16[3,4,2,2,2,96,768]{6,5,4,3,2,1,0:T(8,128)(2,1)} %get-tuple-element.58.refs_0_, bf16[12,1024,512]{2,1,0:T(8,128)(2,1)} %get-tuple-element.59.refs_1_, bf16[4,512,768]{2,1,0:T(8,128)(2,1)} %get-tuple-element.60.refs_2_, ...), custom_call_target="tpu_custom_call" | custom-call | tf_op jit(solution)/shard_map/backward/pallas_call | solution.py:1502
  156.0 3.3 %finish.1 = (bf16[512,768]{1,0:T(8,128)(2,1)}, bf16[512,768]{1,0:T(8,128)(2,1)}, f32[96,192]{1,0:T(8,128)}, f32[96,192]{1,0:T(8,128)}, f32[96,192]{1,0:T(8,128)}...) custom-call(f32[3,96,768]{2,1,0:T(8,128)} %get-tuple-element.76.grad, ...), custom_call_target="tpu_custom_call" | custom-call | tf_op jit(solution)/shard_map/finish/pallas_call | solution.py:1596

commit v7 on v6

--- a/solution.py
+++ b/solution.py
@@ -358,7 +358,7 @@
         low[r, :] = (unit * vec_ref[2:3, :] + vec_ref[3:4, :]).astype(BF16)
         return 0
 
-    lax.fori_loop(0, rows // chunk, norm_one, 0, unroll=2)
+    lax.fori_loop(0, rows // chunk, norm_one, 0, unroll=4)
     n1t_ref[...] = low[...].T
     keep(9, 10, 11)
     hooks.after("norm")
@@ -414,7 +414,7 @@
         )
 
     zero = jnp.zeros((1, 768), F32)
-    sums = lax.fori_loop(0, rows // chunk, norm_two, (zero, zero, zero), unroll=2)
+    sums = lax.fori_loop(0, rows // chunk, norm_two, (zero, zero, zero), unroll=4)
     sums_ref[...] = jnp.concatenate([*sums, jnp.zeros((5, 768), F32)], axis=0)
     keep(14)
     hooks.finish()
@@ -562,10 +562,10 @@
 
 
 def forward_linked(*refs):
-    (lengths, starts, frames, cot, query, key, value, out_w, up, down, query_bias, value_bias, up_bias) = refs[:13]
+    (lengths, starts, frames, cot_hbm, query, key, value, out_w, up, down, query_bias, value_bias, up_bias) = refs[:13]
     vecs, refs = refs[13:20], refs[20:]
     blocks_hbm, probs_hbm, out_hbm, masked_hbm, *outs = refs[: 4 + N_KEPT]
-    blocks, biases, xs, keybias, valid, vec, masked_ref, masked_sem, *scratch = refs[4 + N_KEPT :]
+    blocks, biases, xs, keybias, valid, vec, masked_ref, masked_sem, cot, cot_sem, *scratch = refs[4 + N_KEPT :]
     scratch, links = scratch[:N_FORWARD_SCRATCH], scratch[N_FORWARD_SCRATCH:]
     z_send, z_recv, p_send, p_recv, x_send, x_recv, keep_sem = links
     at = Place()
@@ -606,6 +606,8 @@
         if side == 0:
             valid[...] = jnp.where(slots[:, 0:1] < length, 1.0, 0.0)
     masked_copy = pltpu.make_async_copy(masked_ref, masked_hbm, masked_sem)
+    cot_load = pltpu.make_async_copy(cot_hbm, cot, cot_sem)
+    cot_load.start()
     masked_copy.start()
     xs[0] = jnp.where(masked_ref[0] > 0, vec[6:7, :], frames[...].astype(F32)).astype(BF16)
     swap = remote(xs.at[0], xs.at[1], x_send, x_recv, at.mate)
@@ -637,6 +639,7 @@
         gather.z_step(DOWN, 0)
 
     gather.third(ATT, 3)
+    cot_load.wait()
     hooks = GatherHooks(gather, swap, blocks_hbm, keep_sem)
     forward_compute(blocks, biases, xs, keybias, valid, cot, vec, probs_hbm, out_hbm, outs, *scratch, hooks)
     masked_copy.wait()
@@ -708,7 +711,7 @@
         forward_linked,
         name="forward",
         out_shape=[jax.ShapeDtypeStruct(BLOCKS, BF16), probs, frames, masked, *outs],
-        in_specs=[pl.BlockSpec(memory_space=pltpu.SMEM)] + [vmem()] * 19,
+        in_specs=[pl.BlockSpec(memory_space=pltpu.SMEM), vmem(), vmem(), hbm()] + [vmem()] * 16,
         out_specs=[hbm()] * (4 + N_KEPT),
         scratch_shapes=[
             pltpu.VMEM(BLOCKS, BF16),
@@ -718,6 +721,8 @@
             pltpu.VMEM((rows, 1), F32),
             pltpu.VMEM((8, 768), F32),
             pltpu.VMEM((2, rows, 1), F32),
+            pltpu.SemaphoreType.DMA,
+            pltpu.VMEM((rows, 768), BF16),
             pltpu.SemaphoreType.DMA,
             *forward_scratch(rows),
             pltpu.SemaphoreType.DMA((4, 2)),
@@ -1117,9 +1122,10 @@
         width = value.shape[1]
         grads[kind, m, :, :, :, :, pl.ds(low, width)] = value.astype(BF16).reshape(2, 2, 2, 96, width)
 
-    begin([gb2_load, *(act_load(acted_hbm, m) for m in DOWN_ORDER)])
+    begin((gb2_load, act_load(acted_hbm, DOWN_ORDER[0])))
     parts[...] = jnp.zeros_like(parts)
     finish((gb2_load,))
+    begin([act_load(acted_hbm, m) for m in DOWN_ORDER[1:]])
     gb2t_ref[...] = gb2_ref[...].T
 
     def feed_down(m):
@@ -1192,7 +1198,7 @@
     finish((n1_load, xt_load))
     finish(small_loads)
     gain = gain_ref[...].astype(F32).reshape(1, 768)
-    sums = lax.fori_loop(0, rows // chunk, norm_back, (zero, zero, zero), unroll=2)
+    sums = lax.fori_loop(0, rows // chunk, norm_back, (zero, zero, zero), unroll=4)
     rows_ref[0, 0:1, :] = sums[0]
     rows_ref[0, 1:2, :] = sums_ref[0:1, :]
     rows_ref[0, 2:3, :] = sums[1]
@@ -1265,7 +1271,7 @@
         gb1[r, :] = other.astype(BF16)
         return total + jnp.sum(other * masked_ref[1, r, :], axis=0, keepdims=True)
 
-    fill = lax.fori_loop(0, rows // chunk, fill_other, zero)
+    fill = lax.fori_loop(0, rows // chunk, fill_other, zero, unroll=4)
     hooks.after("mate")
 
     def back_own(place, _):
@@ -1310,7 +1316,7 @@
         r = pl.ds(pl.multiple_of(i * chunk, chunk), chunk)
         return total + jnp.sum(grad_one[r, :] * masked_ref[0, r, :], axis=0, keepdims=True)
 
-    rows_ref[0, 6:7, :] = lax.fori_loop(0, rows // chunk, fill_own, fill)
+    rows_ref[0, 6:7, :] = lax.fori_loop(0, rows // chunk, fill_own, fill, unroll=4)
     rows_ref[0, 7:8, :] = zero
     for row in range(8):
         rows_ref[0, 8 + row : 9 + row, :] = parts[row, 0:1, :]
@@ -1325,7 +1331,7 @@
         frames_ref[r, :] = jnp.where(masked_ref[0, r, :] > 0, 0.0, total).astype(BF16)
         return 0
 
-    lax.fori_loop(0, grad_one.shape[0] // chunk, body, 0)
+    lax.fori_loop(0, grad_one.shape[0] // chunk, body, 0, unroll=4)
 
 
 class NoScatter:

time: 160 us -> 159 us (level)
  no operation moved by 1% of the time
where the time goes in v7:
time: 159 us
  Pallas kernels  158 us (99%)
    pallas_call x1, Pallas kernels, run_backward(): pl.pallas_call(backward_linked, name='backward', out_shape=[jax.ShapeDtyp...  79.8 us
    pallas_call x1, Pallas kernels, run_forward_linked(): pl.pallas_call(forward_linked, name='forward', out_shape=[jax.ShapeDtypeS...  74.6 us
    pallas_call x1, Pallas kernels, run_finish(): pl.pallas_call(functools.partial(finish_kernel, (n_dp, n_mp)), name='fini...  3.34 us

profile of v7, /device:TPU:16, one launch (start us, length us, event | category | flops | bytes accessed | tf_op | source)
XLA Modules:
  0.0 158.6 jit_solution(17081065690434108022)
XLA Ops:
  0.7 74.6 %forward.1 = (bf16[3,4,2,2,2,96,768]{6,5,4,3,2,1,0:T(8,128)(2,1)}, bf16[12,1024,512]{2,1,0:T(8,128)(2,1)}, bf16[512,768]{1,0:T(8,128)(2,1)}, f32[2,512,1]{2,1,0:...) custom-call(s32[2]{0:T(128)} %refs_0_.1, ...), custom_call_target="tpu_custom_call" | custom-call | tf_op jit(solution)/shard_map/forward/pallas_call | solution.py:710
  75.3 79.8 %backward.1 = (f32[3,96,768]{2,1,0:T(8,128)}, f32[16,768]{1,0:T(8,128)}, bf16[512,768]{1,0:T(8,128)(2,1)}) custom-call(bf16[3,4,2,2,2,96,768]{6,5,4,3,2,1,0:T(8,128)(2,1)} %get-tuple-element.58.refs_0_, bf16[12,1024,512]{2,1,0:T(8,128)(2,1)} %get-tuple-element.59.refs_1_, bf16[4,512,768]{2,1,0:T(8,128)(2,1)} %get-tuple-element.60.refs_2_, ...), custom_call_target="tpu_custom_call" | custom-call | tf_op jit(solution)/shard_map/backward/pallas_call | solution.py:1508
  155.1 3.3 %finish.1 = (bf16[512,768]{1,0:T(8,128)(2,1)}, bf16[512,768]{1,0:T(8,128)(2,1)}, f32[96,192]{1,0:T(8,128)}, f32[96,192]{1,0:T(8,128)}, f32[96,192]{1,0:T(8,128)}...) custom-call(f32[3,96,768]{2,1,0:T(8,128)} %get-tuple-element.76.grad, ...), custom_call_target="tpu_custom_call" | custom-call | tf_op jit(solution)/shard_map/finish/pallas_call | solution.py:1602
